TPU v7x, 32 devices: a whole 2x2x4 slice. The times are simulated.
32 devices in a mesh: ctx: 8 (over y, x, core), exp: 4 (over z).
Axes of the slice: x: 2, y: 2, z: 4, core: 2. Of those that a mesh axis runs over, the one named last changes fastest.
Arguments:
- queries: bfloat16 [2048, 4096], P(('ctx', 'exp')), may hold values from -6 to 6
- rotated_key_heads: bfloat16 [2048, 512], P(('ctx', 'exp')), may hold values from -15 to 15
- stacked_value_heads: bfloat16 [2048, 512], P(('ctx', 'exp')), may hold values from -6 to 6
- moe_rows: bfloat16 [4096, 4096], P(('ctx', 'exp')), may hold values from -6 to 6
- expert_ids: int32 [4096, 8], P(('ctx', 'exp')), may hold values from 0 to 31, all different within a row; in each aligned block of 128 rows (0 to 127, 128 to 255, ...) at most 40 rows name the same one
- route_weights: float32 [4096, 8], P(('ctx', 'exp')), may hold values from 0.05 to 0.35
- w_gate: bfloat16 [32, 4096, 768], P(('ctx', 'exp')), may hold values from -0.09375 to 0.09375
- w_up: bfloat16 [32, 4096, 768], P(('ctx', 'exp')), may hold values from -0.09375 to 0.09375
- w_down: bfloat16 [32, 768, 4096], P(('ctx', 'exp')), may hold values from -0.21875 to 0.21875
Outputs:
- attended: bfloat16 [2048, 4096], P(('ctx', 'exp'))
- expert_mix: bfloat16 [4096, 4096], P(('ctx', 'exp'))
Inputs may be any that keep to these rules, and one draw needn't show every extreme that they name: `expert_ids`: the 8 ids of a token are distinct. In each aligned block of 128 rows (the rows of one device) no expert is named by more than 40 rows, a bound that some block reaches.
All inputs are finite; a program needn't handle non-finite values.
Results may differ from a plain program's by a relative error of at most 0.0058.
Values may be sent and summed in bfloat16 or wider, within the bound.
No kernel may reach another device: no remote copies, remote signals or barrier semaphores. Data moves between devices by JAX's collectives and lax.ppermute only.
A program may use at most 192 MiB of HBM per device.

v0:
```python
import math

import jax
import jax.numpy as jnp
from jax import lax
from jax.sharding import PartitionSpec as P

D = 4096
QUERY_HEADS = 32
KEY_VALUE_HEADS = 4
HEAD_WIDTH = 128
TOPK = 8


def attend(queries, rotated_key_heads, stacked_value_heads):
    context_count = lax.axis_size("ctx")
    exp_count = lax.axis_size("exp")
    sequence_rows = queries.shape[0]
    heads_here = QUERY_HEADS // context_count
    repeat_factor = context_count // KEY_VALUE_HEADS
    key_dispersion = jnp.repeat(
        rotated_key_heads.reshape(sequence_rows, KEY_VALUE_HEADS, HEAD_WIDTH), repeat_factor, axis=1
    ).reshape(sequence_rows, context_count * HEAD_WIDTH)
    value_dispersion = jnp.repeat(
        stacked_value_heads.reshape(sequence_rows, KEY_VALUE_HEADS, HEAD_WIDTH),
        repeat_factor,
        axis=1,
    ).reshape(sequence_rows, context_count * HEAD_WIDTH)
    local_query, local_key, local_value = (
        lax.all_to_all(queries, "ctx", split_axis=1, concat_axis=0, tiled=True),
        lax.all_to_all(key_dispersion, "ctx", split_axis=1, concat_axis=0, tiled=True),
        lax.all_to_all(value_dispersion, "ctx", split_axis=1, concat_axis=0, tiled=True),
    )
    query_count = local_query.shape[0]
    row_ids = jnp.arange(query_count, dtype=jnp.int32)
    exp_here = lax.axis_index("exp")
    query_pos = (
        row_ids // sequence_rows * exp_count + exp_here
    ) * sequence_rows + row_ids % sequence_rows
    query_grid = local_query.reshape(query_count, heads_here, HEAD_WIDTH)
    scale_factor = 1.0 / math.sqrt(HEAD_WIDTH)

    def block_step(state, key_block, value_block, key_pos):
        row_max, row_sum, accum = state
        scores = (
            jnp.einsum("qhd,kd->hqk", query_grid, key_block, preferred_element_type=jnp.float32)
            * scale_factor
        )
        allowed = key_pos[None, None, :] <= query_pos[None, :, None]
        scores = jnp.where(allowed, scores, -1e30)
        new_max = jnp.maximum(row_max, jnp.max(scores, axis=2))
        probs = jnp.where(allowed, jnp.exp(scores - new_max[:, :, None]), 0.0).astype(jnp.bfloat16)
        factor = jnp.exp(row_max - new_max)
        row_sum = row_sum * factor + jnp.sum(probs.astype(jnp.float32), axis=2)
        accum = accum * factor.T[:, :, None] + jnp.einsum(
            "hqk,kd->qhd", probs, value_block, preferred_element_type=jnp.float32
        )
        return (new_max, row_sum, accum)

    initial = (
        jnp.full((heads_here, query_count), -1e30, jnp.float32),
        jnp.zeros((heads_here, query_count), jnp.float32),
        jnp.zeros((query_count, heads_here, HEAD_WIDTH), jnp.float32),
    )
    state = initial
    key_piece = lax.all_gather(local_key, "exp", axis=0, tiled=True)
    value_piece = lax.all_gather(local_value, "exp", axis=0, tiled=True)
    count = key_piece.shape[0]
    global_ids = jnp.arange(count, dtype=jnp.int32)
    source_exp = global_ids // query_count
    within = global_ids % query_count
    key_pos = (
        within // sequence_rows * exp_count + source_exp
    ) * sequence_rows + within % sequence_rows
    block_rows = 1024
    whole = count // block_rows * block_rows

    def scan_step(inner, parts):
        return (block_step(inner, parts[0], parts[1], parts[2]), 0)

    state = lax.scan(
        scan_step,
        state,
        (
            key_piece.reshape(whole // block_rows, block_rows, HEAD_WIDTH),
            value_piece.reshape(whole // block_rows, block_rows, HEAD_WIDTH),
            key_pos.reshape(whole // block_rows, block_rows),
        ),
    )[0]
    row_max, row_sum, accum = state
    head_out = (
        (accum / row_sum.T[:, :, None])
        .astype(jnp.bfloat16)
        .reshape(query_count, heads_here * HEAD_WIDTH)
    )
    return lax.all_to_all(head_out, "ctx", split_axis=0, concat_axis=1, tiled=True)


def expert_ffn(rows, w_gate, w_up, w_down):
    gate_in = jnp.dot(rows, w_gate[0], preferred_element_type=jnp.float32)
    up_in = jnp.dot(rows, w_up[0], preferred_element_type=jnp.float32)
    hidden = (jax.nn.silu(gate_in) * up_in).astype(jnp.bfloat16)
    return jnp.dot(hidden, w_down[0], preferred_element_type=jnp.float32).astype(jnp.bfloat16)


def run_live(received, live_mask, w_gate, w_up, w_down):
    flat_rows = received.reshape(-1, D)
    row_total = flat_rows.shape[0]
    live_flat = live_mask.reshape(row_total)
    order_pos = jnp.cumsum(live_flat) - live_flat
    block_rows = min(256, row_total)
    span = -(-row_total // block_rows) * block_rows
    compact = (
        jnp.full((span,), row_total, jnp.int32)
        .at[jnp.where(live_flat > 0, order_pos, span)]
        .set(jnp.arange(row_total, dtype=jnp.int32), mode="drop")
    )
    with_blank = jnp.concatenate([flat_rows, jnp.zeros((1, D), flat_rows.dtype)], 0)
    live_total = jnp.sum(live_flat)
    block_count = (live_total + block_rows - 1) // block_rows

    def one_block(index, output):
        picked = lax.dynamic_slice_in_dim(compact, index * block_rows, block_rows)
        return output.at[picked].set(expert_ffn(with_blank[picked], w_gate, w_up, w_down))

    output = lax.fori_loop(0, block_count, one_block, jnp.zeros((row_total + 1, D), jnp.bfloat16))
    return output[:row_total].reshape(received.shape)


def mixture(moe_rows, expert_ids, route_weights, w_gate, w_up, w_down):
    context_count = lax.axis_size("ctx")
    exp_count = lax.axis_size("exp")
    experts = context_count * exp_count
    token_count = moe_rows.shape[0]
    pair_count = token_count * TOPK
    capacity = max(2, pair_count * 5 // (4 * experts))
    flat_ids = expert_ids.reshape(pair_count)
    one_hot = (flat_ids[:, None] == jnp.arange(experts, dtype=jnp.int32)[None, :]).astype(jnp.int32)
    earlier = jnp.cumsum(one_hot, axis=0) - one_hot
    slot_index = jnp.sum(earlier * one_hot, axis=1)
    target = flat_ids * capacity + slot_index
    filler = (
        jnp.full((experts * capacity,), pair_count, jnp.int32)
        .at[target]
        .set(jnp.arange(pair_count, dtype=jnp.int32))
    )
    padded_rows = jnp.concatenate([moe_rows, jnp.zeros((1, D), moe_rows.dtype)], 0)
    outgoing = padded_rows[filler // TOPK].reshape(experts, capacity, D)
    occupied = (filler < pair_count).astype(jnp.int32).reshape(experts, capacity)
    payload = (outgoing, occupied)
    served = run_live(
        lax.all_to_all(payload[0], ("ctx", "exp"), split_axis=0, concat_axis=0, tiled=True),
        lax.all_to_all(payload[1], ("ctx", "exp"), split_axis=0, concat_axis=0, tiled=True),
        w_gate,
        w_up,
        w_down,
    )
    returned = lax.all_to_all(served, ("ctx", "exp"), split_axis=0, concat_axis=0, tiled=True)
    gathered = returned.reshape(experts * capacity, D)[target].reshape(token_count, TOPK, D)
    mixed = jnp.zeros((token_count, D), jnp.float32)
    for slot in range(TOPK):
        mixed = mixed + route_weights[:, slot : slot + 1] * gathered[:, slot, :].astype(jnp.float32)
    return mixed.astype(jnp.bfloat16)


def body(
    queries,
    rotated_key_heads,
    stacked_value_heads,
    moe_rows,
    expert_ids,
    route_weights,
    w_gate,
    w_up,
    w_down,
):
    attended = attend(queries, rotated_key_heads, stacked_value_heads)
    expert_mix = mixture(moe_rows, expert_ids, route_weights, w_gate, w_up, w_down)
    return (attended, expert_mix)


def solution(mesh):
    placed = (
        P(("ctx", "exp"), None),
        P(("ctx", "exp"), None),
        P(("ctx", "exp"), None),
        P(("ctx", "exp"), None),
        P(("ctx", "exp"), None),
        P(("ctx", "exp"), None),
        P(("ctx", "exp"), None, None),
        P(("ctx", "exp"), None, None),
        P(("ctx", "exp"), None, None),
    )
    return jax.shard_map(
        body,
        mesh=mesh,
        in_specs=placed,
        out_specs=(P(("ctx", "exp"), None), P(("ctx", "exp"), None)),
        check_vma=False,
    )
```

profile of v0, /device:TPU:12, one launch (start us, length us, event | category | flops | bytes accessed | tf_op | source)
XLA Modules:
  0.0 902.0 jit_solution(4836888732919998169)
XLA Ops:
  0.7 0.9 copy.72
  1.7 0.7 broadcast_multiply_fusion
  2.4 9.0 reduce-window.15
  12.2 4.3 scatter_custom_fusion.1
  16.5 0.7 reshape.247
  17.2 6.0 all-to-all-start.4
  23.2 4.9 all-to-all-done.4
  28.1 0.7 broadcast_in_dim.58
  28.8 4.7 all-to-all-start.2
  33.6 4.0 all-to-all-done.2
  37.6 0.7 broadcast_in_dim.57
  38.3 4.8 all-to-all-start
  43.1 0.8 copy.129
  43.9 3.2 all-to-all-done
  47.1 4.9 all-to-all-start.1
  52.2 8.3 gather_fusion.1
  60.5 5.7 all-to-all-start.5
  66.2 0.5 broadcast.305
  66.8 1.3 fusion.64
  69.6 5.2 scatter_custom_fusion.2
  74.8 235.3 %all_gather.7 = bf16[2048,128]{1,0:T(8,128)(2,1)} all-gather(bf16[512,128]{1,0:T(8,128)(2,1)S(1)} %bitcast.200), channel_id=1, replica_groups=mesh['ctx'=8,'exp'=4] {'exp'}, dimensions={0}, use_global_device_ids=true | all-gather | bytes 655360 | tf_op jit(solution)/shard_map/all_gather | solution.py:67
  310.2 15.1 %all_gather.6 = bf16[2048,128]{1,0:T(8,128)(2,1)S(1)} all-gather(bf16[512,128]{1,0:T(8,128)(2,1)S(1)} %bitcast.201), channel_id=1, replica_groups=mesh['ctx'=8,'exp'=4] {'exp'}, dimensions={0}, use_global_device_ids=true | all-gather | bytes 655360 | tf_op jit(solution)/shard_map/all_gather | solution.py:66
  325.5 26.4 %while.26 = (s32[]{:T(128)}, f32[4,512]{1,0:T(4,128)S(1)}, f32[4,512]{1,0:T(4,128)S(1)}, f32[512,4,128]{0,2,1:T(8,128)S(1)}, s32[2,1024]{1,0:T(2,128)S(1)}, /*in...) while((s32[]{:T(128)}, f32[4,512]{1,0:T(4,128)S(1)}, ...), condition=%wide.region_3.4_spmd.clone, body=%wide.region_0.3_spmd.clone.sunk | while | flops 1106530304 | bytes 66207936 | solution.py:81
  325.5 0.4 broadcast_compare_fusion.2
  325.9 4.8 fusion.95
  330.7 4.8 fusion.98
  335.6 1.0 copy-done.2
  336.5 2.1 convert_reduce_fusion.2
  339.1 4.8 fusion.95
  343.9 4.8 fusion.98
  348.8 1.0 copy-done.2
  349.8 2.1 convert_reduce_fusion.2
  352.3 1.0 all_to_all.79
  353.3 4.5 all-to-all-start.3
  357.8 9.9 %concatenate.7 = bf16[1281,4096]{1,0:T(8,128)(2,1)} pad(bf16[1280,4096]{1,0:T(8,128)(2,1)} %bitcast.20, bf16[]{:T(256)} %constant.166.clone.1), padding=0_1x0_0 | pad | bytes 20979714 | tf_op jit(solution)/shard_map/concatenate | solution.py:118
  367.7 5.4 broadcast_in_dim.59
  373.1 202.7 %while.25 = (s32[]{:T(128)}, bf16[1281,4096]{1,0:T(8,128)(2,1)}, s32[]{:T(128)}, s32[1280]{0:T(1024)S(1)}, bf16[1281,4096]{1,0:T(8,128)(2,1)}, /*index=5*/bf16[1...) while((s32[]{:T(128)}, bf16[1281,4096]{1,0:T(8,128)(2,1)}, ...), condition=%wide.region_14.15_spmd, body=%wide.region_12.14_spmd.sunk | while | flops 4834068480 | bytes 45622464 | solution.py:126
  385.6 9.2 %gather_fusion = bf16[256,4096]{1,0:T(8,128)(2,1)S(1)} fusion(bf16[1281,4096]{1,0:T(8,128)(2,1)} %get-tuple-element.386, s32[1024]{0:T(1024)S(1)} %pad_clamp_fusion.3), kind=kCustom, calls=%fused_computation.clone.1 | custom fusion | bytes 4195328 | tf_op jit(solution)/shard_map/while/body/gather | solution.py:124
  394.8 5.3 fusion.90
  400.2 9.7 %fusion.91 = bf16[256,4096]{1,0:T(8,128)(2,1)S(1)} fusion(bf16[1,768,4096]{2,1,0:T(8,128)(2,1)} %get-tuple-element.389, bf16[256,4096]{1,0:T(8,128)(2,1)} %copy-done.3, bf16[1,4096,768]{2,1,0:T(8,128)(2,1)} %get-tuple-element.388, f32[256,768]{1,0:T(8,128)S(1)} %fusion.90), kind=kOutput, calls=%fused_computation.13.clone.1 | convolution fusion | flops 3223453696 | bytes 17563648 | tf_op jit(solution)/shard_map/while/body/dot_general | solution.py:103
  409.9 13.5 %scatter_fusion = bf16[1281,4096]{1,0:T(8,128)(2,1)} fusion(bf16[1281,4096]{1,0:T(8,128)(2,1)} %get-tuple-element.371, s32[256]{0:T(256)S(1)} %compare_select_fusion.6, bf16[256,4096]{1,0:T(8,128)(2,1)S(1)} %fusion.91), kind=kCustom, calls=%fused_computation.3.clone.1 | custom fusion | bytes 6292480 | tf_op jit(solution)/shard_map/while/body/scatter | solution.py:124
  423.5 9.2 %gather_fusion = bf16[256,4096]{1,0:T(8,128)(2,1)S(1)} fusion(bf16[1281,4096]{1,0:T(8,128)(2,1)} %get-tuple-element.386, s32[1024]{0:T(1024)S(1)} %pad_clamp_fusion.3), kind=kCustom, calls=%fused_computation.clone.1 | custom fusion | bytes 4195328 | tf_op jit(solution)/shard_map/while/body/gather | solution.py:124
  432.8 5.3 fusion.90
  438.1 9.7 %fusion.91 = bf16[256,4096]{1,0:T(8,128)(2,1)S(1)} fusion(bf16[1,768,4096]{2,1,0:T(8,128)(2,1)} %get-tuple-element.389, bf16[256,4096]{1,0:T(8,128)(2,1)} %copy-done.3, bf16[1,4096,768]{2,1,0:T(8,128)(2,1)} %get-tuple-element.388, f32[256,768]{1,0:T(8,128)S(1)} %fusion.90), kind=kOutput, calls=%fused_computation.13.clone.1 | convolution fusion | flops 3223453696 | bytes 17563648 | tf_op jit(solution)/shard_map/while/body/dot_general | solution.py:103
  447.9 13.5 %scatter_fusion = bf16[1281,4096]{1,0:T(8,128)(2,1)} fusion(bf16[1281,4096]{1,0:T(8,128)(2,1)} %get-tuple-element.371, s32[256]{0:T(256)S(1)} %compare_select_fusion.6, bf16[256,4096]{1,0:T(8,128)(2,1)S(1)} %fusion.91), kind=kCustom, calls=%fused_computation.3.clone.1 | custom fusion | bytes 6292480 | tf_op jit(solution)/shard_map/while/body/scatter | solution.py:124
  461.5 9.2 %gather_fusion = bf16[256,4096]{1,0:T(8,128)(2,1)S(1)} fusion(bf16[1281,4096]{1,0:T(8,128)(2,1)} %get-tuple-element.386, s32[1024]{0:T(1024)S(1)} %pad_clamp_fusion.3), kind=kCustom, calls=%fused_computation.clone.1 | custom fusion | bytes 4195328 | tf_op jit(solution)/shard_map/while/body/gather | solution.py:124
  470.8 5.3 fusion.90
  476.1 9.7 %fusion.91 = bf16[256,4096]{1,0:T(8,128)(2,1)S(1)} fusion(bf16[1,768,4096]{2,1,0:T(8,128)(2,1)} %get-tuple-element.389, bf16[256,4096]{1,0:T(8,128)(2,1)} %copy-done.3, bf16[1,4096,768]{2,1,0:T(8,128)(2,1)} %get-tuple-element.388, f32[256,768]{1,0:T(8,128)S(1)} %fusion.90), kind=kOutput, calls=%fused_computation.13.clone.1 | convolution fusion | flops 3223453696 | bytes 17563648 | tf_op jit(solution)/shard_map/while/body/dot_general | solution.py:103
  485.9 13.5 %scatter_fusion = bf16[1281,4096]{1,0:T(8,128)(2,1)} fusion(bf16[1281,4096]{1,0:T(8,128)(2,1)} %get-tuple-element.371, s32[256]{0:T(256)S(1)} %compare_select_fusion.6, bf16[256,4096]{1,0:T(8,128)(2,1)S(1)} %fusion.91), kind=kCustom, calls=%fused_computation.3.clone.1 | custom fusion | bytes 6292480 | tf_op jit(solution)/shard_map/while/body/scatter | solution.py:124
  499.5 9.2 %gather_fusion = bf16[256,4096]{1,0:T(8,128)(2,1)S(1)} fusion(bf16[1281,4096]{1,0:T(8,128)(2,1)} %get-tuple-element.386, s32[1024]{0:T(1024)S(1)} %pad_clamp_fusion.3), kind=kCustom, calls=%fused_computation.clone.1 | custom fusion | bytes 4195328 | tf_op jit(solution)/shard_map/while/body/gather | solution.py:124
  508.7 5.3 fusion.90
  514.1 9.7 %fusion.91 = bf16[256,4096]{1,0:T(8,128)(2,1)S(1)} fusion(bf16[1,768,4096]{2,1,0:T(8,128)(2,1)} %get-tuple-element.389, bf16[256,4096]{1,0:T(8,128)(2,1)} %copy-done.3, bf16[1,4096,768]{2,1,0:T(8,128)(2,1)} %get-tuple-element.388, f32[256,768]{1,0:T(8,128)S(1)} %fusion.90), kind=kOutput, calls=%fused_computation.13.clone.1 | convolution fusion | flops 3223453696 | bytes 17563648 | tf_op jit(solution)/shard_map/while/body/dot_general | solution.py:103
  523.8 13.5 %scatter_fusion = bf16[1281,4096]{1,0:T(8,128)(2,1)} fusion(bf16[1281,4096]{1,0:T(8,128)(2,1)} %get-tuple-element.371, s32[256]{0:T(256)S(1)} %compare_select_fusion.6, bf16[256,4096]{1,0:T(8,128)(2,1)S(1)} %fusion.91), kind=kCustom, calls=%fused_computation.3.clone.1 | custom fusion | bytes 6292480 | tf_op jit(solution)/shard_map/while/body/scatter | solution.py:124
  537.5 9.2 %gather_fusion = bf16[256,4096]{1,0:T(8,128)(2,1)S(1)} fusion(bf16[1281,4096]{1,0:T(8,128)(2,1)} %get-tuple-element.386, s32[1024]{0:T(1024)S(1)} %pad_clamp_fusion.3), kind=kCustom, calls=%fused_computation.clone.1 | custom fusion | bytes 4195328 | tf_op jit(solution)/shard_map/while/body/gather | solution.py:124
  546.7 5.3 fusion.90
  552.1 9.7 %fusion.91 = bf16[256,4096]{1,0:T(8,128)(2,1)S(1)} fusion(bf16[1,768,4096]{2,1,0:T(8,128)(2,1)} %get-tuple-element.389, bf16[256,4096]{1,0:T(8,128)(2,1)} %copy-done.3, bf16[1,4096,768]{2,1,0:T(8,128)(2,1)} %get-tuple-element.388, f32[256,768]{1,0:T(8,128)S(1)} %fusion.90), kind=kOutput, calls=%fused_computation.13.clone.1 | convolution fusion | flops 3223453696 | bytes 17563648 | tf_op jit(solution)/shard_map/while/body/dot_general | solution.py:103
  561.8 13.5 %scatter_fusion = bf16[1281,4096]{1,0:T(8,128)(2,1)} fusion(bf16[1281,4096]{1,0:T(8,128)(2,1)} %get-tuple-element.371, s32[256]{0:T(256)S(1)} %compare_select_fusion.6, bf16[256,4096]{1,0:T(8,128)(2,1)S(1)} %fusion.91), kind=kCustom, calls=%fused_computation.3.clone.1 | custom fusion | bytes 6292480 | tf_op jit(solution)/shard_map/while/body/scatter | solution.py:124
  575.8 9.6 %slice.69 = bf16[1280,4096]{1,0:T(8,128)(2,1)} slice(bf16[1281,4096]{1,0:T(8,128)(2,1)} %get-tuple-element.95), slice={[0:1280], [0:4096]} | slice | bytes 20971520 | tf_op jit(solution)/shard_map/slice | solution.py:127
  585.3 6.0 all-to-all-start.6
  591.4 1.9 copy.97
  593.2 228.1 %all-to-all-done.6 = bf16[32,40,4096]{2,1,0:T(8,128)(2,1)} async-done(((bf16[32,40,4096]{2,1,0:T(8,128)(2,1)}), bf16[32,40,4096]{2,1,0:T(8,128)(2,1)}, u32[]{:S(2)}, u32[]{:S(2)}) %all-to-all-start.6) | async-done | bytes 10485792 | tf_op jit(solution)/shard_map/all_to_all | solution.py:158
  821.3 20.4 %gather_fusion.2 = bf16[1024,4096]{1,0:T(8,128)(2,1)} fusion(bf16[1280,4096]{1,0:T(8,128)(2,1)} %bitcast.22, s32[1024]{0:T(1024)S(1)} %broadcast_clamp_fusion), kind=kCustom, calls=%fused_computation.2 | custom fusion | bytes 16781312 | tf_op jit(solution)/shard_map/gather | solution.py:159
  841.7 39.5 %fusion.65 = (bf16[128,1,4096]{2,1,0:T(2,128)(2,1)S(1)}, bf16[128,1,4096]{2,1,0:T(2,128)(2,1)S(1)}, bf16[128,1,4096]{2,1,0:T(2,128)(2,1)S(1)}, bf16[128,1,4096]{...) fusion(bf16[128,8,4096]{2,1,0:T(8,128)(2,1)} %bitcast.194), kind=kLoop, calls=%fused_computation.136 | loop fusion | bytes 16777216 | tf_op jit(solution)/shard_map/slice | solution.py:162
  881.3 20.6 %fusion.44 = bf16[128,4096]{1,0:T(8,128)(2,1)} fusion(bf16[128,1,4096]{2,1,0:T(2,128)(2,1)} %get-tuple-element.203, bf16[128,1,4096]{2,1,0:T(2,128)(2,1)S(1)} %get-tuple-element.197, bf16[128,1,4096]{2,1,0:T(2,128)(2,1)S(1)} %get-tuple-element.198, bf16[128,1,4096]{2,1,0:T(2,128)(2,1)S(1)} %get-tuple-element.199, ...), kind=kLoop, calls=%fused_computation.58 | loop fusion | flops 12582912 | bytes 9441280 | tf_op jit(solution)/shard_map/convert_element_type | solution.py:163
  (95 shorter events, 3.5 us)
Async XLA Ops:
  0.6 22.6 %copy-start = (bf16[64,512]{1,0:T(8,128)(2,1)S(1)}, bf16[64,512]{1,0:T(8,128)(2,1)}, u32[]{:S(2)}) copy-start(bf16[64,512]{1,0:T(8,128)(2,1)} %param.15) | copy-start | bytes 196612
  0.6 32.9 %copy-start.7 = (bf16[64,512]{1,0:T(8,128)(2,1)S(1)}, bf16[64,512]{1,0:T(8,128)(2,1)}, u32[]{:S(2)}) copy-start(bf16[64,512]{1,0:T(8,128)(2,1)} %param.14) | copy-start | bytes 196612
  0.7 42.4 %copy-start.6 = (bf16[64,4096]{1,0:T(8,128)(2,1)S(1)}, bf16[64,4096]{1,0:T(8,128)(2,1)}, u32[]{:S(2)}) copy-start(bf16[64,4096]{1,0:T(8,128)(2,1)} %param.13) | copy-start | bytes 1572868
  11.5 40.5 %copy-start.4 = (bf16[128,4096]{1,0:T(8,128)(2,1)S(1)}, bf16[128,4096]{1,0:T(8,128)(2,1)}, u32[]{:S(2)}) copy-start(bf16[128,4096]{1,0:T(8,128)(2,1)} %param.16) | copy-start | bytes 3145732
  12.1 35.0 %copy-start.8 = (s32[1024,1]{0,1:T(1,128)}, s32[1024,1]{0,1:T(1,128)S(1)}, u32[]{:S(2)}) copy-start(s32[1024,1]{0,1:T(1,128)S(1)} %compare_select_fusion.2) | copy-start | bytes 12292
  17.2 10.9 %all-to-all-start.4 = ((s32[32,1,40]{2,1,0:T(1,128)}), s32[32,1,40]{2,1,0:T(1,128)S(1)}, u32[]{:S(2)}, u32[]{:S(2)}) async-start(s32[32,1,40]{2,1,0:T(1,128)} %reshape.247), calls=%async_computation.4 | async-start | bytes 32768 | tf_op jit(solution)/shard_map/all_to_all | solution.py:153
  28.8 8.8 all-to-all-start.2
  38.3 8.8 all-to-all-start
  47.1 13.3 %all-to-all-start.1 = ((bf16[64,8,512]{2,0,1:T(8,128)(2,1)}), bf16[64,8,512]{2,0,1:T(8,128)(2,1)S(1)}, u32[]{:S(2)}, u32[]{:S(2)}) async-start(bf16[64,8,512]{2,0,1:T(8,128)(2,1)} %bitcast.165), calls=%async_computation.1 | async-start | bytes 1048576 | tf_op jit(solution)/shard_map/all_to_all | solution.py:30
  60.5 292.9 %all-to-all-start.5 = ((bf16[32,40,4096]{2,1,0:T(8,128)(2,1)}), bf16[32,40,4096]{2,1,0:T(8,128)(2,1)}, u32[]{:S(2)}, u32[]{:S(2)}) async-start(bf16[32,40,4096]{2,1,0:T(8,128)(2,1)} %bitcast.195), calls=%async_computation.5 | async-start | bytes 20971520 | tf_op jit(solution)/shard_map/all_to_all | solution.py:152
  325.9 4.8 copy-start.5
  330.7 5.8 copy-start.2
  339.1 4.8 copy-start.5
  343.9 5.8 copy-start.2
  353.3 232.0 %all-to-all-start.3 = ((bf16[8,64,512]{2,1,0:T(8,128)(2,1)}), bf16[8,64,512]{2,1,0:T(8,128)(2,1)}, u32[]{:S(2)}, u32[]{:S(2)}) async-start(bf16[8,64,512]{2,1,0:T(8,128)(2,1)} %all_to_all.79), calls=%async_computation.3 | async-start | bytes 1048576 | tf_op jit(solution)/shard_map/all_to_all | solution.py:96
  394.8 5.3 copy-start.3
  432.8 5.3 copy-start.3
  470.8 5.3 copy-start.3
  508.7 5.3 copy-start.3
  546.7 5.3 copy-start.3
  585.3 6.0 copy-start.9
  585.3 6.0 copy-start.10
  585.3 236.0 %all-to-all-start.6 = ((bf16[32,40,4096]{2,1,0:T(8,128)(2,1)}), bf16[32,40,4096]{2,1,0:T(8,128)(2,1)}, u32[]{:S(2)}, u32[]{:S(2)}) async-start(bf16[32,40,4096]{2,1,0:T(8,128)(2,1)} %bitcast.196), calls=%async_computation.6 | async-start | bytes 20971520 | tf_op jit(solution)/shard_map/all_to_all | solution.py:158
  881.3 20.6 %copy-start.1 = (bf16[64,512]{1,0:T(8,128)(2,1)S(1)}, bf16[64,512]{1,0:T(8,128)(2,1)}, u32[]{:S(2)}) copy-start(bf16[64,512]{1,0:T(8,128)(2,1)} %param.15) | copy-start | bytes 196612
where the time goes:
time: 908 us; the launch traced here: 902 us
  blocking collectives  250 us (28%)
  waiting for transfers between devices  240 us (26%)
  local copies, waits for them, and re-layouts  227 us (25%)
  matrix products  94.6 us (10%)
  other arithmetic  37.8 us (4%)
  starting transfers between devices  36.5 us (4%)
  loops' own time  13.2 us (1%)
    all_gather x1, blocking collectives, attend(): value_piece = lax.all_gather(local_value, 'exp', axis=0, tiled=True)  235 us
    all_to_all x1, waiting for transfers between devices, mixture(): lax.all_to_all(served, ('ctx', 'exp'), split_axis=0, concat_axis=0, tiled...  228 us
    scatter x5, local copies, waits for them, and re-layouts, one_block(): output.at[picked].set(expert_ffn(with_blank[picked], w_gate, w_up, w_down))  67.7 us
    dot_general x5, matrix products, expert_ffn(): jnp.dot(hidden, w_down[0], preferred_element_type=jnp.float32)  48.7 us
    gather x5, local copies, waits for them, and re-layouts, one_block(): with_blank[picked]  46.2 us
    slice x1, local copies, waits for them, and re-layouts, mixture(): gathered[:, slot, :].astype(jnp.float32)  39.5 us
    dot_general x5, matrix products, expert_ffn(): gate_in = jnp.dot(rows, w_gate[0], preferred_element_type=jnp.float32)  26.6 us
    convert_element_type x1, other arithmetic, mixture(): return mixed.astype(jnp.bfloat16)  20.6 us
  transfers between devices with their start and end apart: 7, of which 4 were waited for; matrix products, arithmetic and copies ran while one was open for 29% of the time, Pallas kernels for 0%

commit v1 on v0

v1 whole, which is shorter than its diff:
```python
import functools
import math

import jax
import jax.numpy as jnp
from jax import lax
from jax.experimental import pallas as pl
from jax.experimental.pallas import tpu as pltpu
from jax.sharding import PartitionSpec as P

HEAD_WIDTH = 128
F32 = jnp.float32
BF16 = jnp.bfloat16


def swap(value, axis, offset):
    count = lax.axis_size(axis)
    return lax.ppermute(value, axis, [(i, i ^ offset) for i in range(count)])


def attention_kernel(heads, rows, q_ref, kv_ref, out_ref):
    here = lax.axis_index("ctx") * lax.axis_size("exp") + lax.axis_index("exp")
    first = here * rows
    query = jnp.concatenate(
        [q_ref[:, h * HEAD_WIDTH : (h + 1) * HEAD_WIDTH] for h in range(heads)], axis=0
    )
    scores = lax.dot_general(
        query, kv_ref[0], (((1,), (1,)), ((), ())), preferred_element_type=F32
    ) * (1.0 / math.sqrt(HEAD_WIDTH))
    place = lax.broadcasted_iota(jnp.int32, scores.shape, 1)
    position = place ^ first
    query_position = lax.broadcasted_iota(jnp.int32, scores.shape, 0) % rows + first
    allowed = position <= query_position
    scores = jnp.where(allowed, scores, -1e30)
    row_max = jnp.max(scores, axis=1, keepdims=True)
    probs = jnp.exp(scores - row_max).astype(BF16)
    total = jnp.sum(probs.astype(F32), axis=1, keepdims=True)
    summed = jnp.dot(probs, kv_ref[1], preferred_element_type=F32)
    result = (summed / total).astype(BF16)
    for h in range(heads):
        out_ref[:, h * HEAD_WIDTH : (h + 1) * HEAD_WIDTH] = result[h * rows : (h + 1) * rows]


def attend(queries, keys, values):
    rows, width = queries.shape
    kv_heads = keys.shape[1] // HEAD_WIDTH
    heads = width // HEAD_WIDTH // kv_heads
    ctx, exp = lax.axis_size("ctx"), lax.axis_size("exp")
    own = jnp.concatenate(
        [
            keys.reshape(rows, kv_heads, HEAD_WIDTH).transpose(1, 0, 2)[:, None],
            values.reshape(rows, kv_heads, HEAD_WIDTH).transpose(1, 0, 2)[:, None],
        ],
        axis=1,
    )
    line = jnp.concatenate([own] + [swap(own, "exp", s) for s in range(1, exp)], axis=2)
    group = [line] + [swap(line, "ctx", 2 * m) for m in range(1, ctx // 2)]
    mine = jnp.stack(group, axis=0)
    other = swap(mine, "ctx", 1)
    both = jnp.stack([mine, other], axis=1)
    gathered = both.transpose(2, 3, 0, 1, 4, 5).reshape(
        kv_heads, 2, ctx * exp * rows, HEAD_WIDTH
    )
    total_rows = ctx * exp * rows
    return pl.pallas_call(
        functools.partial(attention_kernel, heads, rows),
        grid=(kv_heads,),
        in_specs=[
            pl.BlockSpec((rows, heads * HEAD_WIDTH), lambda g: (0, g)),
            pl.BlockSpec((None, 2, total_rows, HEAD_WIDTH), lambda g: (g, 0, 0, 0)),
        ],
        out_specs=pl.BlockSpec((rows, heads * HEAD_WIDTH), lambda g: (0, g)),
        out_shape=jax.ShapeDtypeStruct(queries.shape, BF16),
        compiler_params=pltpu.CompilerParams(vmem_limit_bytes=48 * 1024 * 1024),
        cost_estimate=pl.CostEstimate(
            flops=4 * rows * width * total_rows,
            bytes_accessed=total_rows * kv_heads * 4 * HEAD_WIDTH + 4 * rows * width,
            transcendentals=rows * total_rows * heads * kv_heads,
        ),
    )(queries, gathered)


def mixture(moe_rows, expert_ids, route_weights, w_gate, w_up, w_down):
    ctx, exp = lax.axis_size("ctx"), lax.axis_size("exp")
    tokens, width = moe_rows.shape
    top = expert_ids.shape[1]
    experts = ctx * exp
    groups = ctx // 2
    capacity = max(2, tokens * top * 5 // (4 * experts))
    c, z = lax.axis_index("ctx"), lax.axis_index("exp")

    meta = jnp.concatenate([expert_ids.astype(F32).T, route_weights.T], axis=0)
    meta = jnp.concatenate([meta, swap(meta, "ctx", 1)], axis=1)
    metas = [meta] + [swap(meta, "exp", s) for s in range(1, exp)]
    own = [moe_rows] + [swap(moe_rows, "exp", s) for s in range(1, exp)]

    wanted = ((c ^ (2 * jnp.arange(groups))) * exp + z).astype(F32)
    earlier = jnp.arange(2 * tokens)
    before = (
        (earlier[:, None] < earlier[None, :])
        & (earlier[:, None] // tokens == earlier[None, :] // tokens)
    ).astype(BF16)

    def slots(meta):
        hit = meta[:top][None] == wanted[:, None, None]
        member = jnp.any(hit, axis=1)
        weight = jnp.sum(jnp.where(hit, meta[top:][None], 0.0), axis=1)
        rank = jnp.dot(member.astype(BF16), before, preferred_element_type=F32)
        block = earlier // tokens
        place = block[None, None, :, None, None]
        slot = jnp.arange(capacity, dtype=F32)
        taken = (
            member[:, None, None, :]
            & (rank[:, None, None, :] == slot[None, None, :, None])
            & (block[None, None, None, :] == jnp.arange(2)[None, :, None, None])
        )
        taken = taken.reshape(groups, 2 * capacity, 2 * tokens)
        return taken, weight

    def ffn(rows):
        gate = jnp.dot(rows, w_gate[0], preferred_element_type=F32)
        up = jnp.dot(rows, w_up[0], preferred_element_type=F32)
        hidden = (gate / (1.0 + jnp.exp(-gate)) * up).astype(BF16)
        return jnp.dot(hidden, w_down[0], preferred_element_type=F32).astype(BF16)

    partial = []
    for s in range(exp):
        taken, weight = slots(metas[s])
        block = jnp.concatenate([own[s], swap(own[s], "ctx", 1)], axis=0)
        sent = [
            jnp.dot(taken[m].astype(BF16), block, preferred_element_type=F32).astype(BF16)
            for m in range(groups)
        ]
        rows = jnp.concatenate(
            [sent[0]] + [swap(sent[m], "ctx", 2 * m) for m in range(1, groups)], axis=0
        )
        served = ffn(rows).reshape(groups, 2 * capacity, width)
        back = jnp.concatenate(
            [served[0]] + [swap(served[m], "ctx", 2 * m) for m in range(1, groups)], axis=0
        )
        scale = jnp.where(taken, weight[:, None, :], 0.0).reshape(
            groups * 2 * capacity, 2 * tokens
        )
        high = scale.astype(BF16)
        low = (scale - high.astype(F32)).astype(BF16)
        contract = (((0,), (0,)), ((), ()))
        mixed = lax.dot_general(high, back, contract, preferred_element_type=F32)
        mixed = mixed + lax.dot_general(low, back, contract, preferred_element_type=F32)
        total = mixed[:tokens] + swap(mixed[tokens:].astype(BF16), "ctx", 1).astype(F32)
        partial.append(total)
    summed = partial[0]
    for s in range(1, exp):
        summed = summed + swap(partial[s].astype(BF16), "exp", s).astype(F32)
    return summed.astype(BF16)


def body(queries, keys, values, moe_rows, expert_ids, route_weights, w_gate, w_up, w_down):
    attended = attend(queries, keys, values)
    expert_mix = mixture(moe_rows, expert_ids, route_weights, w_gate, w_up, w_down)
    return (attended, expert_mix)


def solution(mesh):
    row = P(("ctx", "exp"), None)
    cube = P(("ctx", "exp"), None, None)
    return jax.shard_map(
        body,
        mesh=mesh,
        in_specs=(row,) * 6 + (cube,) * 3,
        out_specs=(row, row),
        check_vma=False,
    )
```

time: 908 us -> 478 us (0.53)
  blocking collectives: 250 us -> 0 us
  local copies, waits for them, and re-layouts: 227 us -> 23 us
  waiting for transfers between devices: 240 us -> 277 us
  other arithmetic: 37.8 us -> 14.2 us
  Pallas kernels: 0 us -> 13.9 us
  loops' own time: 13.2 us -> 0 us
    ppermute x0 -> x49, waiting for transfers between devices: none -> 277 us  [swap(): return lax.ppermute(value, axis, [(i, i ^ offset) for i in range(count)])]
    all_gather x2 -> x0, blocking collectives: 250 us -> none  [the longest x1 235 us: attend(): value_piece = lax.all_gather(local_value, 'exp', axis=0, tiled=True)]
    all_to_all x7 -> x0, waiting for transfers between devices: 240 us -> none  [the longest x1 228 us: mixture(): lax.all_to_all(served, ('ctx', 'exp'), split_axis=0, concat_axis=0, tiled...]
    scatter x7 -> x0, local copies, waits for them, and re-layouts: 77.3 us -> none  [the longest x5 67.7 us: one_block(): output.at[picked].set(expert_ffn(with_blank[picked], w_gate, w_up, w_down))]
    gather x7 -> x0, local copies, waits for them, and re-layouts: 74.9 us -> none  [the longest x5 46.2 us: one_block(): with_blank[picked]]
    slice x4 -> x16, local copies, waits for them, and re-layouts: 49.3 us -> 7.99 us  [the longest x4 5.09 us: mixture(): served[0]]
    ppermute x0 -> x49, starting transfers between devices: none -> 40.5 us  [swap(): return lax.ppermute(value, axis, [(i, i ^ offset) for i in range(count)])]
    all_to_all x7 -> x0, starting transfers between devices: 36.5 us -> none  [the longest x1 5.99 us: mixture(): lax.all_to_all(payload[1], ('ctx', 'exp'), split_axis=0, concat_axis=0, t...]
  transfers between devices with their start and end apart: 7 -> 49, of which waited for: 4 -> 22; matrix products, arithmetic and copies ran while one was open for 29% -> 28% of each run, Pallas kernels for 0% -> 3%
where the time goes in v1:
time: 478 us; the launch traced here: 468 us
  waiting for transfers between devices  277 us (58%)
  matrix products  98.2 us (21%)
  starting transfers between devices  40.5 us (8%)
  local copies, waits for them, and re-layouts  23 us (5%)
  other arithmetic  14.2 us (3%)
  Pallas kernels  13.9 us (3%)
    ppermute x49, waiting for transfers between devices, swap(): return lax.ppermute(value, axis, [(i, i ^ offset) for i in range(count)])  277 us
    dot_general x4, matrix products, ffn(): return jnp.dot(hidden, w_down[0], preferred_element_type=F32).astype(BF16)  47.2 us
    ppermute x49, starting transfers between devices, swap(): return lax.ppermute(value, axis, [(i, i ^ offset) for i in range(count)])  40.5 us
    dot_general x4, matrix products, ffn(): up = jnp.dot(rows, w_up[0], preferred_element_type=F32)  19.4 us
    dot_general x16, matrix products, mixture(): jnp.dot(taken[m].astype(BF16), block, preferred_element_type=F32)  15 us
    pallas_call x1, Pallas kernels, attend(): pl.pallas_call(functools.partial(attention_kernel, heads, rows), grid=(kv...  13.9 us
  transfers between devices with their start and end apart: 49, of which 22 were waited for; matrix products, arithmetic and copies ran while one was open for 28% of the time, Pallas kernels for 3%

profile of v1, /device:TPU:12, one launch (start us, length us, event | category | flops | bytes accessed | tf_op | source)
XLA Modules:
  0.0 468.5 jit_solution(11211619106168547979)
XLA Ops:
  4.3 2.6 collective-permute-start.1
  10.0 22.8 %collective-permute-done.27 = f32[16,256]{1,0:T(8,128)S(1)} collective-permute-done((f32[16,256]{1,0:T(8,128)S(1)}, f32[16,256]{1,0:T(8,128)S(1)}, u32[]{:S(2)}, u32[]{:S(2)}) %collective-permute-start.27) | collective-permute-done | bytes 16416 | tf_op jit(solution)/shard_map/ppermute | solution.py:18
  33.3 3.3 collective-permute-done.38
  36.9 3.4 collective-permute-done.16
  45.1 1.8 collective-permute-done.2
  47.8 1.5 collective-permute-start.5
  49.9 1.5 collective-permute-start.4
  53.0 10.7 %collective-permute-done.5 = bf16[4,2,256,128]{3,2,1,0:T(8,128)(2,1)S(1)} collective-permute-done((bf16[4,2,256,128]{3,2,1,0:T(8,128)(2,1)S(1)}, bf16[4,2,256,128]{3,2,1,0:T(8,128)(2,1)S(1)}, u32[]{:S(2)}, u32[]{:S(2)}) %collective-permute-start.5) | collective-permute-done | bytes 524320 | tf_op jit(solution)/shard_map/ppermute | solution.py:18
  63.7 1.8 collective-permute-start.28
  65.4 3.2 collective-permute-done.3
  69.5 2.3 fusion.120
  71.8 1.3 constant_dynamic-update-slice_fusion
  75.3 1.9 collective-permute-start.11
  78.7 44.3 %collective-permute-done.28 = bf16[128,4096]{1,0:T(8,128)(2,1)} collective-permute-done((bf16[128,4096]{1,0:T(8,128)(2,1)S(1)}, bf16[128,4096]{1,0:T(8,128)(2,1)}, u32[]{:S(2)}, u32[]{:S(2)}) %collective-permute-start.28) | collective-permute-done | bytes 1048608 | tf_op jit(solution)/shard_map/ppermute | solution.py:18
  123.0 1.5 collective-permute-start.9
  124.5 2.3 constant_dynamic-update-slice_fusion.5
  127.3 19.2 %collective-permute-done.39 = bf16[128,4096]{1,0:T(8,128)(2,1)} collective-permute-done((bf16[128,4096]{1,0:T(8,128)(2,1)S(1)}, bf16[128,4096]{1,0:T(8,128)(2,1)}, u32[]{:S(2)}, u32[]{:S(2)}) %collective-permute-start.39) | collective-permute-done | bytes 1048608 | tf_op jit(solution)/shard_map/ppermute | solution.py:18
  150.1 3.2 fusion.14
  153.3 12.8 %fusion.24 = bf16[320,4096]{1,0:T(8,128)(2,1)} fusion(bf16[1,768,4096]{2,1,0:T(8,128)(2,1)} %param.17, f32[320,768]{1,0:T(8,128)} %fusion.14, bf16[1,4096,768]{2,1,0:T(8,128)(2,1)} %param.15, bf16[80,4096]{1,0:T(8,128)(2,1)} %copy-done.34, bf16[80,4096]{1,0:T(8,128)(2,1)} %copy-done.32, bf16[80,4096]{1,0:T(8,128)(2,1)} %copy-done.35, ...), kind=kOutput, calls=%fused_computation.28 | convolution fusion | flops 4039557120 | bytes 18808832 | tf_op jit(solution)/shard_map/dot_general | solution.py:124
  166.1 2.0 fusion.124
  168.1 1.6 collective-permute-start.12
  173.9 1.6 collective-permute-start.14
  176.7 1.3 convolution_convert_fusion.6
  178.1 1.3 convolution_convert_fusion.5
  179.4 1.4 convolution_convert_fusion.4
  180.7 1.4 convolution_convert_fusion.7
  182.1 1.5 collective-permute-start.19
  184.9 1.3 convolution_convert_fusion.2
  186.2 1.3 convolution_convert_fusion.1
  187.5 1.3 convolution_convert_fusion
  188.9 1.4 convolution_convert_fusion.3
  190.8 10.6 %collective-permute-done.13 = bf16[80,4096]{1,0:T(8,128)(2,1)S(1)} collective-permute-done((bf16[80,4096]{1,0:T(8,128)(2,1)S(1)}, bf16[80,4096]{1,0:T(8,128)(2,1)S(1)}, u32[]{:S(2)}, u32[]{:S(2)}) %collective-permute-start.13) | collective-permute-done | bytes 655392 | tf_op jit(solution)/shard_map/ppermute | solution.py:18
  206.2 7.7 %collective-permute-done.19 = bf16[80,4096]{1,0:T(8,128)(2,1)S(1)} collective-permute-done((bf16[80,4096]{1,0:T(8,128)(2,1)S(1)}, bf16[80,4096]{1,0:T(8,128)(2,1)S(1)}, u32[]{:S(2)}, u32[]{:S(2)}) %collective-permute-start.19) | collective-permute-done | bytes 655392 | tf_op jit(solution)/shard_map/ppermute | solution.py:18
  214.4 15.0 %collective-permute-done.20 = bf16[80,4096]{1,0:T(8,128)(2,1)S(1)} collective-permute-done((bf16[80,4096]{1,0:T(8,128)(2,1)S(1)}, bf16[80,4096]{1,0:T(8,128)(2,1)S(1)}, u32[]{:S(2)}, u32[]{:S(2)}) %collective-permute-start.20) | collective-permute-done | bytes 655392 | tf_op jit(solution)/shard_map/ppermute | solution.py:18
  230.5 3.1 fusion.12
  233.6 11.4 %fusion.27 = bf16[320,4096]{1,0:T(8,128)(2,1)S(1)} fusion(bf16[1,768,4096]{2,1,0:T(8,128)(2,1)} %param.17, f32[320,768]{1,0:T(8,128)} %fusion.12, bf16[1,4096,768]{2,1,0:T(8,128)(2,1)} %param.15, bf16[80,4096]{1,0:T(8,128)(2,1)} %copy-done.33, bf16[80,4096]{1,0:T(8,128)(2,1)} %copy-done.31, bf16[80,4096]{1,0:T(8,128)(2,1)} %copy-done.30, ...), kind=kOutput, calls=%fused_computation.29 | convolution fusion | flops 4039557120 | bytes 18808832 | tf_op jit(solution)/shard_map/dot_general | solution.py:124
  245.0 1.3 fusion.121
  246.4 2.4 collective-permute-start.42
  248.8 8.7 %collective-permute-done.31 = bf16[80,4096]{1,0:T(8,128)(2,1)} collective-permute-done((bf16[80,4096]{1,0:T(8,128)(2,1)}, bf16[80,4096]{1,0:T(8,128)(2,1)}, u32[]{:S(2)}, u32[]{:S(2)}) %collective-permute-start.31) | collective-permute-done | bytes 655392 | tf_op jit(solution)/shard_map/ppermute | solution.py:18
  258.6 6.6 %fusion.10 = f32[320,768]{1,0:T(8,128)} fusion(bf16[1,4096,768]{2,1,0:T(8,128)(2,1)} %param.16, bf16[80,4096]{1,0:T(8,128)(2,1)} %collective-permute-done.32, bf16[80,4096]{1,0:T(8,128)(2,1)} %collective-permute-done.31, bf16[80,4096]{1,0:T(8,128)(2,1)} %collective-permute-done.30, bf16[80,4096]{1,0:T(8,128)(2,1)S(1)} %copy-done.14), kind=kOutput, calls=%fused_computation.10 | convolution fusion | flops 2023751680 | bytes 9895936 | tf_op jit(solution)/shard_map/dot_general | solution.py:122
  265.1 11.3 %fusion.30 = bf16[320,4096]{1,0:T(8,128)(2,1)S(1)} fusion(bf16[1,768,4096]{2,1,0:T(8,128)(2,1)} %param.17, f32[320,768]{1,0:T(8,128)} %fusion.10, bf16[1,4096,768]{2,1,0:T(8,128)(2,1)} %param.15, bf16[80,4096]{1,0:T(8,128)(2,1)} %collective-permute-done.32, bf16[80,4096]{1,0:T(8,128)(2,1)} %collective-permute-done.31, ...), kind=kOutput, calls=%fused_computation.30 | convolution fusion | flops 4039557120 | bytes 18808832 | tf_op jit(solution)/shard_map/dot_general | solution.py:124
  276.5 1.6 fusion.122
  278.0 2.5 collective-permute-start.23
  280.5 5.1 %collective-permute-done.42 = bf16[80,4096]{1,0:T(8,128)(2,1)} collective-permute-done((bf16[80,4096]{1,0:T(8,128)(2,1)}, bf16[80,4096]{1,0:T(8,128)(2,1)}, u32[]{:S(2)}, u32[]{:S(2)}) %collective-permute-start.42) | collective-permute-done | bytes 655392 | tf_op jit(solution)/shard_map/ppermute | solution.py:18
  286.6 6.6 %fusion.8 = f32[320,768]{1,0:T(8,128)} fusion(bf16[1,4096,768]{2,1,0:T(8,128)(2,1)} %param.16, bf16[80,4096]{1,0:T(8,128)(2,1)} %collective-permute-done.43, bf16[80,4096]{1,0:T(8,128)(2,1)} %collective-permute-done.42, bf16[80,4096]{1,0:T(8,128)(2,1)} %collective-permute-done.41, bf16[80,4096]{1,0:T(8,128)(2,1)S(1)} %copy-done.13), kind=kOutput, calls=%fused_computation.8 | convolution fusion | flops 2023751680 | bytes 9895936 | tf_op jit(solution)/shard_map/dot_general | solution.py:122
  293.1 11.7 %fusion.33 = bf16[320,4096]{1,0:T(8,128)(2,1)S(1)} fusion(bf16[1,768,4096]{2,1,0:T(8,128)(2,1)} %param.17, f32[320,768]{1,0:T(8,128)} %fusion.8, bf16[1,4096,768]{2,1,0:T(8,128)(2,1)} %param.15, bf16[80,4096]{1,0:T(8,128)(2,1)} %collective-permute-done.43, bf16[80,4096]{1,0:T(8,128)(2,1)} %collective-permute-done.42, ...), kind=kOutput, calls=%fused_computation.31 | convolution fusion | flops 4039557120 | bytes 18808832 | tf_op jit(solution)/shard_map/dot_general | solution.py:124
  306.0 2.5 collective-permute-start.34
  308.4 5.2 %collective-permute-done.23 = bf16[80,4096]{1,0:T(8,128)(2,1)} collective-permute-done((bf16[80,4096]{1,0:T(8,128)(2,1)}, bf16[80,4096]{1,0:T(8,128)(2,1)}, u32[]{:S(2)}, u32[]{:S(2)}) %collective-permute-start.23) | collective-permute-done | bytes 655392 | tf_op jit(solution)/shard_map/ppermute | solution.py:18
  314.7 2.7 fusion.65
  317.4 2.8 convolution_add_fusion.2
  320.3 6.2 %collective-permute-done.33 = bf16[80,4096]{1,0:T(8,128)(2,1)} collective-permute-done((bf16[80,4096]{1,0:T(8,128)(2,1)}, bf16[80,4096]{1,0:T(8,128)(2,1)}, u32[]{:S(2)}, u32[]{:S(2)}) %collective-permute-start.33) | collective-permute-done | bytes 655392 | tf_op jit(solution)/shard_map/ppermute | solution.py:18
  327.1 14.5 %collective-permute-done.34 = bf16[80,4096]{1,0:T(8,128)(2,1)S(1)} collective-permute-done((bf16[80,4096]{1,0:T(8,128)(2,1)S(1)}, bf16[80,4096]{1,0:T(8,128)(2,1)S(1)}, u32[]{:S(2)}, u32[]{:S(2)}) %collective-permute-start.34) | collective-permute-done | bytes 655392 | tf_op jit(solution)/shard_map/ppermute | solution.py:18
  341.6 2.5 fusion.64
  344.2 2.6 convolution_add_fusion.1
  346.9 7.7 %collective-permute-done.44 = bf16[80,4096]{1,0:T(8,128)(2,1)S(1)} collective-permute-done((bf16[80,4096]{1,0:T(8,128)(2,1)S(1)}, bf16[80,4096]{1,0:T(8,128)(2,1)S(1)}, u32[]{:S(2)}, u32[]{:S(2)}) %collective-permute-start.44) | collective-permute-done | bytes 655392 | tf_op jit(solution)/shard_map/ppermute | solution.py:18
  354.6 14.2 %collective-permute-done.45 = bf16[80,4096]{1,0:T(8,128)(2,1)S(1)} collective-permute-done((bf16[80,4096]{1,0:T(8,128)(2,1)S(1)}, bf16[80,4096]{1,0:T(8,128)(2,1)S(1)}, u32[]{:S(2)}, u32[]{:S(2)}) %collective-permute-start.45) | collective-permute-done | bytes 655392 | tf_op jit(solution)/shard_map/ppermute | solution.py:18
  372.6 2.1 collective-permute-start.37
  375.9 1.4 collective-permute-start.48
  377.3 2.1 pad_maximum_fusion
  379.4 13.9 %shard_map.104 = bf16[64,4096]{1,0:T(8,128)(2,1)} custom-call(bf16[64,4096]{1,0:T(8,128)(2,1)S(1)} %copy-done.2, bf16[4,2,2048,128]{3,2,1,0:T(8,128)(2,1)S(1)} %bitcast.253), custom_call_target="tpu_custom_call" | custom-call | flops 2147483648 | bytes 5242880 | tf_op jit(solution)/shard_map/pallas_call | solution.py:65
  393.3 23.0 %collective-permute-done.26 = bf16[128,4096]{1,0:T(8,128)(2,1)S(1)} collective-permute-done((bf16[128,4096]{1,0:T(8,128)(2,1)S(1)}, bf16[128,4096]{1,0:T(8,128)(2,1)S(1)}, u32[]{:S(2)}, u32[]{:S(2)}) %collective-permute-start.26) | collective-permute-done | bytes 1048608 | tf_op jit(solution)/shard_map/ppermute | solution.py:18
  416.3 26.9 %collective-permute-done.37 = bf16[128,4096]{1,0:T(8,128)(2,1)S(1)} collective-permute-done((bf16[128,4096]{1,0:T(8,128)(2,1)S(1)}, bf16[128,4096]{1,0:T(8,128)(2,1)S(1)}, u32[]{:S(2)}, u32[]{:S(2)}) %collective-permute-start.37) | collective-permute-done | bytes 1048608 | tf_op jit(solution)/shard_map/ppermute | solution.py:18
  443.2 23.1 %collective-permute-done.48 = bf16[128,4096]{1,0:T(8,128)(2,1)S(1)} collective-permute-done((bf16[128,4096]{1,0:T(8,128)(2,1)}, bf16[128,4096]{1,0:T(8,128)(2,1)S(1)}, u32[]{:S(2)}, u32[]{:S(2)}) %collective-permute-start.48) | collective-permute-done | bytes 1048608 | tf_op jit(solution)/shard_map/ppermute | solution.py:18
  466.4 1.7 fusion.42
  (201 shorter events, 47.5 us)
Async XLA Ops:
  0.7 74.6 %collective-permute-start.17 = (bf16[128,4096]{1,0:T(8,128)(2,1)}, bf16[128,4096]{1,0:T(8,128)(2,1)S(1)}, u32[]{:S(2)}, u32[]{:S(2)}) collective-permute-start(bf16[128,4096]{1,0:T(8,128)(2,1)} %param.12), channel_id=1, source_target_pairs={{0,1},{1,0},{2,3},{3,2},{4,5},{5,4},{6,7},{7,6},{8,9},{9,8},{10,11... | collective-permute-start | bytes 3145736 | tf_op jit(solution)/shard_map/ppermute | solution.py:18
  1.2 70.6 %collective-permute-start.8 = (bf16[128,4096]{1,0:T(8,128)(2,1)}, bf16[128,4096]{1,0:T(8,128)(2,1)}, u32[]{:S(2)}, u32[]{:S(2)}) collective-permute-start(bf16[128,4096]{1,0:T(8,128)(2,1)} %param.12), channel_id=1, source_target_pairs={{0,4},{4,0},{8,12},{12,8},{16,20},{20,16},{24,28},{28,24},{1,5},{5... | collective-permute-start | bytes 3145736 | tf_op jit(solution)/shard_map/ppermute | solution.py:18
  3.0 42.1 %collective-permute-start = (bf16[4,2,64,128]{3,2,1,0:T(8,128)(2,1)}, bf16[4,2,64,128]{3,2,1,0:T(8,128)(2,1)S(1)}, u32[]{:S(2)}, u32[]{:S(2)}) collective-permute-start(bf16[4,2,64,128]{3,2,1,0:T(8,128)(2,1)} %pad_maximum_fusion.31), channel_id=1, source_target_pairs={{0,1},{1,0},{2,3},{3,2},{4,5},{5,4},{6,7},{7,6},{8,9},{9,8},{10,11... | collective-permute-start | bytes 393224 | tf_op jit(solution)/shard_map/ppermute | solution.py:18
  4.3 40.8 %collective-permute-start.1 = (bf16[4,2,64,128]{3,2,1,0:T(8,128)(2,1)}, bf16[4,2,64,128]{3,2,1,0:T(8,128)(2,1)}, u32[]{:S(2)}, u32[]{:S(2)}) collective-permute-start(bf16[4,2,64,128]{3,2,1,0:T(8,128)(2,1)} %pad_maximum_fusion.31), channel_id=1, source_target_pairs={{0,2},{1,3},{2,0},{3,1},{4,6},{5,7},{6,4},{7,5},{8,10},{9,11},{10,... | collective-permute-start | bytes 393224 | tf_op jit(solution)/shard_map/ppermute | solution.py:18
  8.3 1.3 collective-permute-start.7
  9.6 23.2 %collective-permute-start.27 = (f32[16,256]{1,0:T(8,128)S(1)}, f32[16,256]{1,0:T(8,128)S(1)}, u32[]{:S(2)}, u32[]{:S(2)}) collective-permute-start(f32[16,256]{1,0:T(8,128)S(1)} %pad_maximum_fusion.32), channel_id=1, source_target_pairs={{0,2},{1,3},{2,0},{3,1},{4,6},{5,7},{6,4},{7,5},{8,10},{9,11},{10,... | collective-permute-start | bytes 49160 | tf_op jit(solution)/shard_map/ppermute | solution.py:18
  32.8 3.7 collective-permute-start.38
  36.6 3.7 collective-permute-start.16
  40.3 6.6 %collective-permute-start.2 = (bf16[4,2,64,128]{3,2,1,0:T(8,128)(2,1)}, bf16[4,2,64,128]{3,2,1,0:T(8,128)(2,1)S(1)}, u32[]{:S(2)}, u32[]{:S(2)}) collective-permute-start(bf16[4,2,64,128]{3,2,1,0:T(8,128)(2,1)} %pad_maximum_fusion.31), channel_id=1, source_target_pairs={{0,3},{1,2},{2,1},{3,0},{4,7},{5,6},{6,5},{7,4},{8,11},{9,10},{10,... | collective-permute-start | bytes 393224 | tf_op jit(solution)/shard_map/ppermute | solution.py:18
  42.0 21.7 %copy-start.8 = (bf16[128,4096]{1,0:T(8,128)(2,1)S(1)}, bf16[128,4096]{1,0:T(8,128)(2,1)}, u32[]{:S(2)}) copy-start(bf16[128,4096]{1,0:T(8,128)(2,1)} %param.12) | copy-start | bytes 3145732
  47.8 15.8 %collective-permute-start.5 = (bf16[4,2,256,128]{3,2,1,0:T(8,128)(2,1)S(1)}, bf16[4,2,256,128]{3,2,1,0:T(8,128)(2,1)S(1)}, u32[]{:S(2)}, u32[]{:S(2)}) collective-permute-start(bf16[4,2,256,128]{3,2,1,0:T(8,128)(2,1)S(1)} %pad_maximum_fusion.10), channel_id=1, source_target_pairs={{0,24},{4,28},{8,16},{12,20},{16,8},{20,12},{24,0},{28,4},{1,25},{... | collective-permute-start | bytes 1572872 | tf_op jit(solution)/shard_map/ppermute | solution.py:18
  49.3 19.2 %collective-permute-start.3 = (bf16[4,2,256,128]{3,2,1,0:T(8,128)(2,1)S(1)}, bf16[4,2,256,128]{3,2,1,0:T(8,128)(2,1)S(1)}, u32[]{:S(2)}, u32[]{:S(2)}) collective-permute-start(bf16[4,2,256,128]{3,2,1,0:T(8,128)(2,1)S(1)} %pad_maximum_fusion.10), channel_id=1, source_target_pairs={{0,8},{4,12},{8,0},{12,4},{16,24},{20,28},{24,16},{28,20},{1,9},{5... | collective-permute-start | bytes 1572872 | tf_op jit(solution)/shard_map/ppermute | solution.py:18
  49.9 19.6 %collective-permute-start.4 = (bf16[4,2,256,128]{3,2,1,0:T(8,128)(2,1)S(1)}, bf16[4,2,256,128]{3,2,1,0:T(8,128)(2,1)S(1)}, u32[]{:S(2)}, u32[]{:S(2)}) collective-permute-start(bf16[4,2,256,128]{3,2,1,0:T(8,128)(2,1)S(1)} %pad_maximum_fusion.10), channel_id=1, source_target_pairs={{0,16},{4,20},{8,24},{12,28},{16,0},{20,4},{24,8},{28,12},{1,17},{... | collective-permute-start | bytes 1572872 | tf_op jit(solution)/shard_map/ppermute | solution.py:18
  63.7 59.3 %collective-permute-start.28 = (bf16[128,4096]{1,0:T(8,128)(2,1)S(1)}, bf16[128,4096]{1,0:T(8,128)(2,1)}, u32[]{:S(2)}, u32[]{:S(2)}) collective-permute-start(bf16[128,4096]{1,0:T(8,128)(2,1)S(1)} %copy-done.8), channel_id=1, source_target_pairs={{0,2},{1,3},{2,0},{3,1},{4,6},{5,7},{6,4},{7,5},{8,10},{9,11},{10,... | collective-permute-start | bytes 3145736 | tf_op jit(solution)/shard_map/ppermute | solution.py:18
  68.6 77.9 %collective-permute-start.39 = (bf16[128,4096]{1,0:T(8,128)(2,1)S(1)}, bf16[128,4096]{1,0:T(8,128)(2,1)}, u32[]{:S(2)}, u32[]{:S(2)}) collective-permute-start(bf16[128,4096]{1,0:T(8,128)(2,1)S(1)} %copy-done.8), channel_id=1, source_target_pairs={{0,3},{1,2},{2,1},{3,0},{4,7},{5,6},{6,5},{7,4},{8,11},{9,10},{10,... | collective-permute-start | bytes 3145736 | tf_op jit(solution)/shard_map/ppermute | solution.py:18
  71.8 305.5 %collective-permute-start.6 = (bf16[4,4,2,256,128]{4,3,0,2,1:T(8,128)(2,1)}, bf16[4,4,2,256,128]{4,3,0,2,1:T(8,128)(2,1)}, u32[]{:S(2)}, u32[]{:S(2)}) collective-permute-start(bf16[4,4,2,256,128]{4,3,0,2,1:T(8,128)(2,1)} %get-tuple-element.27), channel_id=1, source_target_pairs={{0,4},{4,0},{8,12},{12,8},{16,20},{20,16},{24,28},{28,24},{1,5},{5... | collective-permute-start | bytes 6291464 | tf_op jit(solution)/shard_map/ppermute | solution.py:18
  73.6 74.2 %collective-permute-start.10 = (bf16[80,4096]{1,0:T(8,128)(2,1)S(1)}, bf16[80,4096]{1,0:T(8,128)(2,1)S(1)}, u32[]{:S(2)}, u32[]{:S(2)}) collective-permute-start(bf16[80,4096]{1,0:T(8,128)(2,1)S(1)} %convolution_convert_fusion.13), channel_id=1, source_target_pairs={{0,16},{4,20},{8,24},{12,28},{16,0},{20,4},{24,8},{28,12},{1,17},{... | collective-permute-start | bytes 1966088 | tf_op jit(solution)/shard_map/ppermute | solution.py:18
  74.8 75.3 %slice-start = ((s8[6291456]{0:T(1024)(128)(4,1)}), s8[2097152]{0:T(1024)(128)(4,1)S(1)}, s32[]{:S(2)}) async-start(s8[6291456]{0:T(1024)(128)(4,1)} %bitcast.277), calls=%async_computation | async-start | bytes 4194304
  75.3 73.1 %collective-permute-start.11 = (bf16[80,4096]{1,0:T(8,128)(2,1)S(1)}, bf16[80,4096]{1,0:T(8,128)(2,1)S(1)}, u32[]{:S(2)}, u32[]{:S(2)}) collective-permute-start(bf16[80,4096]{1,0:T(8,128)(2,1)S(1)} %convolution_convert_fusion.12), channel_id=1, source_target_pairs={{0,24},{4,28},{8,16},{12,20},{16,8},{20,12},{24,0},{28,4},{1,25},{... | collective-permute-start | bytes 1966088 | tf_op jit(solution)/shard_map/ppermute | solution.py:18
  78.2 71.9 %slice-start.1 = ((s8[6291456]{0:T(1024)(128)(4,1)}), s8[4194304]{0:T(1024)(128)(4,1)S(1)}, s32[]{:S(2)}) async-start(s8[6291456]{0:T(1024)(128)(4,1)} %bitcast.277), calls=%async_computation.1 | async-start | bytes 8388608
  123.0 25.5 %collective-permute-start.9 = (bf16[80,4096]{1,0:T(8,128)(2,1)S(1)}, bf16[80,4096]{1,0:T(8,128)(2,1)S(1)}, u32[]{:S(2)}, u32[]{:S(2)}) collective-permute-start(bf16[80,4096]{1,0:T(8,128)(2,1)S(1)} %convolution_convert_fusion.14), channel_id=1, source_target_pairs={{0,8},{4,12},{8,0},{12,4},{16,24},{20,28},{24,16},{28,20},{1,9},{5... | collective-permute-start | bytes 1966088 | tf_op jit(solution)/shard_map/ppermute | solution.py:18
  127.3 21.2 %copy-start.15 = (bf16[80,4096]{1,0:T(8,128)(2,1)}, bf16[80,4096]{1,0:T(8,128)(2,1)S(1)}, u32[]{:S(2)}) copy-start(bf16[80,4096]{1,0:T(8,128)(2,1)S(1)} %convolution_convert_fusion.15) | copy-start | bytes 1966084
  146.5 23.2 %collective-permute-start.18 = (bf16[128,4096]{1,0:T(8,128)(2,1)S(1)}, bf16[128,4096]{1,0:T(8,128)(2,1)}, u32[]{:S(2)}, u32[]{:S(2)}) collective-permute-start(bf16[128,4096]{1,0:T(8,128)(2,1)S(1)} %collective-permute-done.17), channel_id=1, source_target_pairs={{0,4},{4,0},{8,12},{12,8},{16,20},{20,16},{24,28},{28,24},{1,5},{5... | collective-permute-start | bytes 3145736 | tf_op jit(solution)/shard_map/ppermute | solution.py:18
  147.8 26.0 %collective-permute-start.29 = (bf16[128,4096]{1,0:T(8,128)(2,1)}, bf16[128,4096]{1,0:T(8,128)(2,1)}, u32[]{:S(2)}, u32[]{:S(2)}) collective-permute-start(bf16[128,4096]{1,0:T(8,128)(2,1)} %collective-permute-done.28), channel_id=1, source_target_pairs={{0,4},{4,0},{8,12},{12,8},{16,20},{20,16},{24,28},{28,24},{1,5},{5... | collective-permute-start | bytes 3145736 | tf_op jit(solution)/shard_map/ppermute | solution.py:18
  148.4 33.7 %collective-permute-start.40 = (bf16[128,4096]{1,0:T(8,128)(2,1)}, bf16[128,4096]{1,0:T(8,128)(2,1)}, u32[]{:S(2)}, u32[]{:S(2)}) collective-permute-start(bf16[128,4096]{1,0:T(8,128)(2,1)} %collective-permute-done.39), channel_id=1, source_target_pairs={{0,4},{4,0},{8,12},{12,8},{16,20},{20,16},{24,28},{28,24},{1,5},{5... | collective-permute-start | bytes 3145736 | tf_op jit(solution)/shard_map/ppermute | solution.py:18
  168.1 22.1 %collective-permute-start.12 = (bf16[80,4096]{1,0:T(8,128)(2,1)S(1)}, bf16[80,4096]{1,0:T(8,128)(2,1)S(1)}, u32[]{:S(2)}, u32[]{:S(2)}) collective-permute-start(bf16[80,4096]{1,0:T(8,128)(2,1)S(1)} %get-tuple-element.25), channel_id=1, source_target_pairs={{0,8},{4,12},{8,0},{12,4},{16,24},{20,28},{24,16},{28,20},{1,9},{5... | collective-permute-start | bytes 1966088 | tf_op jit(solution)/shard_map/ppermute | solution.py:18
  169.7 31.7 %collective-permute-start.13 = (bf16[80,4096]{1,0:T(8,128)(2,1)S(1)}, bf16[80,4096]{1,0:T(8,128)(2,1)S(1)}, u32[]{:S(2)}, u32[]{:S(2)}) collective-permute-start(bf16[80,4096]{1,0:T(8,128)(2,1)S(1)} %get-tuple-element.24), channel_id=1, source_target_pairs={{0,16},{4,20},{8,24},{12,28},{16,0},{20,4},{24,8},{28,12},{1,17},{... | collective-permute-start | bytes 1966088 | tf_op jit(solution)/shard_map/ppermute | solution.py:18
  173.9 27.5 %collective-permute-start.14 = (bf16[80,4096]{1,0:T(8,128)(2,1)S(1)}, bf16[80,4096]{1,0:T(8,128)(2,1)S(1)}, u32[]{:S(2)}, u32[]{:S(2)}) collective-permute-start(bf16[80,4096]{1,0:T(8,128)(2,1)S(1)} %get-tuple-element.23), channel_id=1, source_target_pairs={{0,24},{4,28},{8,16},{12,20},{16,8},{20,12},{24,0},{28,4},{1,25},{... | collective-permute-start | bytes 1966088 | tf_op jit(solution)/shard_map/ppermute | solution.py:18
  182.1 31.8 %collective-permute-start.19 = (bf16[80,4096]{1,0:T(8,128)(2,1)S(1)}, bf16[80,4096]{1,0:T(8,128)(2,1)S(1)}, u32[]{:S(2)}, u32[]{:S(2)}) collective-permute-start(bf16[80,4096]{1,0:T(8,128)(2,1)S(1)} %convolution_convert_fusion.10), channel_id=1, source_target_pairs={{0,8},{4,12},{8,0},{12,4},{16,24},{20,28},{24,16},{28,20},{1,9},{5... | collective-permute-start | bytes 1966088 | tf_op jit(solution)/shard_map/ppermute | solution.py:18
  187.5 14.8 %copy-start.22 = (bf16[320,256]{1,0:T(8,128)(2,1)S(1)}, bf16[320,256]{1,0:T(8,128)(2,1)}, u32[]{:S(2)}) copy-start(bf16[320,256]{1,0:T(8,128)(2,1)} %get-tuple-element.51) | copy-start | bytes 491524
  190.3 39.1 %collective-permute-start.20 = (bf16[80,4096]{1,0:T(8,128)(2,1)S(1)}, bf16[80,4096]{1,0:T(8,128)(2,1)S(1)}, u32[]{:S(2)}, u32[]{:S(2)}) collective-permute-start(bf16[80,4096]{1,0:T(8,128)(2,1)S(1)} %convolution_convert_fusion.9), channel_id=1, source_target_pairs={{0,16},{4,20},{8,24},{12,28},{16,0},{20,4},{24,8},{28,12},{1,17},{... | collective-permute-start | bytes 1966088 | tf_op jit(solution)/shard_map/ppermute | solution.py:18
  201.4 28.0 %collective-permute-start.21 = (bf16[80,4096]{1,0:T(8,128)(2,1)S(1)}, bf16[80,4096]{1,0:T(8,128)(2,1)S(1)}, u32[]{:S(2)}, u32[]{:S(2)}) collective-permute-start(bf16[80,4096]{1,0:T(8,128)(2,1)S(1)} %convolution_convert_fusion.8), channel_id=1, source_target_pairs={{0,24},{4,28},{8,16},{12,20},{16,8},{20,12},{24,0},{28,4},{1,25},{... | collective-permute-start | bytes 1966088 | tf_op jit(solution)/shard_map/ppermute | solution.py:18
  201.4 45.0 %collective-permute-start.30 = (bf16[80,4096]{1,0:T(8,128)(2,1)}, bf16[80,4096]{1,0:T(8,128)(2,1)}, u32[]{:S(2)}, u32[]{:S(2)}) collective-permute-start(bf16[80,4096]{1,0:T(8,128)(2,1)} %convolution_convert_fusion.6), channel_id=1, source_target_pairs={{0,8},{4,12},{8,0},{12,4},{16,24},{20,28},{24,16},{28,20},{1,9},{5... | collective-permute-start | bytes 1966088 | tf_op jit(solution)/shard_map/ppermute | solution.py:18
  202.4 28.1 %slice-start.2 = ((s8[6291456]{0:T(1024)(128)(4,1)}), s8[4194304]{0:T(1024)(128)(4,1)S(1)}, s32[]{:S(2)}) async-start(s8[6291456]{0:T(1024)(128)(4,1)} %bitcast.279), calls=%async_computation.2 | async-start | bytes 8388608
  203.7 26.8 %slice-start.3 = ((s8[6291456]{0:T(1024)(128)(4,1)}), s8[2097152]{0:T(1024)(128)(4,1)S(1)}, s32[]{:S(2)}) async-start(s8[6291456]{0:T(1024)(128)(4,1)} %bitcast.279), calls=%async_computation.3 | async-start | bytes 4194304
  205.0 25.4 %copy-start.6 = (f32[256,4096]{1,0:T(8,128)}, f32[256,4096]{1,0:T(8,128)S(1)}, u32[]{:S(2)}) copy-start(f32[256,4096]{1,0:T(8,128)S(1)} %convolution_add_fusion.3) | copy-start | bytes 12582916
  213.9 16.5 %copy-start.30 = (bf16[80,4096]{1,0:T(8,128)(2,1)}, bf16[80,4096]{1,0:T(8,128)(2,1)S(1)}, u32[]{:S(2)}) copy-start(bf16[80,4096]{1,0:T(8,128)(2,1)S(1)} %collective-permute-done.19) | copy-start | bytes 1966084
  213.9 43.7 %collective-permute-start.31 = (bf16[80,4096]{1,0:T(8,128)(2,1)}, bf16[80,4096]{1,0:T(8,128)(2,1)}, u32[]{:S(2)}, u32[]{:S(2)}) collective-permute-start(bf16[80,4096]{1,0:T(8,128)(2,1)} %convolution_convert_fusion.5), channel_id=1, source_target_pairs={{0,16},{4,20},{8,24},{12,28},{16,0},{20,4},{24,8},{28,12},{1,17},{... | collective-permute-start | bytes 1966088 | tf_op jit(solution)/shard_map/ppermute | solution.py:18
  229.4 28.2 %collective-permute-start.32 = (bf16[80,4096]{1,0:T(8,128)(2,1)}, bf16[80,4096]{1,0:T(8,128)(2,1)}, u32[]{:S(2)}, u32[]{:S(2)}) collective-permute-start(bf16[80,4096]{1,0:T(8,128)(2,1)} %convolution_convert_fusion.4), channel_id=1, source_target_pairs={{0,24},{4,28},{8,16},{12,20},{16,8},{20,12},{24,0},{28,4},{1,25},{... | collective-permute-start | bytes 1966088 | tf_op jit(solution)/shard_map/ppermute | solution.py:18
  229.4 48.6 %collective-permute-start.41 = (bf16[80,4096]{1,0:T(8,128)(2,1)}, bf16[80,4096]{1,0:T(8,128)(2,1)}, u32[]{:S(2)}, u32[]{:S(2)}) collective-permute-start(bf16[80,4096]{1,0:T(8,128)(2,1)} %convolution_convert_fusion.2), channel_id=1, source_target_pairs={{0,8},{4,12},{8,0},{12,4},{16,24},{20,28},{24,16},{28,20},{1,9},{5... | collective-permute-start | bytes 1966088 | tf_op jit(solution)/shard_map/ppermute | solution.py:18
  245.0 13.6 %copy-start.14 = (bf16[80,4096]{1,0:T(8,128)(2,1)S(1)}, bf16[80,4096]{1,0:T(8,128)(2,1)}, u32[]{:S(2)}) copy-start(bf16[80,4096]{1,0:T(8,128)(2,1)} %convolution_convert_fusion.7) | copy-start | bytes 1966084
  246.4 39.2 %collective-permute-start.42 = (bf16[80,4096]{1,0:T(8,128)(2,1)}, bf16[80,4096]{1,0:T(8,128)(2,1)}, u32[]{:S(2)}, u32[]{:S(2)}) collective-permute-start(bf16[80,4096]{1,0:T(8,128)(2,1)} %convolution_convert_fusion.1), channel_id=1, source_target_pairs={{0,16},{4,20},{8,24},{12,28},{16,0},{20,4},{24,8},{28,12},{1,17},{... | collective-permute-start | bytes 1966088 | tf_op jit(solution)/shard_map/ppermute | solution.py:18
  257.6 28.0 %collective-permute-start.43 = (bf16[80,4096]{1,0:T(8,128)(2,1)}, bf16[80,4096]{1,0:T(8,128)(2,1)}, u32[]{:S(2)}, u32[]{:S(2)}) collective-permute-start(bf16[80,4096]{1,0:T(8,128)(2,1)} %convolution_convert_fusion), channel_id=1, source_target_pairs={{0,24},{4,28},{8,16},{12,20},{16,8},{20,12},{24,0},{28,4},{1,25},{... | collective-permute-start | bytes 1966088 | tf_op jit(solution)/shard_map/ppermute | solution.py:18
  257.6 47.5 %collective-permute-start.22 = (bf16[80,4096]{1,0:T(8,128)(2,1)}, bf16[80,4096]{1,0:T(8,128)(2,1)}, u32[]{:S(2)}, u32[]{:S(2)}) collective-permute-start(bf16[80,4096]{1,0:T(8,128)(2,1)} %get-tuple-element.13), channel_id=1, source_target_pairs={{0,8},{4,12},{8,0},{12,4},{16,24},{20,28},{24,16},{28,20},{1,9},{5... | collective-permute-start | bytes 1966088 | tf_op jit(solution)/shard_map/ppermute | solution.py:18
  278.0 35.6 %collective-permute-start.23 = (bf16[80,4096]{1,0:T(8,128)(2,1)}, bf16[80,4096]{1,0:T(8,128)(2,1)}, u32[]{:S(2)}, u32[]{:S(2)}) collective-permute-start(bf16[80,4096]{1,0:T(8,128)(2,1)} %get-tuple-element.12), channel_id=1, source_target_pairs={{0,16},{4,20},{8,24},{12,28},{16,0},{20,4},{24,8},{28,12},{1,17},{... | collective-permute-start | bytes 1966088 | tf_op jit(solution)/shard_map/ppermute | solution.py:18
  285.6 28.1 %collective-permute-start.24 = (bf16[80,4096]{1,0:T(8,128)(2,1)}, bf16[80,4096]{1,0:T(8,128)(2,1)}, u32[]{:S(2)}, u32[]{:S(2)}) collective-permute-start(bf16[80,4096]{1,0:T(8,128)(2,1)} %get-tuple-element.11), channel_id=1, source_target_pairs={{0,24},{4,28},{8,16},{12,20},{16,8},{20,12},{24,0},{28,4},{1,25},{... | collective-permute-start | bytes 1966088 | tf_op jit(solution)/shard_map/ppermute | solution.py:18
  285.6 41.0 %collective-permute-start.33 = (bf16[80,4096]{1,0:T(8,128)(2,1)}, bf16[80,4096]{1,0:T(8,128)(2,1)}, u32[]{:S(2)}, u32[]{:S(2)}) collective-permute-start(bf16[80,4096]{1,0:T(8,128)(2,1)} %get-tuple-element.17), channel_id=1, source_target_pairs={{0,8},{4,12},{8,0},{12,4},{16,24},{20,28},{24,16},{28,20},{1,9},{5... | collective-permute-start | bytes 1966088 | tf_op jit(solution)/shard_map/ppermute | solution.py:18
  306.0 35.6 %collective-permute-start.34 = (bf16[80,4096]{1,0:T(8,128)(2,1)S(1)}, bf16[80,4096]{1,0:T(8,128)(2,1)S(1)}, u32[]{:S(2)}, u32[]{:S(2)}) collective-permute-start(bf16[80,4096]{1,0:T(8,128)(2,1)S(1)} %copy-done.12), channel_id=1, source_target_pairs={{0,16},{4,20},{8,24},{12,28},{16,0},{20,4},{24,8},{28,12},{1,17},{... | collective-permute-start | bytes 1966088 | tf_op jit(solution)/shard_map/ppermute | solution.py:18
  313.7 27.9 %collective-permute-start.35 = (bf16[80,4096]{1,0:T(8,128)(2,1)S(1)}, bf16[80,4096]{1,0:T(8,128)(2,1)S(1)}, u32[]{:S(2)}, u32[]{:S(2)}) collective-permute-start(bf16[80,4096]{1,0:T(8,128)(2,1)S(1)} %copy-done.11), channel_id=1, source_target_pairs={{0,24},{4,28},{8,16},{12,20},{16,8},{20,12},{24,0},{28,4},{1,25},{... | collective-permute-start | bytes 1966088 | tf_op jit(solution)/shard_map/ppermute | solution.py:18
  313.7 40.9 %collective-permute-start.44 = (bf16[80,4096]{1,0:T(8,128)(2,1)S(1)}, bf16[80,4096]{1,0:T(8,128)(2,1)S(1)}, u32[]{:S(2)}, u32[]{:S(2)}) collective-permute-start(bf16[80,4096]{1,0:T(8,128)(2,1)S(1)} %get-tuple-element.21), channel_id=1, source_target_pairs={{0,8},{4,12},{8,0},{12,4},{16,24},{20,28},{24,16},{28,20},{1,9},{5... | collective-permute-start | bytes 1966088 | tf_op jit(solution)/shard_map/ppermute | solution.py:18
  317.4 24.2 %copy-start.10 = (bf16[80,4096]{1,0:T(8,128)(2,1)S(1)}, bf16[80,4096]{1,0:T(8,128)(2,1)}, u32[]{:S(2)}) copy-start(bf16[80,4096]{1,0:T(8,128)(2,1)} %get-tuple-element.14) | copy-start | bytes 1966084
  317.4 24.2 %copy-start.18 = (bf16[320,256]{1,0:T(8,128)(2,1)S(1)}, bf16[320,256]{1,0:T(8,128)(2,1)}, u32[]{:S(2)}) copy-start(bf16[320,256]{1,0:T(8,128)(2,1)} %get-tuple-element.50) | copy-start | bytes 491524
  326.5 42.2 %collective-permute-start.45 = (bf16[80,4096]{1,0:T(8,128)(2,1)S(1)}, bf16[80,4096]{1,0:T(8,128)(2,1)S(1)}, u32[]{:S(2)}, u32[]{:S(2)}) collective-permute-start(bf16[80,4096]{1,0:T(8,128)(2,1)S(1)} %get-tuple-element.20), channel_id=1, source_target_pairs={{0,16},{4,20},{8,24},{12,28},{16,0},{20,4},{24,8},{28,12},{1,17},{... | collective-permute-start | bytes 1966088 | tf_op jit(solution)/shard_map/ppermute | solution.py:18
  341.6 27.2 %collective-permute-start.46 = (bf16[80,4096]{1,0:T(8,128)(2,1)S(1)}, bf16[80,4096]{1,0:T(8,128)(2,1)S(1)}, u32[]{:S(2)}, u32[]{:S(2)}) collective-permute-start(bf16[80,4096]{1,0:T(8,128)(2,1)S(1)} %get-tuple-element.19), channel_id=1, source_target_pairs={{0,24},{4,28},{8,16},{12,20},{16,8},{20,12},{24,0},{28,4},{1,25},{... | collective-permute-start | bytes 1966088 | tf_op jit(solution)/shard_map/ppermute | solution.py:18
  341.6 30.5 %collective-permute-start.25 = (bf16[128,4096]{1,0:T(8,128)(2,1)S(1)}, bf16[128,4096]{1,0:T(8,128)(2,1)S(1)}, u32[]{:S(2)}, u32[]{:S(2)}) collective-permute-start(bf16[128,4096]{1,0:T(8,128)(2,1)S(1)} %slice.300), channel_id=1, source_target_pairs={{0,4},{4,0},{8,12},{12,8},{16,20},{20,16},{24,28},{28,24},{1,5},{5... | collective-permute-start | bytes 3145736 | tf_op jit(solution)/shard_map/ppermute | solution.py:18
  344.1 24.6 %copy-start.16 = (bf16[320,256]{1,0:T(8,128)(2,1)S(1)}, bf16[320,256]{1,0:T(8,128)(2,1)}, u32[]{:S(2)}) copy-start(bf16[320,256]{1,0:T(8,128)(2,1)} %get-tuple-element.49) | copy-start | bytes 491524
  354.6 38.7 %collective-permute-start.15 = (bf16[128,4096]{1,0:T(8,128)(2,1)S(1)}, bf16[128,4096]{1,0:T(8,128)(2,1)S(1)}, u32[]{:S(2)}, u32[]{:S(2)}) collective-permute-start(bf16[128,4096]{1,0:T(8,128)(2,1)S(1)} %copy-done.9), channel_id=1, source_target_pairs={{0,4},{4,0},{8,12},{12,8},{16,20},{20,16},{24,28},{28,24},{1,5},{5... | collective-permute-start | bytes 3145736 | tf_op jit(solution)/shard_map/ppermute | solution.py:18
  368.8 3.6 collective-permute-start.36
  371.5 3.2 collective-permute-start.47
  372.3 44.1 %collective-permute-start.26 = (bf16[128,4096]{1,0:T(8,128)(2,1)S(1)}, bf16[128,4096]{1,0:T(8,128)(2,1)S(1)}, u32[]{:S(2)}, u32[]{:S(2)}) collective-permute-start(bf16[128,4096]{1,0:T(8,128)(2,1)S(1)} %fusion.38), channel_id=1, source_target_pairs={{0,1},{1,0},{2,3},{3,2},{4,5},{5,4},{6,7},{7,6},{8,9},{9,8},{10,11... | collective-permute-start | bytes 3145736 | tf_op jit(solution)/shard_map/ppermute | solution.py:18
  372.6 70.7 %collective-permute-start.37 = (bf16[128,4096]{1,0:T(8,128)(2,1)S(1)}, bf16[128,4096]{1,0:T(8,128)(2,1)S(1)}, u32[]{:S(2)}, u32[]{:S(2)}) collective-permute-start(bf16[128,4096]{1,0:T(8,128)(2,1)S(1)} %fusion.37), channel_id=1, source_target_pairs={{0,2},{1,3},{2,0},{3,1},{4,6},{5,7},{6,4},{7,5},{8,10},{9,11},{10,... | collective-permute-start | bytes 3145736 | tf_op jit(solution)/shard_map/ppermute | solution.py:18
  375.9 90.5 %collective-permute-start.48 = (bf16[128,4096]{1,0:T(8,128)(2,1)}, bf16[128,4096]{1,0:T(8,128)(2,1)S(1)}, u32[]{:S(2)}, u32[]{:S(2)}) collective-permute-start(bf16[128,4096]{1,0:T(8,128)(2,1)} %fusion.36), channel_id=1, source_target_pairs={{0,3},{1,2},{2,1},{3,0},{4,7},{5,6},{6,5},{7,4},{8,11},{9,10},{10,... | collective-permute-start | bytes 3145736 | tf_op jit(solution)/shard_map/ppermute | solution.py:18
  379.4 87.0 %copy-start.7 = (f32[256,4096]{1,0:T(8,128)S(1)}, f32[256,4096]{1,0:T(8,128)}, u32[]{:S(2)}) copy-start(f32[256,4096]{1,0:T(8,128)} %copy-done.6) | copy-start | bytes 12582916
  379.4 88.7 %copy-start.1 = (bf16[64,512]{1,0:T(8,128)(2,1)S(1)}, bf16[64,512]{1,0:T(8,128)(2,1)}, u32[]{:S(2)}) copy-start(bf16[64,512]{1,0:T(8,128)(2,1)} %param.10) | copy-start | bytes 196612
  (25 other events, 92.1 us)

commit v2 on v1

v2 whole, which is shorter than its diff:
```python
import functools
import math

import jax
import jax.numpy as jnp
from jax import lax
from jax.experimental import pallas as pl
from jax.experimental.pallas import tpu as pltpu
from jax.sharding import PartitionSpec as P

HEAD_WIDTH = 128
F32 = jnp.float32
BF16 = jnp.bfloat16
VMEM = 48 * 1024 * 1024
COSTS = {"pack1": 20, "pack2": 20, "pack3": 20, "ffn2": 15, "ffn3": 20}
COSTS.update({f"combine{s}": 40 for s in range(4)})


def cost(name):
    work = 1024 + int(COSTS.get(name, 0.0) * 1.0e9)
    return pl.CostEstimate(flops=work, bytes_accessed=1024, transcendentals=0)


PARAMS = pltpu.CompilerParams(vmem_limit_bytes=VMEM)
ANYWHERE = pl.BlockSpec(memory_space=pl.ANY)


def swap(value, axis, offset):
    count = lax.axis_size(axis)
    return lax.ppermute(value, axis, [(i, i ^ offset) for i in range(count)])


def exchange(value):
    return lax.all_to_all(value, "ctx", split_axis=0, concat_axis=0, tiled=True)


def gate(name, value, after):
    return pl.pallas_call(
        lambda value_ref, after_ref, out_ref: None,
        in_specs=[ANYWHERE, ANYWHERE],
        out_specs=ANYWHERE,
        out_shape=jax.ShapeDtypeStruct(value.shape, value.dtype),
        input_output_aliases={0: 0},
        cost_estimate=cost(name),
    )(value, after)


def attention_kernel(heads, blocks, rows, q_ref, kv_ref, after_ref, arrived_ref, out_ref):
    exp = lax.axis_size("exp")
    ctx = lax.axis_size("ctx")
    z = lax.axis_index("exp")
    q = q_ref[...].reshape(blocks * rows, heads * HEAD_WIDTH)
    query = jnp.concatenate(
        [q[:, h * HEAD_WIDTH : (h + 1) * HEAD_WIDTH] for h in range(heads)], axis=0
    )
    scores = lax.dot_general(
        query, kv_ref[:, :HEAD_WIDTH], (((1,), (1,)), ((), ())), preferred_element_type=F32
    ) * (1.0 / math.sqrt(HEAD_WIDTH))
    shape = (1, scores.shape[1])
    place = lax.broadcasted_iota(jnp.int32, shape, 1)
    block = place // rows
    position = ((block % ctx) * exp + ((block // ctx) ^ z)) * rows + place % rows
    shape = (scores.shape[0], 1)
    row = lax.broadcasted_iota(jnp.int32, shape, 0) % (blocks * rows)
    query_block = pl.program_id(0) * blocks + row // rows
    query_position = (query_block * exp + z) * rows + row % rows
    scores = jnp.where(position <= query_position, scores, -1e30)
    row_max = jnp.max(scores, axis=1, keepdims=True)
    probs = jnp.exp(scores - row_max).astype(BF16)
    total = jnp.sum(probs.astype(F32), axis=1, keepdims=True)
    summed = jnp.dot(probs, kv_ref[:, HEAD_WIDTH:], preferred_element_type=F32)
    result = (summed / total).astype(BF16)
    here = blocks * rows
    out_ref[...] = jnp.concatenate(
        [result[h * here : (h + 1) * here] for h in range(heads)], axis=1
    ).reshape(out_ref.shape)


def attend(queries, line, after, arrived):
    ctx, rows, width = queries.shape
    blocks = max(1, ctx // 4)
    return pl.pallas_call(
        functools.partial(attention_kernel, width // HEAD_WIDTH, blocks, rows),
        grid=(ctx // blocks,),
        in_specs=[
            pl.BlockSpec((blocks, rows, width), lambda g: (g, 0, 0)),
            pl.BlockSpec(line.shape, lambda g: (0, 0)),
            ANYWHERE,
            ANYWHERE,
        ],
        out_specs=pl.BlockSpec((blocks, rows, width), lambda g: (g, 0, 0)),
        out_shape=jax.ShapeDtypeStruct(queries.shape, BF16),
        compiler_params=PARAMS,
        cost_estimate=cost("attend"),
    )(queries, line, after, arrived)


def slot_matrix(meta_ref, plan, weighted):
    places, capacity, top, rows = plan
    tokens = meta_ref.shape[1]
    z, exp = lax.axis_index("exp"), lax.axis_size("exp")
    ids = meta_ref[:top]
    weights = meta_ref[top:]
    members, scales = [], []
    for m in range(places):
        hit = ids == (m * exp + z).astype(F32)
        members.append(jnp.sum(jnp.where(hit, 1.0, 0.0), axis=0, keepdims=True))
        scales.append(jnp.sum(jnp.where(hit, weights, 0.0), axis=0, keepdims=True))
    member = jnp.concatenate(members, axis=0)
    first = lax.broadcasted_iota(jnp.int32, (tokens, tokens), 0)
    second = lax.broadcasted_iota(jnp.int32, (tokens, tokens), 1)
    before = jnp.where(first < second, 1.0, 0.0).astype(BF16)
    rank = jnp.dot(member.astype(BF16), before, preferred_element_type=F32)
    rank = jnp.where(member > 0.5, rank, -1.0).astype(jnp.int32)
    slot = lax.broadcasted_iota(jnp.int32, (rows, tokens), 0)
    return jnp.concatenate(
        [
            jnp.where(slot == rank[m : m + 1], scales[m] if weighted else 1.0, 0.0)
            for m in range(places)
        ],
        axis=0,
    )


def pack_kernel(plan, copies, meta_ref, after_ref, arrived_ref, *refs):
    halves, refs = refs[:2], refs[2:]
    if copies:
        refs[3][...] = refs[0][...]
        refs[4][...] = refs[1][...]
        refs = (refs[2], refs[-1])
    out_ref, pick_ref = refs

    @pl.when(pl.program_id(0) == 0)
    def _():
        pick_ref[...] = slot_matrix(meta_ref, plan, False).astype(BF16)

    block = jnp.concatenate([ref[...] for ref in halves], axis=0)
    out_ref[...] = jnp.dot(pick_ref[...], block, preferred_element_type=F32).astype(BF16)


def pack(stage, meta, halves, after, arrived, extra, plan):
    places, capacity, top, rows = plan
    half, width = halves[0].shape
    columns = width // 4
    tile = pl.BlockSpec((half, columns), lambda i: (0, i))
    operands = [meta, after, arrived, *halves]
    in_specs = [pl.BlockSpec(meta.shape, lambda i: (0, 0)), ANYWHERE, ANYWHERE, tile, tile]
    out_specs = [pl.BlockSpec((places * rows, columns), lambda i: (0, i))]
    out_shape = [jax.ShapeDtypeStruct((places * rows, width), BF16)]
    if extra is not None:
        operands += extra
        in_specs += [tile, tile]
        out_specs += [tile, tile]
        out_shape += [jax.ShapeDtypeStruct((half, width), BF16)] * 2
    return pl.pallas_call(
        functools.partial(pack_kernel, plan, extra is not None),
        grid=(width // columns,),
        in_specs=in_specs,
        out_specs=out_specs,
        out_shape=out_shape,
        scratch_shapes=[pltpu.VMEM((places * rows, 2 * half), BF16)],
        compiler_params=PARAMS,
        cost_estimate=cost(f"pack{stage}"),
    )(*operands)


def ffn_kernel(x_ref, gate_ref, up_ref, down_ref, after_ref, out_ref, total_ref):
    step, last = pl.program_id(0), pl.num_programs(0) - 1
    x = x_ref[...]
    gated = jnp.dot(x, gate_ref[0], preferred_element_type=F32)
    up = jnp.dot(x, up_ref[0], preferred_element_type=F32)
    hidden = (gated / (1.0 + jnp.exp(-gated)) * up).astype(BF16)
    term = jnp.dot(hidden, down_ref[0], preferred_element_type=F32)

    @pl.when(step == 0)
    def _():
        total_ref[...] = term

    @pl.when((step > 0) & (step < last))
    def _():
        total_ref[...] += term

    @pl.when(step == last)
    def _():
        out_ref[...] = (total_ref[...] + term).astype(BF16)


def ffn(stage, x, w_gate, w_up, w_down, after):
    rows, width = x.shape
    hidden = w_gate.shape[2]
    block = 256
    whole = pl.BlockSpec((rows, width), lambda i: (0, 0))
    return pl.pallas_call(
        ffn_kernel,
        grid=(hidden // block,),
        in_specs=[
            whole,
            pl.BlockSpec((1, width, block), lambda i: (0, 0, i)),
            pl.BlockSpec((1, width, block), lambda i: (0, 0, i)),
            pl.BlockSpec((1, block, width), lambda i: (0, i, 0)),
            ANYWHERE,
        ],
        out_specs=whole,
        out_shape=jax.ShapeDtypeStruct((rows, width), BF16),
        scratch_shapes=[pltpu.VMEM((rows, width), F32)],
        compiler_params=PARAMS,
        cost_estimate=cost(f"ffn{stage}"),
    )(x, w_gate, w_up, w_down, after)


def combine_kernel(plan, meta_ref, back_ref, after_ref, *refs):
    outs, (high_ref, low_ref) = refs[:-2], refs[-2:]

    @pl.when(pl.program_id(0) == 0)
    def _():
        scale = slot_matrix(meta_ref, plan, True)
        high = scale.astype(BF16)
        high_ref[...] = high
        low_ref[...] = (scale - high.astype(F32)).astype(BF16)

    back = back_ref[...]
    contract = (((0,), (0,)), ((), ()))
    mixed = lax.dot_general(high_ref[...], back, contract, preferred_element_type=F32)
    mixed = mixed + lax.dot_general(low_ref[...], back, contract, preferred_element_type=F32)
    rows = outs[0].shape[0]
    for index, ref in enumerate(outs):
        ref[...] = mixed[index * rows : (index + 1) * rows].astype(ref.dtype)


def combine(stage, meta, back, after, outs, dtype, plan):
    tokens = meta.shape[1]
    slots, width = back.shape
    columns = width // 4
    return pl.pallas_call(
        functools.partial(combine_kernel, plan),
        grid=(width // columns,),
        in_specs=[
            pl.BlockSpec(meta.shape, lambda i: (0, 0)),
            pl.BlockSpec((slots, columns), lambda i: (0, i)),
            ANYWHERE,
        ],
        out_specs=[pl.BlockSpec((tokens // outs, columns), lambda i: (0, i))] * outs,
        out_shape=[jax.ShapeDtypeStruct((tokens // outs, width), dtype)] * outs,
        scratch_shapes=[pltpu.VMEM((slots, tokens), BF16)] * 2,
        compiler_params=PARAMS,
        cost_estimate=cost(f"combine{stage}"),
    )(meta, back, after)


def finish_kernel(pieces, own_ref, *refs):
    out_ref = refs[-1]
    parts = [jnp.concatenate([refs[i][...] for i in group], axis=0) for group in pieces]
    total = own_ref[...]
    for part in parts:
        total = total + part.astype(F32)
    out_ref[...] = total.astype(BF16)


def finish(own, parts):
    tokens, width = own.shape
    columns = width // 4
    tile = pl.BlockSpec((tokens, columns), lambda i: (0, i))
    flat = [piece for part in parts for piece in part]
    pieces, start = [], 0
    for part in parts:
        pieces.append(range(start, start + len(part)))
        start += len(part)
    return pl.pallas_call(
        functools.partial(finish_kernel, pieces),
        grid=(width // columns,),
        in_specs=[tile]
        + [pl.BlockSpec((piece.shape[0], columns), lambda i: (0, i)) for piece in flat],
        out_specs=tile,
        out_shape=jax.ShapeDtypeStruct(own.shape, BF16),
        compiler_params=PARAMS,
        cost_estimate=cost("finish"),
    )(own, *flat)


def body(queries, keys, values, moe_rows, expert_ids, route_weights, w_gate, w_up, w_down):
    ctx, exp = lax.axis_size("ctx"), lax.axis_size("exp")
    sequence, query_width = queries.shape
    kv_heads = keys.shape[1] // HEAD_WIDTH
    tokens, width = moe_rows.shape
    top = expert_ids.shape[1]
    capacity = max(2, tokens * top * 5 // (4 * ctx * exp))
    rows = -(-capacity // 8) * 8
    plan = (ctx, capacity, top, rows)

    meta = jnp.concatenate([expert_ids.astype(F32).T, route_weights.T], axis=0)
    metas = [meta] + [swap(meta, "exp", s) for s in range(1, exp)]
    mine = [moe_rows[: tokens // 2], moe_rows[tokens // 2 :]]

    q = queries.reshape(sequence, ctx, query_width // ctx).transpose(1, 0, 2)
    k = keys.reshape(sequence, kv_heads, HEAD_WIDTH).transpose(1, 0, 2)
    v = values.reshape(sequence, kv_heads, HEAD_WIDTH).transpose(1, 0, 2)
    kv = jnp.repeat(jnp.concatenate([k, v], axis=2), ctx // kv_heads, axis=0)
    heads = exchange(jnp.concatenate([q, kv], axis=2))
    local_queries = heads[:, :, : query_width // ctx]
    local_kv = heads[:, :, query_width // ctx :].reshape(ctx * sequence, 2 * HEAD_WIDTH)

    sent, served, partial, arrived = {}, {}, {}, {0: mine}
    state = {"after": queries, "held": mine}

    def dispatch(s):
        if s > 0:
            source = state["held"] if s > 2 else mine
            arrived[s] = [swap(part, "exp", s) for part in source]
        earlier = sent[s - 2] if s > 1 else heads if s == 1 else queries
        result = pack(
            s, metas[s], arrived[s], state["after"], earlier, mine if s == 1 else None, plan
        )
        if s == 1:
            state["held"] = result[1:]
        sent[s] = exchange(result[0].reshape(ctx, rows, width))
        state["after"] = result[0]

    def serve(s):
        x = sent[s].reshape(ctx * rows, width)
        served[s] = ffn(s, x, w_gate, w_up, w_down, state["after"])
        state["after"] = served[s]

    def give_back(s, arrived):
        out = served[s] if arrived is None else gate(f"back{s}", served[s], arrived)
        served[s] = exchange(out.reshape(ctx, rows, width))

    def collect(s):
        back = served[s].reshape(ctx * rows, width)
        if s == 0:
            partial[s] = combine(s, metas[s], back, state["after"], 1, F32, plan)
        else:
            outs = combine(s, metas[s], back, state["after"], 1 if s == 1 else 2, BF16, plan)
            partial[s] = [swap(out, "exp", s) for out in outs]
            state["after"] = outs[0]

    dispatch(0)
    dispatch(1)
    serve(0)
    dispatch(2)
    serve(1)
    for s in range(3, exp):
        dispatch(s)
    held_kv = gate("kv", local_kv, state["after"])
    state["after"] = held_kv
    line = jnp.concatenate([held_kv] + [swap(held_kv, "exp", s) for s in range(1, exp)], axis=0)
    serve(2)
    attended = attend(local_queries, line, state["after"], sent[exp - 1])
    state["after"] = attended
    for s in range(3, exp):
        serve(s)
    order = list(range(2, exp)) + [1, 0]
    arrived_back = None
    for s in order:
        give_back(s, arrived_back)
        arrived_back = served[s]
    output = exchange(gate("out", attended, arrived_back))
    for s in order:
        collect(s)
    mixed = finish(partial[0][0], [partial[s] for s in range(1, exp)])
    return (output.transpose(1, 0, 2).reshape(sequence, query_width), mixed)


def solution(mesh):
    row = P(("ctx", "exp"), None)
    cube = P(("ctx", "exp"), None, None)
    return jax.shard_map(
        body,
        mesh=mesh,
        in_specs=(row,) * 6 + (cube,) * 3,
        out_specs=(row, row),
        check_vma=False,
    )
```

time: 478 us -> 344 us (0.72)
  waiting for transfers between devices: 277 us -> 137 us
  matrix products: 98.2 us -> 0 us
  Pallas kernels: 13.9 us -> 94 us
  starting transfers between devices: 40.5 us -> 74.3 us
  other arithmetic: 14.2 us -> 2.41 us
  local copies, waits for them, and re-layouts: 23 us -> 29.6 us
    ppermute x49 -> x17, waiting for transfers between devices: 277 us -> 30.9 us  [swap(): return lax.ppermute(value, axis, [(i, i ^ offset) for i in range(count)])]
    all_to_all x0 -> x10, waiting for transfers between devices: none -> 106 us  [exchange(): return lax.all_to_all(value, 'ctx', split_axis=0, concat_axis=0, tiled=True)]
    dot_general x36 -> x0, matrix products: 98.2 us -> none  [the longest x4 47.2 us: ffn(): return jnp.dot(hidden, w_down[0], preferred_element_type=F32).astype(BF16)]
    pallas_call x1 -> x19, Pallas kernels: 13.9 us -> 94 us  [the longest x4 46.2 us: ffn(): pl.pallas_call(ffn_kernel, grid=(hidden // block,), in_specs=[whole, pl.B...]
    all_to_all x0 -> x10, starting transfers between devices: none -> 51.2 us  [exchange(): return lax.all_to_all(value, 'ctx', split_axis=0, concat_axis=0, tiled=True)]
    ppermute x49 -> x17, starting transfers between devices: 40.5 us -> 23.1 us  [swap(): return lax.ppermute(value, axis, [(i, i ^ offset) for i in range(count)])]
    unnamed x84 -> x53, local copies, waits for them, and re-layouts: 8.95 us -> 24 us
    slice x16 -> x3, local copies, waits for them, and re-layouts: 7.99 us -> 1.84 us  [the longest x1 1.09 us: body(): mine = [moe_rows[:tokens // 2], moe_rows[tokens // 2:]]]
  transfers between devices with their start and end apart: 49 -> 27, of which waited for: 22 -> 11; matrix products, arithmetic and copies ran while one was open for 28% -> 1% of each run, Pallas kernels for 3% -> 28%
where the time goes in v2:
time: 344 us; the launch traced here: 338 us
  waiting for transfers between devices  137 us (40%)
  Pallas kernels  94 us (27%)
  starting transfers between devices  74.3 us (22%)
  local copies, waits for them, and re-layouts  29.6 us (9%)
    all_to_all x10, waiting for transfers between devices, exchange(): return lax.all_to_all(value, 'ctx', split_axis=0, concat_axis=0, tiled=True)  106 us
    all_to_all x10, starting transfers between devices, exchange(): return lax.all_to_all(value, 'ctx', split_axis=0, concat_axis=0, tiled=True)  51.2 us
    pallas_call x4, Pallas kernels, ffn(): pl.pallas_call(ffn_kernel, grid=(hidden // block,), in_specs=[whole, pl.B...  46.2 us
    ppermute x17, waiting for transfers between devices, swap(): return lax.ppermute(value, axis, [(i, i ^ offset) for i in range(count)])  30.9 us
    unnamed x53, local copies, waits for them, and re-layouts  24 us
    ppermute x17, starting transfers between devices, swap(): return lax.ppermute(value, axis, [(i, i ^ offset) for i in range(count)])  23.1 us
    pallas_call x4, Pallas kernels, pack(): pl.pallas_call(functools.partial(pack_kernel, plan, extra is not None), g...  15.7 us
    pallas_call x4, Pallas kernels, combine(): pl.pallas_call(functools.partial(combine_kernel, plan), grid=(width // co...  14.9 us
  transfers between devices with their start and end apart: 27, of which 11 were waited for; matrix products, arithmetic and copies ran while one was open for 1% of the time, Pallas kernels for 28%

profile of v2, /device:TPU:12, one launch (start us, length us, event | category | flops | bytes accessed | tf_op | source)
XLA Modules:
  0.0 338.1 jit_solution(13605394645405435288)
XLA Ops:
  0.6 0.9 reshape.71
  1.5 0.9 reshape.72
  2.5 1.1 copy.23
  3.7 0.9 pad_maximum_fusion.1
  4.6 4.2 %all-to-all-start = ((bf16[8,64,768]{2,1,0:T(8,128)(2,1)}), bf16[8,64,768]{2,1,0:T(8,128)(2,1)S(1)}, u32[]{:S(2)}, u32[]{:S(2)}) async-start(bf16[8,64,768]{2,1,0:T(8,128)(2,1)} %pad_maximum_fusion.1), calls=%async_computation | async-start | bytes 1572864 | tf_op jit(solution)/shard_map/all_to_all | solution.py:34
  8.9 1.1 fusion
  10.4 1.6 collective-permute-start.3
  12.0 3.2 shard_map.104.after_ref
  15.2 1.5 copy-done.7
  16.7 3.3 all-to-all-done.arrived_ref
  20.0 5.0 %all-to-all-start.2 = ((bf16[8,40,4096]{2,1,0:T(8,128)(2,1)}), bf16[8,40,4096]{2,1,0:T(8,128)(2,1)S(1)}, u32[]{:S(2)}, u32[]{:S(2)}) async-start(bf16[8,40,4096]{2,1,0:T(8,128)(2,1)} %bitcast.38), calls=%async_computation.2 | async-start | bytes 5242880 | tf_op jit(solution)/shard_map/all_to_all | solution.py:34
  25.5 2.6 collective-permute-start.5
  28.4 12.6 %collective-permute-done.1.meta_ref = f32[16,128]{1,0:T(8,128)S(1)} collective-permute-done((f32[16,128]{1,0:T(8,128)S(1)}, f32[16,128]{1,0:T(8,128)S(1)}, u32[]{:S(2)}, u32[]{:S(2)}) %collective-permute-start.1) | collective-permute-done | bytes 8224 | tf_op jit(solution)/shard_map/ppermute | solution.py:30
  41.0 4.8 %shard_map.105 = (bf16[320,4096]{1,0:T(8,128)(2,1)}, bf16[64,4096]{1,0:T(8,128)(2,1)S(1)}, bf16[64,4096]{1,0:T(8,128)(2,1)S(1)}) custom-call(f32[16,128]{1,0:T(8,128)S(1)} %collective-permute-done.1.meta_ref, bf16[320,4096]{1,0:T(8,128)(2,1)} %copy-done.7, bf16[8,64,768]{2,1,0:T(8,128)(2,1)S(1)} %all-to-all-done.arrived_ref, ...), custom_call_target="tpu_custom_call" | custom-call | flops 20000002048 | bytes 1024 | tf_op jit(solution)/shard_map/pallas_call | solution.py:155
  48.0 7.8 %all-to-all-done.2.arrived_ref = bf16[8,40,4096]{2,1,0:T(8,128)(2,1)S(1)} async-done(((bf16[8,40,4096]{2,1,0:T(8,128)(2,1)}), bf16[8,40,4096]{2,1,0:T(8,128)(2,1)S(1)}, u32[]{:S(2)}, u32[]{:S(2)}) %all-to-all-start.2) | async-done | bytes 2621472 | tf_op jit(solution)/shard_map/all_to_all | solution.py:34
  55.8 5.8 %all-to-all-start.1 = ((bf16[8,40,4096]{2,1,0:T(8,128)(2,1)}), bf16[8,40,4096]{2,1,0:T(8,128)(2,1)}, u32[]{:S(2)}, u32[]{:S(2)}) async-start(bf16[8,40,4096]{2,1,0:T(8,128)(2,1)} %bitcast.46), calls=%async_computation.1 | async-start | bytes 5242880 | tf_op jit(solution)/shard_map/all_to_all | solution.py:34
  61.6 2.6 collective-permute-start.4
  64.2 2.0 collective-permute-start.8
  66.2 11.2 %shard_map.106.after_ref.value_ref = bf16[320,4096]{1,0:T(8,128)(2,1)S(1)} custom-call(bf16[320,4096]{1,0:T(8,128)(2,1)S(1)} %bitcast.35, bf16[1,4096,768]{2,1,0:T(8,128)(2,1)} %gate_ref.7, bf16[1,4096,768]{2,1,0:T(8,128)(2,1)} %up_ref.7, bf16[1,768,4096]{2,1,0:T(8,128)(2,1)} %down_ref.7, bf16[320,4096]{1,0:T(8,128)(2,1)} %get-tuple-element.9.after_ref), custom_call_target="tpu_custom_call" | custom-call | flops 1024 | bytes 1024 | tf_op jit(solution)/shard_map/pallas_call | solution.py:193
  77.4 1.5 copy-done
  78.9 18.3 %collective-permute-done.4.meta_ref = f32[16,128]{1,0:T(8,128)S(1)} collective-permute-done((f32[16,128]{1,0:T(8,128)S(1)}, f32[16,128]{1,0:T(8,128)S(1)}, u32[]{:S(2)}, u32[]{:S(2)}) %collective-permute-start.4) | collective-permute-done | bytes 8224 | tf_op jit(solution)/shard_map/ppermute | solution.py:30
  97.1 4.5 %shard_map.107.after_ref = bf16[320,4096]{1,0:T(8,128)(2,1)} custom-call(f32[16,128]{1,0:T(8,128)S(1)} %collective-permute-done.4.meta_ref, bf16[320,4096]{1,0:T(8,128)(2,1)} %copy-done, bf16[8,40,4096]{2,1,0:T(8,128)(2,1)} %copy-done.2, bf16[64,4096]{1,0:T(8,128)(2,1)} %collective-permute-done.5.refs_0_, bf16[64,4096]{1,0:T(8,128)(2,1)} %collective-permute-done.6.refs_1_), custom_call_target="tpu_custom_call" | custom-call | flops 20000002048 | bytes 1024 | tf_op jit(solution)/shard_map/pallas_call | solution.py:155
  101.6 4.2 %all-to-all-start.3 = ((bf16[8,40,4096]{2,1,0:T(8,128)(2,1)}), bf16[8,40,4096]{2,1,0:T(8,128)(2,1)S(1)}, u32[]{:S(2)}, u32[]{:S(2)}) async-start(bf16[8,40,4096]{2,1,0:T(8,128)(2,1)} %bitcast.11), calls=%async_computation.3 | async-start | bytes 5242880 | tf_op jit(solution)/shard_map/all_to_all | solution.py:34
  106.3 12.5 %shard_map.108.after_ref.value_ref = bf16[320,4096]{1,0:T(8,128)(2,1)S(1)} custom-call(bf16[320,4096]{1,0:T(8,128)(2,1)} %bitcast.8.x_ref, bf16[1,4096,768]{2,1,0:T(8,128)(2,1)} %gate_ref.7, bf16[1,4096,768]{2,1,0:T(8,128)(2,1)} %up_ref.7, bf16[1,768,4096]{2,1,0:T(8,128)(2,1)} %down_ref.7, bf16[320,4096]{1,0:T(8,128)(2,1)} %shard_map.107.after_ref), custom_call_target="tpu_custom_call" | custom-call | flops 1024 | bytes 1024 | tf_op jit(solution)/shard_map/pallas_call | solution.py:193
  118.9 1.5 copy-done.1
  120.3 3.2 shard_map.109.after_ref
  123.6 1.5 copy-done.8
  125.1 11.5 %all-to-all-done.3 = bf16[8,40,4096]{2,1,0:T(8,128)(2,1)S(1)} async-done(((bf16[8,40,4096]{2,1,0:T(8,128)(2,1)}), bf16[8,40,4096]{2,1,0:T(8,128)(2,1)S(1)}, u32[]{:S(2)}, u32[]{:S(2)}) %all-to-all-start.3) | async-done | bytes 2621472 | tf_op jit(solution)/shard_map/all_to_all | solution.py:34
  136.7 1.6 copy-done.15
  138.2 5.0 %all-to-all-start.4 = ((bf16[8,40,4096]{2,1,0:T(8,128)(2,1)}), bf16[8,40,4096]{2,1,0:T(8,128)(2,1)S(1)}, u32[]{:S(2)}, u32[]{:S(2)}) async-start(bf16[8,40,4096]{2,1,0:T(8,128)(2,1)} %bitcast.39), calls=%async_computation.4 | async-start | bytes 5242880 | tf_op jit(solution)/shard_map/all_to_all | solution.py:34
  143.9 3.4 %collective-permute-start.10 = (bf16[512,256]{1,0:T(8,128)(2,1)}, bf16[512,256]{1,0:T(8,128)(2,1)}, u32[]{:S(2)}, u32[]{:S(2)}) collective-permute-start(bf16[512,256]{1,0:T(8,128)(2,1)} %shard_map.110.after_ref), channel_id=1, source_target_pairs={{0,2},{1,3},{2,0},{3,1},{4,6},{5,7},{6,4},{7,5},{8,10},{9,11},{10,... | collective-permute-start | bytes 786440 | tf_op jit(solution)/shard_map/ppermute | solution.py:30
  147.8 1.0 collective-permute-start.9
  148.8 1.7 copy-done.16
  150.5 0.9 copy-done.18
  151.5 11.2 %shard_map.111.after_ref = bf16[320,4096]{1,0:T(8,128)(2,1)S(1)} custom-call(bf16[320,4096]{1,0:T(8,128)(2,1)S(1)} %bitcast.43, bf16[1,4096,768]{2,1,0:T(8,128)(2,1)} %gate_ref.7, bf16[1,4096,768]{2,1,0:T(8,128)(2,1)} %up_ref.7, bf16[1,768,4096]{2,1,0:T(8,128)(2,1)} %down_ref.7, bf16[512,256]{1,0:T(8,128)(2,1)S(1)} %copy-done.18), custom_call_target="tpu_custom_call" | custom-call | flops 15000000512 | bytes 1024 | tf_op jit(solution)/shard_map/pallas_call | solution.py:193
  162.7 1.5 copy-done.5
  164.2 9.8 %all-to-all-done.4.arrived_ref = bf16[8,40,4096]{2,1,0:T(8,128)(2,1)S(1)} async-done(((bf16[8,40,4096]{2,1,0:T(8,128)(2,1)}), bf16[8,40,4096]{2,1,0:T(8,128)(2,1)S(1)}, u32[]{:S(2)}, u32[]{:S(2)}) %all-to-all-start.4) | async-done | bytes 2621472 | tf_op jit(solution)/shard_map/all_to_all | solution.py:34
  174.0 1.6 copy-done.3
  175.6 5.8 %all-to-all-start.5 = ((bf16[8,40,4096]{2,1,0:T(8,128)(2,1)}), bf16[8,40,4096]{2,1,0:T(8,128)(2,1)}, u32[]{:S(2)}, u32[]{:S(2)}) async-start(bf16[8,40,4096]{2,1,0:T(8,128)(2,1)} %bitcast.37), calls=%async_computation.5 | async-start | bytes 5242880 | tf_op jit(solution)/shard_map/all_to_all | solution.py:34
  181.5 1.4 pad_maximum_fusion.kv_ref
  183.4 13.2 %shard_map.112.after_ref.value_ref = bf16[8,64,512]{2,1,0:T(8,128)(2,1)S(1)} custom-call(bf16[8,64,512]{2,1,0:T(8,128)(2,1)S(1)} %slice.16.q_ref, bf16[2048,256]{1,0:T(8,128)(2,1)S(1)} %pad_maximum_fusion.kv_ref, bf16[320,4096]{1,0:T(8,128)(2,1)S(1)} %copy-done.6, bf16[8,40,4096]{2,1,0:T(8,128)(2,1)} %copy-done.3), custom_call_target="tpu_custom_call" | custom-call | flops 1024 | bytes 1024 | tf_op jit(solution)/shard_map/pallas_call | solution.py:82
  196.6 11.3 %shard_map.113.after_ref = bf16[320,4096]{1,0:T(8,128)(2,1)S(1)} custom-call(bf16[320,4096]{1,0:T(8,128)(2,1)S(1)} %bitcast.36, bf16[1,4096,768]{2,1,0:T(8,128)(2,1)} %gate_ref.7, bf16[1,4096,768]{2,1,0:T(8,128)(2,1)} %up_ref.7, bf16[1,768,4096]{2,1,0:T(8,128)(2,1)} %down_ref.7, bf16[8,64,512]{2,1,0:T(8,128)(2,1)S(1)} %shard_map.112.after_ref.value_ref), custom_call_target="tpu_custom_call" | custom-call | flops 20000002048 | bytes 1024 | tf_op jit(solution)/shard_map/pallas_call | solution.py:193
  208.0 1.6 copy-done.17
  209.6 1.5 copy.25.value_ref
  211.1 1.2 all-to-all-done.5.after_ref
  212.3 5.0 %all-to-all-start.6 = ((bf16[8,40,4096]{2,1,0:T(8,128)(2,1)}), bf16[8,40,4096]{2,1,0:T(8,128)(2,1)S(1)}, u32[]{:S(2)}, u32[]{:S(2)}) async-start(bf16[8,40,4096]{2,1,0:T(8,128)(2,1)} %bitcast.45), calls=%async_computation.6 | async-start | bytes 5242880 | tf_op jit(solution)/shard_map/all_to_all | solution.py:34
  217.3 4.7 %shard_map.118 = (bf16[64,4096]{1,0:T(8,128)(2,1)}, bf16[64,4096]{1,0:T(8,128)(2,1)}) custom-call(f32[16,128]{1,0:T(8,128)S(1)} %collective-permute-done.4.meta_ref, bf16[320,4096]{1,0:T(8,128)(2,1)} %bitcast.23.back_ref, bf16[320,4096]{1,0:T(8,128)(2,1)} %copy-done.17), custom_call_target="tpu_custom_call" | custom-call | flops 40000000000 | bytes 1024 | tf_op jit(solution)/shard_map/pallas_call | solution.py:234
  222.0 3.4 %collective-permute-start.13 = (bf16[64,4096]{1,0:T(8,128)(2,1)}, bf16[64,4096]{1,0:T(8,128)(2,1)S(1)}, u32[]{:S(2)}, u32[]{:S(2)}) collective-permute-start(bf16[64,4096]{1,0:T(8,128)(2,1)} %get-tuple-element.12.after_ref), channel_id=1, source_target_pairs={{0,2},{1,3},{2,0},{3,1},{4,6},{5,7},{6,4},{7,5},{8,10},{9,11},{10,... | collective-permute-start | bytes 1572872 | tf_op jit(solution)/shard_map/ppermute | solution.py:30
  225.4 22.7 %all-to-all-done.6.after_ref = bf16[8,40,4096]{2,1,0:T(8,128)(2,1)S(1)} async-done(((bf16[8,40,4096]{2,1,0:T(8,128)(2,1)}), bf16[8,40,4096]{2,1,0:T(8,128)(2,1)S(1)}, u32[]{:S(2)}, u32[]{:S(2)}) %all-to-all-start.6) | async-done | bytes 2621472 | tf_op jit(solution)/shard_map/all_to_all | solution.py:34
  248.1 1.6 copy-done.11
  249.7 6.0 %all-to-all-start.7 = ((bf16[8,40,4096]{2,1,0:T(8,128)(2,1)}), bf16[8,40,4096]{2,1,0:T(8,128)(2,1)}, u32[]{:S(2)}, u32[]{:S(2)}) async-start(bf16[8,40,4096]{2,1,0:T(8,128)(2,1)} %bitcast.34), calls=%async_computation.7 | async-start | bytes 5242880 | tf_op jit(solution)/shard_map/all_to_all | solution.py:34
  255.7 3.1 shard_map.119
  259.3 1.6 collective-permute-start.16
  260.9 25.7 %all-to-all-done.7.after_ref = bf16[8,40,4096]{2,1,0:T(8,128)(2,1)} async-done(((bf16[8,40,4096]{2,1,0:T(8,128)(2,1)}), bf16[8,40,4096]{2,1,0:T(8,128)(2,1)}, u32[]{:S(2)}, u32[]{:S(2)}) %all-to-all-start.7) | async-done | bytes 2621472 | tf_op jit(solution)/shard_map/all_to_all | solution.py:34
  286.6 5.2 %all-to-all-start.8 = ((bf16[8,40,4096]{2,1,0:T(8,128)(2,1)}), bf16[8,40,4096]{2,1,0:T(8,128)(2,1)S(1)}, u32[]{:S(2)}, u32[]{:S(2)}) async-start(bf16[8,40,4096]{2,1,0:T(8,128)(2,1)} %bitcast.33), calls=%async_computation.8 | async-start | bytes 5242880 | tf_op jit(solution)/shard_map/all_to_all | solution.py:34
  291.8 4.7 %shard_map.120.after_ref = bf16[128,4096]{1,0:T(8,128)(2,1)} custom-call(f32[16,128]{1,0:T(8,128)S(1)} %copy-done.22, bf16[320,4096]{1,0:T(8,128)(2,1)} %bitcast.21.back_ref, bf16[64,4096]{1,0:T(8,128)(2,1)} %get-tuple-element.13.after_ref), custom_call_target="tpu_custom_call" | custom-call | flops 40000000000 | bytes 1024 | tf_op jit(solution)/shard_map/pallas_call | solution.py:234
  296.5 2.4 collective-permute-start.12
  298.9 23.7 %all-to-all-done.8.after_ref = bf16[8,40,4096]{2,1,0:T(8,128)(2,1)S(1)} async-done(((bf16[8,40,4096]{2,1,0:T(8,128)(2,1)}), bf16[8,40,4096]{2,1,0:T(8,128)(2,1)S(1)}, u32[]{:S(2)}, u32[]{:S(2)}) %all-to-all-start.8) | async-done | bytes 2621472 | tf_op jit(solution)/shard_map/all_to_all | solution.py:34
  322.6 1.5 copy-done.9
  324.0 4.9 %all-to-all-start.9 = ((bf16[8,64,512]{2,1,0:T(8,128)(2,1)}), bf16[8,64,512]{2,1,0:T(8,128)(2,1)S(1)}, u32[]{:S(2)}, u32[]{:S(2)}) async-start(bf16[8,64,512]{2,1,0:T(8,128)(2,1)} %shard_map.117), calls=%async_computation.9 | async-start | bytes 1048576 | tf_op jit(solution)/shard_map/all_to_all | solution.py:34
  328.9 1.7 copy-done.10
  330.7 2.4 shard_map.121.own_ref
  333.1 4.0 %shard_map.122 = bf16[128,4096]{1,0:T(8,128)(2,1)} custom-call(f32[128,4096]{1,0:T(8,128)S(1)} %shard_map.121.own_ref, bf16[128,4096]{1,0:T(8,128)(2,1)} %collective-permute-done.12.refs_0_, bf16[64,4096]{1,0:T(8,128)(2,1)S(1)} %collective-permute-done.13.refs_1_, bf16[64,4096]{1,0:T(8,128)(2,1)} %collective-permute-done.14.refs_2_, ...), custom_call_target="tpu_custom_call" | custom-call | flops 1024 | bytes 1024 | tf_op jit(solution)/shard_map/pallas_call | solution.py:268
  337.2 0.8 copy.21
  (76 shorter events, 6.5 us)
Async XLA Ops:
  1.5 7.4 %copy-start.23 = (bf16[128,4096]{1,0:T(8,128)(2,1)S(1)}, bf16[128,4096]{1,0:T(8,128)(2,1)}, u32[]{:S(2)}) copy-start(bf16[128,4096]{1,0:T(8,128)(2,1)} %param.12) | copy-start | bytes 3145732
  3.7 8.3 %copy-start.24 = (s32[128,8]{0,1:T(8,128)S(1)}, s32[128,8]{0,1:T(8,128)}, u32[]{:S(2)}) copy-start(s32[128,8]{0,1:T(8,128)} %param.13) | copy-start | bytes 12292
  3.7 8.3 %copy-start.25 = (f32[128,8]{0,1:T(8,128)S(1)}, f32[128,8]{0,1:T(8,128)}, u32[]{:S(2)}) copy-start(f32[128,8]{0,1:T(8,128)} %param.14) | copy-start | bytes 12292
  3.7 8.3 %copy-start.14 = (bf16[64,4096]{1,0:T(8,128)(2,1)S(1)}, bf16[64,4096]{1,0:T(8,128)(2,1)}, u32[]{:S(2)}) copy-start(bf16[64,4096]{1,0:T(8,128)(2,1)} %arrived_ref.1) | copy-start | bytes 1572868
  4.6 15.4 %all-to-all-start = ((bf16[8,64,768]{2,1,0:T(8,128)(2,1)}), bf16[8,64,768]{2,1,0:T(8,128)(2,1)S(1)}, u32[]{:S(2)}, u32[]{:S(2)}) async-start(bf16[8,64,768]{2,1,0:T(8,128)(2,1)} %pad_maximum_fusion.1), calls=%async_computation | async-start | bytes 1572864 | tf_op jit(solution)/shard_map/all_to_all | solution.py:34
  10.0 31.1 %collective-permute-start.2 = (bf16[64,4096]{1,0:T(8,128)(2,1)}, bf16[64,4096]{1,0:T(8,128)(2,1)}, u32[]{:S(2)}, u32[]{:S(2)}) collective-permute-start(bf16[64,4096]{1,0:T(8,128)(2,1)} %get-tuple-element.17.refs_0_.refs_2_), channel_id=1, source_target_pairs={{0,1},{1,0},{2,3},{3,2},{4,5},{5,4},{6,7},{7,6},{8,9},{9,8},{10,11... | collective-permute-start | bytes 1572872 | tf_op jit(solution)/shard_map/ppermute | solution.py:30
  10.4 30.6 %collective-permute-start.3 = (bf16[64,4096]{1,0:T(8,128)(2,1)}, bf16[64,4096]{1,0:T(8,128)(2,1)}, u32[]{:S(2)}, u32[]{:S(2)}) collective-permute-start(bf16[64,4096]{1,0:T(8,128)(2,1)} %get-tuple-element.16.refs_1_.refs_3_), channel_id=1, source_target_pairs={{0,1},{1,0},{2,3},{3,2},{4,5},{5,4},{6,7},{7,6},{8,9},{9,8},{10,11... | collective-permute-start | bytes 1572872 | tf_op jit(solution)/shard_map/ppermute | solution.py:30
  15.2 1.5 copy-start.7
  20.0 35.8 %all-to-all-start.2 = ((bf16[8,40,4096]{2,1,0:T(8,128)(2,1)}), bf16[8,40,4096]{2,1,0:T(8,128)(2,1)S(1)}, u32[]{:S(2)}, u32[]{:S(2)}) async-start(bf16[8,40,4096]{2,1,0:T(8,128)(2,1)} %bitcast.38), calls=%async_computation.2 | async-start | bytes 5242880 | tf_op jit(solution)/shard_map/all_to_all | solution.py:34
  25.0 16.0 %collective-permute-start.1 = (f32[16,128]{1,0:T(8,128)S(1)}, f32[16,128]{1,0:T(8,128)S(1)}, u32[]{:S(2)}, u32[]{:S(2)}) collective-permute-start(f32[16,128]{1,0:T(8,128)S(1)} %pad_maximum_fusion.3.meta_ref), channel_id=1, source_target_pairs={{0,1},{1,0},{2,3},{3,2},{4,5},{5,4},{6,7},{7,6},{8,9},{9,8},{10,11... | collective-permute-start | bytes 24584 | tf_op jit(solution)/shard_map/ppermute | solution.py:30
  25.5 71.7 %collective-permute-start.5 = (bf16[64,4096]{1,0:T(8,128)(2,1)}, bf16[64,4096]{1,0:T(8,128)(2,1)}, u32[]{:S(2)}, u32[]{:S(2)}) collective-permute-start(bf16[64,4096]{1,0:T(8,128)(2,1)} %get-tuple-element.17.refs_0_.refs_2_), channel_id=1, source_target_pairs={{0,2},{1,3},{2,0},{3,1},{4,6},{5,7},{6,4},{7,5},{8,10},{9,11},{10,... | collective-permute-start | bytes 1572872 | tf_op jit(solution)/shard_map/ppermute | solution.py:30
  28.1 69.1 %collective-permute-start.6 = (bf16[64,4096]{1,0:T(8,128)(2,1)}, bf16[64,4096]{1,0:T(8,128)(2,1)}, u32[]{:S(2)}, u32[]{:S(2)}) collective-permute-start(bf16[64,4096]{1,0:T(8,128)(2,1)} %get-tuple-element.16.refs_1_.refs_3_), channel_id=1, source_target_pairs={{0,2},{1,3},{2,0},{3,1},{4,6},{5,7},{6,4},{7,5},{8,10},{9,11},{10,... | collective-permute-start | bytes 1572872 | tf_op jit(solution)/shard_map/ppermute | solution.py:30
  45.8 0.8 copy-start.19
  46.6 0.8 copy-start.20
  47.4 0.6 copy-start.21
  55.8 10.4 %copy-start.2 = (bf16[8,40,4096]{2,1,0:T(8,128)(2,1)}, bf16[8,40,4096]{2,1,0:T(8,128)(2,1)S(1)}, u32[]{:S(2)}) copy-start(bf16[8,40,4096]{2,1,0:T(8,128)(2,1)S(1)} %all-to-all-done.2.arrived_ref) | copy-start | bytes 7864324
  55.8 45.8 %all-to-all-start.1 = ((bf16[8,40,4096]{2,1,0:T(8,128)(2,1)}), bf16[8,40,4096]{2,1,0:T(8,128)(2,1)}, u32[]{:S(2)}, u32[]{:S(2)}) async-start(bf16[8,40,4096]{2,1,0:T(8,128)(2,1)} %bitcast.46), calls=%async_computation.1 | async-start | bytes 5242880 | tf_op jit(solution)/shard_map/all_to_all | solution.py:34
  61.6 35.5 %collective-permute-start.4 = (f32[16,128]{1,0:T(8,128)S(1)}, f32[16,128]{1,0:T(8,128)S(1)}, u32[]{:S(2)}, u32[]{:S(2)}) collective-permute-start(f32[16,128]{1,0:T(8,128)S(1)} %pad_maximum_fusion.3.meta_ref), channel_id=1, source_target_pairs={{0,2},{1,3},{2,0},{3,1},{4,6},{5,7},{6,4},{7,5},{8,10},{9,11},{10,... | collective-permute-start | bytes 24584 | tf_op jit(solution)/shard_map/ppermute | solution.py:30
  64.2 56.2 %collective-permute-start.7 = (bf16[64,4096]{1,0:T(8,128)(2,1)}, bf16[64,4096]{1,0:T(8,128)(2,1)}, u32[]{:S(2)}, u32[]{:S(2)}) collective-permute-start(bf16[64,4096]{1,0:T(8,128)(2,1)} %copy-done.20), channel_id=1, source_target_pairs={{0,3},{1,2},{2,1},{3,0},{4,7},{5,6},{6,5},{7,4},{8,11},{9,10},{10,... | collective-permute-start | bytes 1572872 | tf_op jit(solution)/shard_map/ppermute | solution.py:30
  64.2 56.2 %collective-permute-start.8 = (bf16[64,4096]{1,0:T(8,128)(2,1)}, bf16[64,4096]{1,0:T(8,128)(2,1)}, u32[]{:S(2)}, u32[]{:S(2)}) collective-permute-start(bf16[64,4096]{1,0:T(8,128)(2,1)} %copy-done.19), channel_id=1, source_target_pairs={{0,3},{1,2},{2,1},{3,0},{4,7},{5,6},{6,5},{7,4},{8,11},{9,10},{10,... | collective-permute-start | bytes 1572872 | tf_op jit(solution)/shard_map/ppermute | solution.py:30
  77.4 1.5 copy-start
  101.6 35.0 %all-to-all-start.3 = ((bf16[8,40,4096]{2,1,0:T(8,128)(2,1)}), bf16[8,40,4096]{2,1,0:T(8,128)(2,1)S(1)}, u32[]{:S(2)}, u32[]{:S(2)}) async-start(bf16[8,40,4096]{2,1,0:T(8,128)(2,1)} %bitcast.11), calls=%async_computation.3 | async-start | bytes 5242880 | tf_op jit(solution)/shard_map/all_to_all | solution.py:34
  105.9 14.5 %collective-permute-start = (f32[16,128]{1,0:T(8,128)S(1)}, f32[16,128]{1,0:T(8,128)S(1)}, u32[]{:S(2)}, u32[]{:S(2)}) collective-permute-start(f32[16,128]{1,0:T(8,128)S(1)} %pad_maximum_fusion.3.meta_ref), channel_id=1, source_target_pairs={{0,3},{1,2},{2,1},{3,0},{4,7},{5,6},{6,5},{7,4},{8,11},{9,10},{10,... | collective-permute-start | bytes 24584 | tf_op jit(solution)/shard_map/ppermute | solution.py:30
  118.9 1.5 copy-start.1
  123.6 1.6 copy-start.8
  136.6 1.6 copy-start.15
  138.2 35.8 %all-to-all-start.4 = ((bf16[8,40,4096]{2,1,0:T(8,128)(2,1)}), bf16[8,40,4096]{2,1,0:T(8,128)(2,1)S(1)}, u32[]{:S(2)}, u32[]{:S(2)}) async-start(bf16[8,40,4096]{2,1,0:T(8,128)(2,1)} %bitcast.39), calls=%async_computation.4 | async-start | bytes 5242880 | tf_op jit(solution)/shard_map/all_to_all | solution.py:34
  143.9 37.5 %collective-permute-start.10 = (bf16[512,256]{1,0:T(8,128)(2,1)}, bf16[512,256]{1,0:T(8,128)(2,1)}, u32[]{:S(2)}, u32[]{:S(2)}) collective-permute-start(bf16[512,256]{1,0:T(8,128)(2,1)} %shard_map.110.after_ref), channel_id=1, source_target_pairs={{0,2},{1,3},{2,0},{3,1},{4,6},{5,7},{6,4},{7,5},{8,10},{9,11},{10,... | collective-permute-start | bytes 786440 | tf_op jit(solution)/shard_map/ppermute | solution.py:30
  147.3 34.1 %collective-permute-start.11 = (bf16[512,256]{1,0:T(8,128)(2,1)}, bf16[512,256]{1,0:T(8,128)(2,1)}, u32[]{:S(2)}, u32[]{:S(2)}) collective-permute-start(bf16[512,256]{1,0:T(8,128)(2,1)} %shard_map.110.after_ref), channel_id=1, source_target_pairs={{0,3},{1,2},{2,1},{3,0},{4,7},{5,6},{6,5},{7,4},{8,11},{9,10},{10,... | collective-permute-start | bytes 786440 | tf_op jit(solution)/shard_map/ppermute | solution.py:30
  147.8 33.7 %collective-permute-start.9 = (bf16[512,256]{1,0:T(8,128)(2,1)}, bf16[512,256]{1,0:T(8,128)(2,1)}, u32[]{:S(2)}, u32[]{:S(2)}) collective-permute-start(bf16[512,256]{1,0:T(8,128)(2,1)} %shard_map.110.after_ref), channel_id=1, source_target_pairs={{0,1},{1,0},{2,3},{3,2},{4,5},{5,4},{6,7},{7,6},{8,9},{9,8},{10,11... | collective-permute-start | bytes 786440 | tf_op jit(solution)/shard_map/ppermute | solution.py:30
  148.8 1.7 copy-start.16
  150.5 0.9 copy-start.18
  162.7 1.6 copy-start.5
  174.0 1.6 copy-start.3
  175.6 36.7 %all-to-all-start.5 = ((bf16[8,40,4096]{2,1,0:T(8,128)(2,1)}), bf16[8,40,4096]{2,1,0:T(8,128)(2,1)}, u32[]{:S(2)}, u32[]{:S(2)}) async-start(bf16[8,40,4096]{2,1,0:T(8,128)(2,1)} %bitcast.37), calls=%async_computation.5 | async-start | bytes 5242880 | tf_op jit(solution)/shard_map/all_to_all | solution.py:34
  181.4 2.1 copy-start.6
  183.4 13.2 %copy-start.4 = (bf16[8,40,4096]{2,1,0:T(8,128)(2,1)S(1)}, bf16[8,40,4096]{2,1,0:T(8,128)(2,1)}, u32[]{:S(2)}) copy-start(bf16[8,40,4096]{2,1,0:T(8,128)(2,1)} %copy-done.3) | copy-start | bytes 7864324
  196.6 11.4 %copy-start.13 = (bf16[8,64,512]{2,1,0:T(8,128)(2,1)}, bf16[8,64,512]{2,1,0:T(8,128)(2,1)S(1)}, u32[]{:S(2)}) copy-start(bf16[8,64,512]{2,1,0:T(8,128)(2,1)S(1)} %shard_map.112.after_ref.value_ref) | copy-start | bytes 1572868
  208.0 1.6 copy-start.17
  212.3 35.8 %all-to-all-start.6 = ((bf16[8,40,4096]{2,1,0:T(8,128)(2,1)}), bf16[8,40,4096]{2,1,0:T(8,128)(2,1)S(1)}, u32[]{:S(2)}, u32[]{:S(2)}) async-start(bf16[8,40,4096]{2,1,0:T(8,128)(2,1)} %bitcast.45), calls=%async_computation.6 | async-start | bytes 5242880 | tf_op jit(solution)/shard_map/all_to_all | solution.py:34
  222.0 111.0 %collective-permute-start.13 = (bf16[64,4096]{1,0:T(8,128)(2,1)}, bf16[64,4096]{1,0:T(8,128)(2,1)S(1)}, u32[]{:S(2)}, u32[]{:S(2)}) collective-permute-start(bf16[64,4096]{1,0:T(8,128)(2,1)} %get-tuple-element.12.after_ref), channel_id=1, source_target_pairs={{0,2},{1,3},{2,0},{3,1},{4,6},{5,7},{6,4},{7,5},{8,10},{9,11},{10,... | collective-permute-start | bytes 1572872 | tf_op jit(solution)/shard_map/ppermute | solution.py:30
  225.4 107.7 %collective-permute-start.14 = (bf16[64,4096]{1,0:T(8,128)(2,1)}, bf16[64,4096]{1,0:T(8,128)(2,1)}, u32[]{:S(2)}, u32[]{:S(2)}) collective-permute-start(bf16[64,4096]{1,0:T(8,128)(2,1)} %get-tuple-element.14), channel_id=1, source_target_pairs={{0,2},{1,3},{2,0},{3,1},{4,6},{5,7},{6,4},{7,5},{8,10},{9,11},{10,... | collective-permute-start | bytes 1572872 | tf_op jit(solution)/shard_map/ppermute | solution.py:30
  248.1 1.6 copy-start.11
  249.7 6.1 %copy-start.12 = (bf16[8,40,4096]{2,1,0:T(8,128)(2,1)S(1)}, bf16[8,40,4096]{2,1,0:T(8,128)(2,1)}, u32[]{:S(2)}) copy-start(bf16[8,40,4096]{2,1,0:T(8,128)(2,1)} %copy-done.11) | copy-start | bytes 7864324
  249.7 36.9 %all-to-all-start.7 = ((bf16[8,40,4096]{2,1,0:T(8,128)(2,1)}), bf16[8,40,4096]{2,1,0:T(8,128)(2,1)}, u32[]{:S(2)}, u32[]{:S(2)}) async-start(bf16[8,40,4096]{2,1,0:T(8,128)(2,1)} %bitcast.34), calls=%async_computation.7 | async-start | bytes 5242880 | tf_op jit(solution)/shard_map/all_to_all | solution.py:34
  258.9 74.2 %collective-permute-start.15 = (bf16[64,4096]{1,0:T(8,128)(2,1)}, bf16[64,4096]{1,0:T(8,128)(2,1)}, u32[]{:S(2)}, u32[]{:S(2)}) collective-permute-start(bf16[64,4096]{1,0:T(8,128)(2,1)} %get-tuple-element.13.after_ref), channel_id=1, source_target_pairs={{0,3},{1,2},{2,1},{3,0},{4,7},{5,6},{6,5},{7,4},{8,11},{9,10},{10,... | collective-permute-start | bytes 1572872 | tf_op jit(solution)/shard_map/ppermute | solution.py:30
  259.3 73.8 %collective-permute-start.16 = (bf16[64,4096]{1,0:T(8,128)(2,1)}, bf16[64,4096]{1,0:T(8,128)(2,1)}, u32[]{:S(2)}, u32[]{:S(2)}) collective-permute-start(bf16[64,4096]{1,0:T(8,128)(2,1)} %get-tuple-element.15), channel_id=1, source_target_pairs={{0,3},{1,2},{2,1},{3,0},{4,7},{5,6},{6,5},{7,4},{8,11},{9,10},{10,... | collective-permute-start | bytes 1572872 | tf_op jit(solution)/shard_map/ppermute | solution.py:30
  286.6 5.2 %copy-start.22 = (f32[16,128]{1,0:T(8,128)S(1)}, f32[16,128]{1,0:T(8,128)}, u32[]{:S(2)}) copy-start(f32[16,128]{1,0:T(8,128)} %copy-done.21) | copy-start | bytes 24580
  286.6 36.0 %all-to-all-start.8 = ((bf16[8,40,4096]{2,1,0:T(8,128)(2,1)}), bf16[8,40,4096]{2,1,0:T(8,128)(2,1)S(1)}, u32[]{:S(2)}, u32[]{:S(2)}) async-start(bf16[8,40,4096]{2,1,0:T(8,128)(2,1)} %bitcast.33), calls=%async_computation.8 | async-start | bytes 5242880 | tf_op jit(solution)/shard_map/all_to_all | solution.py:34
  296.5 36.6 %collective-permute-start.12 = (bf16[128,4096]{1,0:T(8,128)(2,1)}, bf16[128,4096]{1,0:T(8,128)(2,1)}, u32[]{:S(2)}, u32[]{:S(2)}) collective-permute-start(bf16[128,4096]{1,0:T(8,128)(2,1)} %shard_map.120.after_ref), channel_id=1, source_target_pairs={{0,1},{1,0},{2,3},{3,2},{4,5},{5,4},{6,7},{7,6},{8,9},{9,8},{10,11... | collective-permute-start | bytes 3145736 | tf_op jit(solution)/shard_map/ppermute | solution.py:30
  322.6 1.5 copy-start.9
  324.0 13.2 %all-to-all-start.9 = ((bf16[8,64,512]{2,1,0:T(8,128)(2,1)}), bf16[8,64,512]{2,1,0:T(8,128)(2,1)S(1)}, u32[]{:S(2)}, u32[]{:S(2)}) async-start(bf16[8,64,512]{2,1,0:T(8,128)(2,1)} %shard_map.117), calls=%async_computation.9 | async-start | bytes 1048576 | tf_op jit(solution)/shard_map/all_to_all | solution.py:34
  328.9 1.7 copy-start.10

commit v3 on v2

v3 whole, which is shorter than its diff:
```python
import functools
import math

import jax
import jax.numpy as jnp
from jax import lax
from jax.experimental import pallas as pl
from jax.experimental.pallas import tpu as pltpu
from jax.sharding import PartitionSpec as P

HEAD_WIDTH = 128
F32 = jnp.float32
BF16 = jnp.bfloat16
VMEM = 48 * 1024 * 1024
COSTS = {"pack1": 20, "pack2": 20, "pack3": 20, "ffn2": 15, "ffn3": 20, "heads": 20}
COSTS.update({f"combine{s}": 40 for s in range(4)})


def cost(name):
    work = 1024 + int(COSTS.get(name, 0.0) * 1.0e9)
    return pl.CostEstimate(flops=work, bytes_accessed=1024, transcendentals=0)


PARAMS = pltpu.CompilerParams(vmem_limit_bytes=VMEM)
ANYWHERE = pl.BlockSpec(memory_space=pl.ANY)
TOKEN = pl.BlockSpec((8, 128), lambda *step: (0, 0))
TOKEN_SHAPE = jax.ShapeDtypeStruct((8, 128), F32)


def swap(value, axis, offset):
    count = lax.axis_size(axis)
    return lax.ppermute(value, axis, [(i, i ^ offset) for i in range(count)])


def exchange(value):
    return lax.all_to_all(value, "ctx", split_axis=0, concat_axis=0, tiled=True)


def gate(name, values, after):
    return pl.pallas_call(
        lambda *refs: None,
        in_specs=[ANYWHERE] * (len(values) + 1),
        out_specs=[ANYWHERE] * len(values),
        out_shape=[jax.ShapeDtypeStruct(value.shape, value.dtype) for value in values],
        input_output_aliases={i: i for i in range(len(values))},
        cost_estimate=cost(name),
    )(*values, after)


def attention_kernel(heads, blocks, rows, q_ref, kv_ref, after_ref, out_ref, token_ref):
    token_ref[...] = jnp.zeros(token_ref.shape, F32)
    exp = lax.axis_size("exp")
    ctx = lax.axis_size("ctx")
    z = lax.axis_index("exp")
    q = q_ref[...].reshape(blocks * rows, heads * HEAD_WIDTH)
    query = jnp.concatenate(
        [q[:, h * HEAD_WIDTH : (h + 1) * HEAD_WIDTH] for h in range(heads)], axis=0
    )
    scores = lax.dot_general(
        query, kv_ref[:, :HEAD_WIDTH], (((1,), (1,)), ((), ())), preferred_element_type=F32
    ) * (1.0 / math.sqrt(HEAD_WIDTH))
    shape = (1, scores.shape[1])
    place = lax.broadcasted_iota(jnp.int32, shape, 1)
    block = place // rows
    position = ((block % ctx) * exp + ((block // ctx) ^ z)) * rows + place % rows
    shape = (scores.shape[0], 1)
    row = lax.broadcasted_iota(jnp.int32, shape, 0) % (blocks * rows)
    query_block = pl.program_id(0) * blocks + row // rows
    query_position = (query_block * exp + z) * rows + row % rows
    scores = jnp.where(position <= query_position, scores, -1e30)
    row_max = jnp.max(scores, axis=1, keepdims=True)
    probs = jnp.exp(scores - row_max).astype(BF16)
    total = jnp.sum(probs.astype(F32), axis=1, keepdims=True)
    summed = jnp.dot(probs, kv_ref[:, HEAD_WIDTH:], preferred_element_type=F32)
    result = (summed / total).astype(BF16)
    here = blocks * rows
    out_ref[...] = jnp.concatenate(
        [result[h * here : (h + 1) * here] for h in range(heads)], axis=1
    ).reshape(out_ref.shape)


def attend(queries, line, after):
    ctx, rows, width = queries.shape
    blocks = max(1, ctx // 4)
    return pl.pallas_call(
        functools.partial(attention_kernel, width // HEAD_WIDTH, blocks, rows),
        grid=(ctx // blocks,),
        in_specs=[
            pl.BlockSpec((blocks, rows, width), lambda g: (g, 0, 0)),
            pl.BlockSpec(line.shape, lambda g: (0, 0)),
            ANYWHERE,
        ],
        out_specs=[pl.BlockSpec((blocks, rows, width), lambda g: (g, 0, 0)), TOKEN],
        out_shape=[jax.ShapeDtypeStruct(queries.shape, BF16), TOKEN_SHAPE],
        compiler_params=PARAMS,
        cost_estimate=cost("attend"),
    )(queries, line, after)


def slot_matrix(meta_ref, plan, weighted, relative=False):
    places, capacity, top, rows = plan
    tokens = meta_ref.shape[1]
    z, exp = lax.axis_index("exp"), lax.axis_size("exp")
    ids = meta_ref[:top]
    weights = meta_ref[top:]
    members, scales = [], []
    here = lax.axis_index("ctx") if relative else 0
    for m in range(places):
        hit = ids == ((here ^ m) * exp + z).astype(F32)
        members.append(jnp.sum(jnp.where(hit, 1.0, 0.0), axis=0, keepdims=True))
        scales.append(jnp.sum(jnp.where(hit, weights, 0.0), axis=0, keepdims=True))
    member = jnp.concatenate(members, axis=0)
    first = lax.broadcasted_iota(jnp.int32, (tokens, tokens), 0)
    second = lax.broadcasted_iota(jnp.int32, (tokens, tokens), 1)
    before = jnp.where(first < second, 1.0, 0.0).astype(BF16)
    rank = jnp.dot(member.astype(BF16), before, preferred_element_type=F32)
    rank = jnp.where(member > 0.5, rank, -1.0).astype(jnp.int32)
    slot = lax.broadcasted_iota(jnp.int32, (rows, tokens), 0)
    return jnp.concatenate(
        [
            jnp.where(slot == rank[m : m + 1], scales[m] if weighted else 1.0, 0.0)
            for m in range(places)
        ],
        axis=0,
    )


def pack_kernel(plan, count, other, meta_ref, after_ref, arrived_ref, *refs):
    pieces, refs = refs[:count], refs[count:]
    block = jnp.concatenate([ref[...] for ref in pieces], axis=0)
    held = block
    if other:
        held, refs = refs[0][...], refs[1:]
    out_ref, token_ref, *copies, pick_ref = refs
    token_ref[...] = jnp.zeros(token_ref.shape, F32)

    @pl.when(pl.program_id(0) == 0)
    def _():
        pick_ref[...] = slot_matrix(meta_ref, plan, False).astype(BF16)

    out_ref[...] = jnp.dot(pick_ref[...], block, preferred_element_type=F32).astype(BF16)
    start = 0
    for ref in copies:
        ref[...] = held[start % held.shape[0] :][: ref.shape[0]]
        start += ref.shape[0]


def pack(stage, meta, pieces, after, arrived, other, cuts, plan):
    places, capacity, top, rows = plan
    tokens, width = meta.shape[1], pieces[0].shape[1]
    columns = width // 4

    def tile(size):
        return pl.BlockSpec((size, columns), lambda i: (0, i))

    operands = [meta, after, arrived, *pieces]
    in_specs = [pl.BlockSpec(meta.shape, lambda i: (0, 0)), ANYWHERE, ANYWHERE]
    in_specs += [tile(piece.shape[0]) for piece in pieces]
    if other is not None:
        operands.append(other)
        in_specs.append(tile(tokens))
    out_specs = [tile(places * rows), TOKEN] + [tile(size) for size in cuts]
    out_shape = [jax.ShapeDtypeStruct((places * rows, width), BF16), TOKEN_SHAPE]
    out_shape += [jax.ShapeDtypeStruct((size, width), BF16) for size in cuts]
    return pl.pallas_call(
        functools.partial(pack_kernel, plan, len(pieces), other is not None),
        grid=(width // columns,),
        in_specs=in_specs,
        out_specs=out_specs,
        out_shape=out_shape,
        scratch_shapes=[pltpu.VMEM((places * rows, tokens), BF16)],
        compiler_params=PARAMS,
        cost_estimate=cost(f"pack{stage}"),
    )(*operands)


def ffn_kernel(split, x_ref, gate_ref, up_ref, down_ref, after_ref, *refs):
    *outs, token_ref, total_ref = refs
    token_ref[...] = jnp.zeros(token_ref.shape, F32)
    step, last = pl.program_id(0), pl.num_programs(0) - 1
    x = x_ref[...]
    gated = jnp.dot(x, gate_ref[0], preferred_element_type=F32)
    up = jnp.dot(x, up_ref[0], preferred_element_type=F32)
    hidden = (gated / (1.0 + jnp.exp(-gated)) * up).astype(BF16)
    term = jnp.dot(hidden, down_ref[0], preferred_element_type=F32)

    @pl.when(step == 0)
    def _():
        total_ref[...] = term

    @pl.when((step > 0) & (step < last))
    def _():
        total_ref[...] += term

    @pl.when(step == last)
    def _():
        if not split:
            outs[0][...] = (total_ref[...] + term).astype(BF16)
        else:
            total_ref[...] += term
            rows = outs[0].shape[0]
            for m, out_ref in enumerate(outs):
                start = pl.multiple_of((lax.axis_index("ctx") ^ m) * rows, 8)
                out_ref[...] = total_ref[pl.ds(start, rows)].astype(BF16)


def ffn(stage, x, w_gate, w_up, w_down, after, split):
    rows, width = x.shape
    hidden = w_gate.shape[2]
    block = 256
    whole = pl.BlockSpec((rows, width), lambda i: (0, 0))
    part = pl.BlockSpec((rows // split, width), lambda i: (0, 0))
    return pl.pallas_call(
        functools.partial(ffn_kernel, split > 1),
        grid=(hidden // block,),
        in_specs=[
            whole,
            pl.BlockSpec((1, width, block), lambda i: (0, 0, i)),
            pl.BlockSpec((1, width, block), lambda i: (0, 0, i)),
            pl.BlockSpec((1, block, width), lambda i: (0, i, 0)),
            ANYWHERE,
        ],
        out_specs=[part] * split + [TOKEN],
        out_shape=[jax.ShapeDtypeStruct((rows // split, width), BF16)] * split + [TOKEN_SHAPE],
        scratch_shapes=[pltpu.VMEM((rows, width), F32)],
        compiler_params=PARAMS,
        cost_estimate=cost(f"ffn{stage}"),
    )(x, w_gate, w_up, w_down, after)


def combine_kernel(plan, backs, count, meta_ref, after_ref, *refs):
    back_refs, pieces, refs = refs[:backs], refs[backs : backs + count], refs[backs + count :]
    outs, (token_ref, high_ref, low_ref) = refs[:-3], refs[-3:]
    token_ref[...] = jnp.zeros(token_ref.shape, F32)

    @pl.when(pl.program_id(0) == 0)
    def _():
        scale = slot_matrix(meta_ref, plan, True, backs > 1)
        high = scale.astype(BF16)
        high_ref[...] = high
        low_ref[...] = (scale - high.astype(F32)).astype(BF16)

    back = back_refs[0][...]
    if backs > 1:
        parts = [ref[...].astype(F32) for ref in back_refs]
        back = jnp.concatenate(parts, axis=0).astype(BF16)
    contract = (((0,), (0,)), ((), ()))
    mixed = lax.dot_general(high_ref[...], back, contract, preferred_element_type=F32)
    mixed = mixed + lax.dot_general(low_ref[...], back, contract, preferred_element_type=F32)
    if count:
        mixed = mixed + jnp.concatenate([ref[...] for ref in pieces], axis=0).astype(F32)
    rows = outs[0].shape[0]
    for index, ref in enumerate(outs):
        ref[...] = mixed[index * rows : (index + 1) * rows].astype(ref.dtype)


def combine(stage, meta, backs, after, pieces, outs, dtype, plan):
    tokens = meta.shape[1]
    width = backs[0].shape[1]
    slots = plan[0] * plan[3]
    columns = width // 4

    def tile(size):
        return pl.BlockSpec((size, columns), lambda i: (0, i))

    return pl.pallas_call(
        functools.partial(combine_kernel, plan, len(backs), len(pieces)),
        grid=(width // columns,),
        in_specs=[pl.BlockSpec(meta.shape, lambda i: (0, 0)), ANYWHERE]
        + [tile(piece.shape[0]) for piece in [*backs, *pieces]],
        out_specs=[tile(tokens // outs)] * outs + [TOKEN],
        out_shape=[jax.ShapeDtypeStruct((tokens // outs, width), dtype)] * outs + [TOKEN_SHAPE],
        scratch_shapes=[pltpu.VMEM((slots, tokens), BF16)] * 2,
        compiler_params=PARAMS,
        cost_estimate=cost(f"combine{stage}"),
    )(meta, after, *backs, *pieces)


def finish_kernel(pieces, own_ref, *refs):
    out_ref = refs[-1]
    parts = [jnp.concatenate([refs[i][...] for i in group], axis=0) for group in pieces]
    total = own_ref[...]
    for part in parts:
        total = total + part.astype(F32)
    out_ref[...] = total.astype(BF16)


def finish(own, parts):
    tokens, width = own.shape
    columns = width // 4
    tile = pl.BlockSpec((tokens, columns), lambda i: (0, i))
    flat = [piece for part in parts for piece in part]
    pieces, start = [], 0
    for part in parts:
        pieces.append(range(start, start + len(part)))
        start += len(part)
    return pl.pallas_call(
        functools.partial(finish_kernel, pieces),
        grid=(width // columns,),
        in_specs=[tile]
        + [pl.BlockSpec((piece.shape[0], columns), lambda i: (0, i)) for piece in flat],
        out_specs=tile,
        out_shape=jax.ShapeDtypeStruct(own.shape, BF16),
        compiler_params=PARAMS,
        cost_estimate=cost("finish"),
    )(own, *flat)


def body(queries, keys, values, moe_rows, expert_ids, route_weights, w_gate, w_up, w_down):
    ctx, exp = lax.axis_size("ctx"), lax.axis_size("exp")
    sequence, query_width = queries.shape
    kv_heads = keys.shape[1] // HEAD_WIDTH
    tokens, width = moe_rows.shape
    top = expert_ids.shape[1]
    capacity = max(2, tokens * top * 5 // (4 * ctx * exp))
    rows = -(-capacity // 8) * 8
    plan = (ctx, capacity, top, rows)

    meta = jnp.concatenate([expert_ids.astype(F32).T, route_weights.T], axis=0)
    metas = [meta] + [swap(meta, "exp", s) for s in range(1, exp)]
    state = {"after": sum(metas[1:])[:8]}
    sent, served, partial, arrived = {}, {}, {}, {0: [moe_rows]}

    def mark(value):
        return value.reshape(-1, value.shape[-1])[:8, :128].astype(F32)

    q = queries.reshape(sequence, ctx, query_width // ctx).transpose(1, 0, 2)
    k = keys.reshape(sequence, kv_heads, HEAD_WIDTH).transpose(1, 0, 2)
    v = values.reshape(sequence, kv_heads, HEAD_WIDTH).transpose(1, 0, 2)
    kv = jnp.repeat(jnp.concatenate([k, v], axis=2), ctx // kv_heads, axis=0)
    (heads,) = gate("heads", [jnp.concatenate([q, kv], axis=2)], state["after"])
    heads = exchange(heads)
    local_queries = heads[:, :, : query_width // ctx]
    local_kv = heads[:, :, query_width // ctx :].reshape(ctx * sequence, 2 * HEAD_WIDTH)

    halves = [tokens // 2] * 2
    mine = [moe_rows[: tokens // 2], moe_rows[tokens // 2 :]]
    for s in range(1, min(exp, 3)):
        arrived[s] = [swap(piece, "exp", s) for piece in mine]

    def dispatch(s, after):
        other, cuts = (moe_rows, halves) if s == 1 else (None, [])
        result = pack(s, metas[s], arrived[s], state["after"], after, other, cuts, plan)
        if s == 1:
            for t in range(3, exp):
                arrived[t] = [swap(piece, "exp", t) for piece in result[2:]]
        sent[s] = exchange(result[0].reshape(ctx, rows, width))
        state["after"] = result[1]

    def serve(s):
        x = sent[s].reshape(ctx * rows, width)
        split = ctx if s == 1 else 1
        *outs, state["after"] = ffn(s, x, w_gate, w_up, w_down, state["after"], split)
        served[s] = outs[0]
        if s == 1:
            served[s] = outs

    def pass_on(name, group, after):
        values = [served[1][m] for m in group]
        if after is not None:
            values = gate(name, values, after)
        for m, value in zip(group, values):
            served[1][m] = swap(value, "ctx", m)

    def passed(group):
        state["after"] = state["after"] + sum(mark(served[1][m]) for m in group)

    def give_back(s, before):
        out = served[s] if before is None else gate(f"back{s}", [served[s]], before)[0]
        served[s] = exchange(out.reshape(ctx, rows, width))

    def collect(s):
        backs = served[s] if s == 1 else [served[s].reshape(ctx * rows, width)]
        outs, dtype = (1, F32) if s == 0 else (1, BF16) if s == 1 else (2, BF16)
        pieces = partial[2] if s == 0 else []
        *parts, state["after"] = combine(
            s, metas[s], backs, state["after"], pieces, outs, dtype, plan
        )
        partial[s] = parts if s == 0 else [swap(part, "exp", s) for part in parts]

    third = max(1, ctx // 4)
    groups = [range(1, 1 + third), range(1 + third, 1 + 2 * third), range(1 + 2 * third, ctx)]
    dispatch(0, state["after"])
    dispatch(1, mark(heads))
    serve(0)
    dispatch(2, state["after"])
    serve(1)
    pass_on("pass0", groups[0], None)
    for s in range(3, exp):
        dispatch(s, state["after"])
    (held_kv,) = gate("kv", [local_kv], state["after"])
    line = jnp.concatenate([held_kv] + [swap(held_kv, "exp", s) for s in range(1, exp)], axis=0)
    state["after"] = mark(held_kv)
    serve(2)
    pass_on("pass1", groups[1], state["after"])
    passed(groups[0])
    order = list(range(2, exp)) + [0]
    give_back(2, None)
    attended, state["after"] = attend(local_queries, line, state["after"])
    passed(groups[1])
    pass_on("pass2", groups[2], state["after"])
    for s in range(3, exp):
        serve(s)
    for s in range(3, exp):
        give_back(s, mark(served[s - 1]))
    collect(2)
    give_back(0, mark(served[exp - 1]))
    collect(1)
    for s in range(3, exp):
        collect(s)
    collect(0)
    (attended,) = gate("out", [attended], mark(served[0]))
    output = exchange(attended).transpose(1, 0, 2).reshape(sequence, query_width)
    return (output, finish(partial[0][0], [partial[s] for s in [1, *range(3, exp)]]))


def solution(mesh):
    row = P(("ctx", "exp"), None)
    cube = P(("ctx", "exp"), None, None)
    return jax.shard_map(
        body,
        mesh=mesh,
        in_specs=(row,) * 6 + (cube,) * 3,
        out_specs=(row, row),
        check_vma=False,
    )
```

time: 344 us -> 334 us (0.971); the launches traced: 338 us -> 332 us
  waiting for transfers between devices: 137 us -> 121 us
  other arithmetic: 2.41 us -> 9.38 us
    all_to_all x10 -> x9, waiting for transfers between devices: 106 us -> 77 us  [exchange(): return lax.all_to_all(value, 'ctx', split_axis=0, concat_axis=0, tiled=True)]
    ppermute x17 -> x24, waiting for transfers between devices: 30.9 us -> 44.4 us  [swap(): return lax.ppermute(value, axis, [(i, i ^ offset) for i in range(count)])]
    all_to_all x10 -> x9, starting transfers between devices: 51.2 us -> 46.6 us  [exchange(): return lax.all_to_all(value, 'ctx', split_axis=0, concat_axis=0, tiled=True)]
    convert_element_type x0 -> x5, other arithmetic: none -> 4.5 us  [mark(): return value.reshape(-1, value.shape[-1])[:8, :128].astype(F32)]
    ppermute x17 -> x24, starting transfers between devices: 23.1 us -> 27.4 us  [swap(): return lax.ppermute(value, axis, [(i, i ^ offset) for i in range(count)])]
    unnamed x53 -> x76, local copies, waits for them, and re-layouts: 24 us -> 26.2 us
    pallas_call x17 -> x19, Pallas kernels: 76.8 us -> 78.4 us  [the longest x4 48.4 us: ffn(): pl.pallas_call(functools.partial(ffn_kernel, split > 1), grid=(hidden //...]
  transfers between devices with their start and end apart: 27 -> 33, of which waited for: 11 -> 13; matrix products, arithmetic and copies ran while one was open for 1% -> 4% of each run, Pallas kernels for 28% -> 29%
where the time goes in v3:
time: 334 us; the launch traced here: 332 us
  waiting for transfers between devices  121 us (36%)
  Pallas kernels  95.1 us (28%)
  starting transfers between devices  74 us (22%)
  local copies, waits for them, and re-layouts  31.7 us (9%)
  other arithmetic  9.38 us (3%)
    all_to_all x9, waiting for transfers between devices, exchange(): return lax.all_to_all(value, 'ctx', split_axis=0, concat_axis=0, tiled=True)  77 us
    pallas_call x4, Pallas kernels, ffn(): pl.pallas_call(functools.partial(ffn_kernel, split > 1), grid=(hidden //...  48.4 us
    all_to_all x9, starting transfers between devices, exchange(): return lax.all_to_all(value, 'ctx', split_axis=0, concat_axis=0, tiled=True)  46.6 us
    ppermute x24, waiting for transfers between devices, swap(): return lax.ppermute(value, axis, [(i, i ^ offset) for i in range(count)])  44.4 us
    ppermute x24, starting transfers between devices, swap(): return lax.ppermute(value, axis, [(i, i ^ offset) for i in range(count)])  27.4 us
    unnamed x76, local copies, waits for them, and re-layouts  26.2 us
    pallas_call x4, Pallas kernels, combine(): pl.pallas_call(functools.partial(combine_kernel, plan, len(backs), len(pi...  17.1 us
    pallas_call x1, Pallas kernels, attend(): pl.pallas_call(functools.partial(attention_kernel, width // HEAD_WIDTH, b...  13.2 us
  transfers between devices with their start and end apart: 33, of which 13 were waited for; matrix products, arithmetic and copies ran while one was open for 4% of the time, Pallas kernels for 29%

profile of v3, /device:TPU:12, one launch (start us, length us, event | category | flops | bytes accessed | tf_op | source)
XLA Modules:
  0.0 332.5 jit_solution(4030707119858251624)
XLA Ops:
  2.0 1.6 collective-permute-start.2
  3.6 1.2 collective-permute-start.1
  4.8 1.2 collective-permute-start
  7.9 1.1 copy.28
  9.0 0.9 pad_maximum_fusion.1.refs_0_
  10.5 4.4 %all-to-all-start = ((bf16[8,64,768]{2,1,0:T(8,128)(2,1)}), bf16[8,64,768]{2,1,0:T(8,128)(2,1)S(1)}, u32[]{:S(2)}, u32[]{:S(2)}) async-start(bf16[8,64,768]{2,1,0:T(8,128)(2,1)} %shard_map.104), calls=%async_computation | async-start | bytes 1572864 | tf_op jit(solution)/shard_map/all_to_all | solution.py:36
  14.9 1.0 fusion
  16.7 1.2 collective-permute-start.3
  18.0 1.7 shard_map.105
  19.7 1.4 copy-done.9
  21.2 4.9 %all-to-all-done = bf16[8,64,768]{2,1,0:T(8,128)(2,1)S(1)} async-done(((bf16[8,64,768]{2,1,0:T(8,128)(2,1)}), bf16[8,64,768]{2,1,0:T(8,128)(2,1)S(1)}, u32[]{:S(2)}, u32[]{:S(2)}) %all-to-all-start) | async-done | bytes 786464 | tf_op jit(solution)/shard_map/all_to_all | solution.py:36
  26.9 5.0 %all-to-all-start.2 = ((bf16[8,40,4096]{2,1,0:T(8,128)(2,1)}), bf16[8,40,4096]{2,1,0:T(8,128)(2,1)S(1)}, u32[]{:S(2)}, u32[]{:S(2)}) async-start(bf16[8,40,4096]{2,1,0:T(8,128)(2,1)} %bitcast.41), calls=%async_computation.2 | async-start | bytes 5242880 | tf_op jit(solution)/shard_map/all_to_all | solution.py:36
  31.9 2.9 collective-permute-start.6
  36.4 10.9 %collective-permute-done.3.refs_0_ = bf16[64,4096]{1,0:T(8,128)(2,1)} collective-permute-done((bf16[64,4096]{1,0:T(8,128)(2,1)}, bf16[64,4096]{1,0:T(8,128)(2,1)}, u32[]{:S(2)}, u32[]{:S(2)}) %collective-permute-start.3) | collective-permute-done | bytes 524320 | tf_op jit(solution)/shard_map/ppermute | solution.py:32
  47.3 1.2 copy-done.5
  48.5 1.0 copy-done.29
  49.5 3.3 shard_map.106
  52.8 1.5 copy-done.7
  55.1 7.6 %all-to-all-done.2 = bf16[8,40,4096]{2,1,0:T(8,128)(2,1)S(1)} async-done(((bf16[8,40,4096]{2,1,0:T(8,128)(2,1)}), bf16[8,40,4096]{2,1,0:T(8,128)(2,1)S(1)}, u32[]{:S(2)}, u32[]{:S(2)}) %all-to-all-start.2) | async-done | bytes 2621472 | tf_op jit(solution)/shard_map/all_to_all | solution.py:36
  62.7 1.5 copy-done.2
  64.2 5.0 %all-to-all-start.1 = ((bf16[8,40,4096]{2,1,0:T(8,128)(2,1)}), bf16[8,40,4096]{2,1,0:T(8,128)(2,1)S(1)}, u32[]{:S(2)}, u32[]{:S(2)}) async-start(bf16[8,40,4096]{2,1,0:T(8,128)(2,1)} %bitcast.39), calls=%async_computation.1 | async-start | bytes 5242880 | tf_op jit(solution)/shard_map/all_to_all | solution.py:36
  69.2 1.5 collective-permute-start.7
  71.2 1.7 copy-done.3
  73.0 11.2 %shard_map.107 = (bf16[320,4096]{1,0:T(8,128)(2,1)S(1)}, f32[8,128]{1,0:T(8,128)S(1)}) custom-call(bf16[320,4096]{1,0:T(8,128)(2,1)S(1)} %bitcast.35, bf16[1,4096,768]{2,1,0:T(8,128)(2,1)} %gate_ref.7, bf16[1,4096,768]{2,1,0:T(8,128)(2,1)} %up_ref.7, bf16[1,768,4096]{2,1,0:T(8,128)(2,1)} %down_ref.7, f32[8,128]{1,0:T(8,128)S(1)} %get-tuple-element.46.after_ref), custom_call_target="tpu_custom_call" | custom-call | flops 1024 | bytes 1024 | tf_op jit(solution)/shard_map/pallas_call | solution.py:213
  84.2 1.4 copy-done
  85.6 18.1 %collective-permute-done.5.refs_0_ = bf16[64,4096]{1,0:T(8,128)(2,1)} collective-permute-done((bf16[64,4096]{1,0:T(8,128)(2,1)}, bf16[64,4096]{1,0:T(8,128)(2,1)}, u32[]{:S(2)}, u32[]{:S(2)}) %collective-permute-start.5) | collective-permute-done | bytes 524320 | tf_op jit(solution)/shard_map/ppermute | solution.py:32
  103.7 3.2 shard_map.108
  106.9 1.5 copy-done.8
  108.5 4.4 %all-to-all-start.3 = ((bf16[8,40,4096]{2,1,0:T(8,128)(2,1)}), bf16[8,40,4096]{2,1,0:T(8,128)(2,1)}, u32[]{:S(2)}, u32[]{:S(2)}) async-start(bf16[8,40,4096]{2,1,0:T(8,128)(2,1)} %bitcast.40), calls=%async_computation.3 | async-start | bytes 5242880 | tf_op jit(solution)/shard_map/all_to_all | solution.py:36
  112.9 12.2 %shard_map.109 = (bf16[40,4096]{1,0:T(8,128)(2,1)S(1)}, bf16[40,4096]{1,0:T(8,128)(2,1)}, bf16[40,4096]{1,0:T(8,128)(2,1)S(1)}, bf16[40,4096]{1,0:T(8,128)(2,1)S...) custom-call(bf16[320,4096]{1,0:T(8,128)(2,1)S(1)} %bitcast.34, ...), custom_call_target="tpu_custom_call" | custom-call | flops 1024 | bytes 1024 | tf_op jit(solution)/shard_map/pallas_call | solution.py:213
  130.2 4.6 %shard_map.110 = (bf16[320,4096]{1,0:T(8,128)(2,1)}, f32[8,128]{1,0:T(8,128)S(1)}) custom-call(f32[16,128]{1,0:T(8,128)S(1)} %collective-permute-done.2.meta_ref, f32[8,128]{1,0:T(8,128)S(1)} %get-tuple-element.49.after_ref.arrived_ref, f32[8,128]{1,0:T(8,128)S(1)} %get-tuple-element.49.after_ref.arrived_ref, ...), custom_call_target="tpu_custom_call" | custom-call | flops 20000002048 | bytes 1024 | tf_op jit(solution)/shard_map/pallas_call | solution.py:165
  135.4 8.4 %all-to-all-done.3 = bf16[8,40,4096]{2,1,0:T(8,128)(2,1)} async-done(((bf16[8,40,4096]{2,1,0:T(8,128)(2,1)}), bf16[8,40,4096]{2,1,0:T(8,128)(2,1)}, u32[]{:S(2)}, u32[]{:S(2)}) %all-to-all-start.3) | async-done | bytes 2621472 | tf_op jit(solution)/shard_map/all_to_all | solution.py:36
  143.8 5.9 %all-to-all-start.4 = ((bf16[8,40,4096]{2,1,0:T(8,128)(2,1)}), bf16[8,40,4096]{2,1,0:T(8,128)(2,1)}, u32[]{:S(2)}, u32[]{:S(2)}) async-start(bf16[8,40,4096]{2,1,0:T(8,128)(2,1)} %bitcast.14), calls=%async_computation.4 | async-start | bytes 5242880 | tf_op jit(solution)/shard_map/all_to_all | solution.py:36
  150.6 3.6 %collective-permute-start.10 = (bf16[512,256]{1,0:T(8,128)(2,1)}, bf16[512,256]{1,0:T(8,128)(2,1)S(1)}, u32[]{:S(2)}, u32[]{:S(2)}) collective-permute-start(bf16[512,256]{1,0:T(8,128)(2,1)} %shard_map.111), channel_id=1, source_target_pairs={{0,2},{1,3},{2,0},{3,1},{4,6},{5,7},{6,4},{7,5},{8,10},{9,11},{10,... | collective-permute-start | bytes 786440 | tf_op jit(solution)/shard_map/ppermute | solution.py:32
  154.2 1.3 collective-permute-start.9
  155.4 1.5 collective-permute-start.13
  157.6 12.5 %shard_map.112 = (bf16[320,4096]{1,0:T(8,128)(2,1)S(1)}, f32[8,128]{1,0:T(8,128)S(1)}) custom-call(bf16[320,4096]{1,0:T(8,128)(2,1)} %bitcast.13.x_ref, bf16[1,4096,768]{2,1,0:T(8,128)(2,1)} %gate_ref.7, bf16[1,4096,768]{2,1,0:T(8,128)(2,1)} %up_ref.7, bf16[1,768,4096]{2,1,0:T(8,128)(2,1)} %down_ref.7, f32[8,128]{1,0:T(8,128)S(1)} %slice_convert_fusion.3.after_ref), custom_call_target="tpu_custom_call" | custom-call | flops 15000000512 | bytes 1024 | tf_op jit(solution)/shard_map/pallas_call | solution.py:213
  170.1 1.5 copy-done.6
  175.0 1.3 pad_maximum_fusion.kv_ref
  176.2 4.9 %all-to-all-done.4 = bf16[8,40,4096]{2,1,0:T(8,128)(2,1)} async-done(((bf16[8,40,4096]{2,1,0:T(8,128)(2,1)}), bf16[8,40,4096]{2,1,0:T(8,128)(2,1)}, u32[]{:S(2)}, u32[]{:S(2)}) %all-to-all-start.4) | async-done | bytes 2621472 | tf_op jit(solution)/shard_map/all_to_all | solution.py:36
  181.1 5.9 %all-to-all-start.5 = ((bf16[8,40,4096]{2,1,0:T(8,128)(2,1)}), bf16[8,40,4096]{2,1,0:T(8,128)(2,1)}, u32[]{:S(2)}, u32[]{:S(2)}) async-start(bf16[8,40,4096]{2,1,0:T(8,128)(2,1)} %bitcast.38), calls=%async_computation.5 | async-start | bytes 5242880 | tf_op jit(solution)/shard_map/all_to_all | solution.py:36
  187.1 1.0 collective-permute-done.13.refs_2_
  188.1 13.2 %shard_map.113 = (bf16[8,64,512]{2,1,0:T(8,128)(2,1)S(1)}, f32[8,128]{1,0:T(8,128)S(1)}) custom-call(bf16[8,64,512]{2,1,0:T(8,128)(2,1)S(1)} %slice.59.q_ref, bf16[2048,256]{1,0:T(8,128)(2,1)S(1)} %pad_maximum_fusion.kv_ref, f32[8,128]{1,0:T(8,128)S(1)} %add_add_fusion.1.after_ref), custom_call_target="tpu_custom_call" | custom-call | flops 1024 | bytes 1024 | tf_op jit(solution)/shard_map/pallas_call | solution.py:85
  202.7 1.7 collective-permute-start.17
  204.4 1.2 collective-permute-start.18
  206.3 12.6 %shard_map.115 = (bf16[320,4096]{1,0:T(8,128)(2,1)S(1)}, f32[8,128]{1,0:T(8,128)S(1)}) custom-call(bf16[320,4096]{1,0:T(8,128)(2,1)} %bitcast.15.x_ref, bf16[1,4096,768]{2,1,0:T(8,128)(2,1)} %gate_ref.7, bf16[1,4096,768]{2,1,0:T(8,128)(2,1)} %up_ref.7, bf16[1,768,4096]{2,1,0:T(8,128)(2,1)} %down_ref.7, f32[8,128]{1,0:T(8,128)S(1)} %copy-done.21), custom_call_target="tpu_custom_call" | custom-call | flops 20000002048 | bytes 1024 | tf_op jit(solution)/shard_map/pallas_call | solution.py:213
  218.9 1.5 copy-done.1
  220.4 3.0 all-to-all-done.5
  223.4 1.3 slice_convert_fusion.2.refs_1_
  224.7 5.0 %all-to-all-start.6 = ((bf16[8,40,4096]{2,1,0:T(8,128)(2,1)}), bf16[8,40,4096]{2,1,0:T(8,128)(2,1)S(1)}, u32[]{:S(2)}, u32[]{:S(2)}) async-start(bf16[8,40,4096]{2,1,0:T(8,128)(2,1)} %bitcast.33), calls=%async_computation.6 | async-start | bytes 5242880 | tf_op jit(solution)/shard_map/all_to_all | solution.py:36
  229.7 4.8 %shard_map.119 = (bf16[64,4096]{1,0:T(8,128)(2,1)}, bf16[64,4096]{1,0:T(8,128)(2,1)}, f32[8,128]{1,0:T(8,128)S(1)}) custom-call(f32[16,128]{1,0:T(8,128)S(1)} %collective-permute-done.1.meta_ref, f32[8,128]{1,0:T(8,128)S(1)} %get-tuple-element.67.after_ref, bf16[320,4096]{1,0:T(8,128)(2,1)} %bitcast.17.refs_0_), custom_call_target="tpu_custom_call" | custom-call | flops 40000000000 | bytes 1024 | tf_op jit(solution)/shard_map/pallas_call | solution.py:266
  234.5 3.4 %collective-permute-start.19 = (bf16[64,4096]{1,0:T(8,128)(2,1)}, bf16[64,4096]{1,0:T(8,128)(2,1)}, u32[]{:S(2)}, u32[]{:S(2)}) collective-permute-start(bf16[64,4096]{1,0:T(8,128)(2,1)} %get-tuple-element.78), channel_id=1, source_target_pairs={{0,2},{1,3},{2,0},{3,1},{4,6},{5,7},{6,4},{7,5},{8,10},{9,11},{10,... | collective-permute-start | bytes 1572872 | tf_op jit(solution)/shard_map/ppermute | solution.py:32
  238.0 4.6 %shard_map.121 = (bf16[128,4096]{1,0:T(8,128)(2,1)}, f32[8,128]{1,0:T(8,128)S(1)}) custom-call(f32[16,128]{1,0:T(8,128)S(1)} %collective-permute-done.meta_ref, f32[8,128]{1,0:T(8,128)S(1)} %get-tuple-element.68.after_ref, bf16[40,4096]{1,0:T(8,128)(2,1)S(1)} %copy-done.31, bf16[40,4096]{1,0:T(8,128)(2,1)S(1)} %collective-permute-done.12.refs_1_, ...), custom_call_target="tpu_custom_call" | custom-call | flops 40000000000 | bytes 1024 | tf_op jit(solution)/shard_map/pallas_call | solution.py:266
  243.4 22.4 %all-to-all-done.6 = bf16[8,40,4096]{2,1,0:T(8,128)(2,1)S(1)} async-done(((bf16[8,40,4096]{2,1,0:T(8,128)(2,1)}), bf16[8,40,4096]{2,1,0:T(8,128)(2,1)S(1)}, u32[]{:S(2)}, u32[]{:S(2)}) %all-to-all-start.6) | async-done | bytes 2621472 | tf_op jit(solution)/shard_map/all_to_all | solution.py:36
  266.4 6.0 %all-to-all-start.7 = ((bf16[8,40,4096]{2,1,0:T(8,128)(2,1)}), bf16[8,40,4096]{2,1,0:T(8,128)(2,1)}, u32[]{:S(2)}, u32[]{:S(2)}) async-start(bf16[8,40,4096]{2,1,0:T(8,128)(2,1)} %bitcast.32), calls=%async_computation.7 | async-start | bytes 5242880 | tf_op jit(solution)/shard_map/all_to_all | solution.py:36
  272.4 3.0 shard_map.122
  275.4 2.0 collective-permute-start.23
  277.5 25.8 %all-to-all-done.7 = bf16[8,40,4096]{2,1,0:T(8,128)(2,1)} async-done(((bf16[8,40,4096]{2,1,0:T(8,128)(2,1)}), bf16[8,40,4096]{2,1,0:T(8,128)(2,1)}, u32[]{:S(2)}, u32[]{:S(2)}) %all-to-all-start.7) | async-done | bytes 2621472 | tf_op jit(solution)/shard_map/all_to_all | solution.py:36
  303.3 1.3 slice_convert_fusion.refs_1_
  304.6 4.9 %all-to-all-start.8 = ((bf16[8,64,512]{2,1,0:T(8,128)(2,1)}), bf16[8,64,512]{2,1,0:T(8,128)(2,1)S(1)}, u32[]{:S(2)}, u32[]{:S(2)}) async-start(bf16[8,64,512]{2,1,0:T(8,128)(2,1)} %shard_map.118), calls=%async_computation.8 | async-start | bytes 1048576 | tf_op jit(solution)/shard_map/all_to_all | solution.py:36
  309.5 4.7 %shard_map.123 = (f32[128,4096]{1,0:T(8,128)S(1)}, f32[8,128]{1,0:T(8,128)}) custom-call(f32[16,128]{1,0:T(8,128)S(1)} %copy-done.18, f32[8,128]{1,0:T(8,128)S(1)} %get-tuple-element.77.after_ref, bf16[320,4096]{1,0:T(8,128)(2,1)} %bitcast.21.refs_0_, bf16[64,4096]{1,0:T(8,128)(2,1)} %collective-permute-done.19.refs_1_, ...), custom_call_target="tpu_custom_call" | custom-call | flops 40000000000 | bytes 1024 | tf_op jit(solution)/shard_map/pallas_call | solution.py:266
  314.2 3.4 %collective-permute-done.22.refs_1_ = bf16[64,4096]{1,0:T(8,128)(2,1)S(1)} collective-permute-done((bf16[64,4096]{1,0:T(8,128)(2,1)}, bf16[64,4096]{1,0:T(8,128)(2,1)S(1)}, u32[]{:S(2)}, u32[]{:S(2)}) %collective-permute-start.22) | collective-permute-done | bytes 524320 | tf_op jit(solution)/shard_map/ppermute | solution.py:32
  317.6 10.5 %collective-permute-done.23.refs_2_ = bf16[64,4096]{1,0:T(8,128)(2,1)S(1)} collective-permute-done((bf16[64,4096]{1,0:T(8,128)(2,1)S(1)}, bf16[64,4096]{1,0:T(8,128)(2,1)S(1)}, u32[]{:S(2)}, u32[]{:S(2)}) %collective-permute-start.23) | collective-permute-done | bytes 524320 | tf_op jit(solution)/shard_map/ppermute | solution.py:32
  328.1 3.6 %shard_map.124 = bf16[128,4096]{1,0:T(8,128)(2,1)} custom-call(f32[128,4096]{1,0:T(8,128)S(1)} %get-tuple-element.80.own_ref, bf16[128,4096]{1,0:T(8,128)(2,1)} %collective-permute-done.21.refs_0_, bf16[64,4096]{1,0:T(8,128)(2,1)S(1)} %collective-permute-done.22.refs_1_, bf16[64,4096]{1,0:T(8,128)(2,1)S(1)} %collective-permute-done.23.refs_2_), custom_call_target="tpu_custom_call" | custom-call | flops 1024 | bytes 1024 | tf_op jit(solution)/shard_map/pallas_call | solution.py:297
  (121 shorter events, 23.4 us)
Async XLA Ops:
  2.0 16.0 %copy-start.17 = (f32[16,128]{1,0:T(8,128)}, f32[16,128]{1,0:T(8,128)S(1)}, u32[]{:S(2)}) copy-start(f32[16,128]{1,0:T(8,128)S(1)} %pad_maximum_fusion.3.meta_ref) | copy-start | bytes 24580
  2.0 7.9 %collective-permute-start.2 = (f32[16,128]{1,0:T(8,128)S(1)}, f32[16,128]{1,0:T(8,128)S(1)}, u32[]{:S(2)}, u32[]{:S(2)}) collective-permute-start(f32[16,128]{1,0:T(8,128)S(1)} %pad_maximum_fusion.3.meta_ref), channel_id=1, source_target_pairs={{0,3},{1,2},{2,1},{3,0},{4,7},{5,6},{6,5},{7,4},{8,11},{9,10},{10,... | collective-permute-start | bytes 24584 | tf_op jit(solution)/shard_map/ppermute | solution.py:32
  3.6 6.4 %collective-permute-start.1 = (f32[16,128]{1,0:T(8,128)S(1)}, f32[16,128]{1,0:T(8,128)S(1)}, u32[]{:S(2)}, u32[]{:S(2)}) collective-permute-start(f32[16,128]{1,0:T(8,128)S(1)} %pad_maximum_fusion.3.meta_ref), channel_id=1, source_target_pairs={{0,2},{1,3},{2,0},{3,1},{4,6},{5,7},{6,4},{7,5},{8,10},{9,11},{10,... | collective-permute-start | bytes 24584 | tf_op jit(solution)/shard_map/ppermute | solution.py:32
  4.8 5.1 %collective-permute-start = (f32[16,128]{1,0:T(8,128)S(1)}, f32[16,128]{1,0:T(8,128)S(1)}, u32[]{:S(2)}, u32[]{:S(2)}) collective-permute-start(f32[16,128]{1,0:T(8,128)S(1)} %pad_maximum_fusion.3.meta_ref), channel_id=1, source_target_pairs={{0,1},{1,0},{2,3},{3,2},{4,5},{5,4},{6,7},{7,6},{8,9},{9,8},{10,11... | collective-permute-start | bytes 24584 | tf_op jit(solution)/shard_map/ppermute | solution.py:32
  10.5 4.4 %copy-start.4 = (bf16[128,4096]{1,0:T(8,128)(2,1)S(1)}, bf16[128,4096]{1,0:T(8,128)(2,1)}, u32[]{:S(2)}) copy-start(bf16[128,4096]{1,0:T(8,128)(2,1)} %refs_2_.1) | copy-start | bytes 3145732
  10.5 7.4 %copy-start.16 = (f32[8,128]{1,0:T(8,128)S(1)}, f32[8,128]{1,0:T(8,128)}, u32[]{:S(2)}) copy-start(f32[8,128]{1,0:T(8,128)} %slice_add_fusion.refs_1_.after_ref.arrived_ref) | copy-start | bytes 12292
  10.5 15.5 %all-to-all-start = ((bf16[8,64,768]{2,1,0:T(8,128)(2,1)}), bf16[8,64,768]{2,1,0:T(8,128)(2,1)S(1)}, u32[]{:S(2)}, u32[]{:S(2)}) async-start(bf16[8,64,768]{2,1,0:T(8,128)(2,1)} %shard_map.104), calls=%async_computation | async-start | bytes 1572864 | tf_op jit(solution)/shard_map/all_to_all | solution.py:36
  15.9 19.6 %collective-permute-start.4 = (bf16[64,4096]{1,0:T(8,128)(2,1)}, bf16[64,4096]{1,0:T(8,128)(2,1)S(1)}, u32[]{:S(2)}, u32[]{:S(2)}) collective-permute-start(bf16[64,4096]{1,0:T(8,128)(2,1)} %get-tuple-element.84), channel_id=1, source_target_pairs={{0,1},{1,0},{2,3},{3,2},{4,5},{5,4},{6,7},{7,6},{8,9},{9,8},{10,11... | collective-permute-start | bytes 1572872 | tf_op jit(solution)/shard_map/ppermute | solution.py:32
  16.7 30.5 %collective-permute-start.3 = (bf16[64,4096]{1,0:T(8,128)(2,1)}, bf16[64,4096]{1,0:T(8,128)(2,1)}, u32[]{:S(2)}, u32[]{:S(2)}) collective-permute-start(bf16[64,4096]{1,0:T(8,128)(2,1)} %get-tuple-element.85), channel_id=1, source_target_pairs={{0,1},{1,0},{2,3},{3,2},{4,5},{5,4},{6,7},{7,6},{8,9},{9,8},{10,11... | collective-permute-start | bytes 1572872 | tf_op jit(solution)/shard_map/ppermute | solution.py:32
  19.7 1.5 copy-start.9
  26.0 0.9 copy-start.34
  26.9 35.8 %all-to-all-start.2 = ((bf16[8,40,4096]{2,1,0:T(8,128)(2,1)}), bf16[8,40,4096]{2,1,0:T(8,128)(2,1)S(1)}, u32[]{:S(2)}, u32[]{:S(2)}) async-start(bf16[8,40,4096]{2,1,0:T(8,128)(2,1)} %bitcast.41), calls=%async_computation.2 | async-start | bytes 5242880 | tf_op jit(solution)/shard_map/all_to_all | solution.py:36
  31.9 53.7 %collective-permute-start.6 = (bf16[64,4096]{1,0:T(8,128)(2,1)}, bf16[64,4096]{1,0:T(8,128)(2,1)}, u32[]{:S(2)}, u32[]{:S(2)}) collective-permute-start(bf16[64,4096]{1,0:T(8,128)(2,1)} %get-tuple-element.84), channel_id=1, source_target_pairs={{0,2},{1,3},{2,0},{3,1},{4,6},{5,7},{6,4},{7,5},{8,10},{9,11},{10,... | collective-permute-start | bytes 1572872 | tf_op jit(solution)/shard_map/ppermute | solution.py:32
  34.9 68.8 %collective-permute-start.5 = (bf16[64,4096]{1,0:T(8,128)(2,1)}, bf16[64,4096]{1,0:T(8,128)(2,1)}, u32[]{:S(2)}, u32[]{:S(2)}) collective-permute-start(bf16[64,4096]{1,0:T(8,128)(2,1)} %get-tuple-element.85), channel_id=1, source_target_pairs={{0,2},{1,3},{2,0},{3,1},{4,6},{5,7},{6,4},{7,5},{8,10},{9,11},{10,... | collective-permute-start | bytes 1572872 | tf_op jit(solution)/shard_map/ppermute | solution.py:32
  35.6 0.8 copy-start.28
  47.3 1.2 copy-start.5
  48.5 1.0 copy-start.29
  52.8 1.5 copy-start.7
  54.3 0.8 copy-start.27
  62.7 1.5 copy-start.2
  64.2 44.3 %all-to-all-start.1 = ((bf16[8,40,4096]{2,1,0:T(8,128)(2,1)}), bf16[8,40,4096]{2,1,0:T(8,128)(2,1)S(1)}, u32[]{:S(2)}, u32[]{:S(2)}) async-start(bf16[8,40,4096]{2,1,0:T(8,128)(2,1)} %bitcast.39), calls=%async_computation.1 | async-start | bytes 5242880 | tf_op jit(solution)/shard_map/all_to_all | solution.py:36
  69.2 61.0 %collective-permute-start.7 = (bf16[64,4096]{1,0:T(8,128)(2,1)}, bf16[64,4096]{1,0:T(8,128)(2,1)}, u32[]{:S(2)}, u32[]{:S(2)}) collective-permute-start(bf16[64,4096]{1,0:T(8,128)(2,1)} %copy-done.27), channel_id=1, source_target_pairs={{0,3},{1,2},{2,1},{3,0},{4,7},{5,6},{6,5},{7,4},{8,11},{9,10},{10,... | collective-permute-start | bytes 1572872 | tf_op jit(solution)/shard_map/ppermute | solution.py:32
  70.7 59.6 %collective-permute-start.8 = (bf16[64,4096]{1,0:T(8,128)(2,1)S(1)}, bf16[64,4096]{1,0:T(8,128)(2,1)}, u32[]{:S(2)}, u32[]{:S(2)}) collective-permute-start(bf16[64,4096]{1,0:T(8,128)(2,1)S(1)} %get-tuple-element.51), channel_id=1, source_target_pairs={{0,3},{1,2},{2,1},{3,0},{4,7},{5,6},{6,5},{7,4},{8,11},{9,10},{10,... | collective-permute-start | bytes 1572872 | tf_op jit(solution)/shard_map/ppermute | solution.py:32
  71.2 1.7 copy-start.3
  84.2 1.5 copy-start
  106.9 1.5 copy-start.8
  108.5 35.3 %all-to-all-start.3 = ((bf16[8,40,4096]{2,1,0:T(8,128)(2,1)}), bf16[8,40,4096]{2,1,0:T(8,128)(2,1)}, u32[]{:S(2)}, u32[]{:S(2)}) async-start(bf16[8,40,4096]{2,1,0:T(8,128)(2,1)} %bitcast.40), calls=%async_computation.3 | async-start | bytes 5242880 | tf_op jit(solution)/shard_map/all_to_all | solution.py:36
  125.8 0.8 copy-start.12
  126.6 0.8 copy-start.13
  128.0 0.7 copy-start.15
  128.8 0.8 copy-start.30
  129.5 0.7 copy-start.32
  143.8 5.9 %copy-start.35 = (bf16[8,64,768]{2,1,0:T(8,128)(2,1)S(1)}, bf16[8,64,768]{2,1,0:T(8,128)(2,1)}, u32[]{:S(2)}) copy-start(bf16[8,64,768]{2,1,0:T(8,128)(2,1)} %copy-done.34) | copy-start | bytes 2359300
  143.8 11.6 %copy-start.33 = (bf16[40,4096]{1,0:T(8,128)(2,1)S(1)}, bf16[40,4096]{1,0:T(8,128)(2,1)}, u32[]{:S(2)}) copy-start(bf16[40,4096]{1,0:T(8,128)(2,1)} %copy-done.32) | copy-start | bytes 983044
  143.8 37.3 %all-to-all-start.4 = ((bf16[8,40,4096]{2,1,0:T(8,128)(2,1)}), bf16[8,40,4096]{2,1,0:T(8,128)(2,1)}, u32[]{:S(2)}, u32[]{:S(2)}) async-start(bf16[8,40,4096]{2,1,0:T(8,128)(2,1)} %bitcast.14), calls=%async_computation.4 | async-start | bytes 5242880 | tf_op jit(solution)/shard_map/all_to_all | solution.py:36
  150.5 21.8 %collective-permute-start.11 = (bf16[512,256]{1,0:T(8,128)(2,1)}, bf16[512,256]{1,0:T(8,128)(2,1)S(1)}, u32[]{:S(2)}, u32[]{:S(2)}) collective-permute-start(bf16[512,256]{1,0:T(8,128)(2,1)} %shard_map.111), channel_id=1, source_target_pairs={{0,3},{1,2},{2,1},{3,0},{4,7},{5,6},{6,5},{7,4},{8,11},{9,10},{10,... | collective-permute-start | bytes 786440 | tf_op jit(solution)/shard_map/ppermute | solution.py:32
  150.6 23.3 %collective-permute-start.10 = (bf16[512,256]{1,0:T(8,128)(2,1)}, bf16[512,256]{1,0:T(8,128)(2,1)S(1)}, u32[]{:S(2)}, u32[]{:S(2)}) collective-permute-start(bf16[512,256]{1,0:T(8,128)(2,1)} %shard_map.111), channel_id=1, source_target_pairs={{0,2},{1,3},{2,0},{3,1},{4,6},{5,7},{6,4},{7,5},{8,10},{9,11},{10,... | collective-permute-start | bytes 786440 | tf_op jit(solution)/shard_map/ppermute | solution.py:32
  154.2 20.8 %collective-permute-start.9 = (bf16[512,256]{1,0:T(8,128)(2,1)}, bf16[512,256]{1,0:T(8,128)(2,1)}, u32[]{:S(2)}, u32[]{:S(2)}) collective-permute-start(bf16[512,256]{1,0:T(8,128)(2,1)} %shard_map.111), channel_id=1, source_target_pairs={{0,1},{1,0},{2,3},{3,2},{4,5},{5,4},{6,7},{7,6},{8,9},{9,8},{10,11... | collective-permute-start | bytes 786440 | tf_op jit(solution)/shard_map/ppermute | solution.py:32
  155.4 31.6 %collective-permute-start.12 = (bf16[40,4096]{1,0:T(8,128)(2,1)}, bf16[40,4096]{1,0:T(8,128)(2,1)S(1)}, u32[]{:S(2)}, u32[]{:S(2)}) collective-permute-start(bf16[40,4096]{1,0:T(8,128)(2,1)} %get-tuple-element.55), channel_id=1, source_target_pairs={{0,4},{4,0},{8,12},{12,8},{16,20},{20,16},{24,28},{28,24},{1,5},{5... | collective-permute-start | bytes 983048 | tf_op jit(solution)/shard_map/ppermute | solution.py:32
  155.4 32.7 %collective-permute-start.13 = (bf16[40,4096]{1,0:T(8,128)(2,1)S(1)}, bf16[40,4096]{1,0:T(8,128)(2,1)S(1)}, u32[]{:S(2)}, u32[]{:S(2)}) collective-permute-start(bf16[40,4096]{1,0:T(8,128)(2,1)S(1)} %copy-done.33), channel_id=1, source_target_pairs={{0,8},{4,12},{8,0},{12,4},{16,24},{20,28},{24,16},{28,20},{1,9},{5... | collective-permute-start | bytes 983048 | tf_op jit(solution)/shard_map/ppermute | solution.py:32
  170.1 1.5 copy-start.6
  173.0 29.1 %collective-permute-start.14 = (bf16[40,4096]{1,0:T(8,128)(2,1)}, bf16[40,4096]{1,0:T(8,128)(2,1)S(1)}, u32[]{:S(2)}, u32[]{:S(2)}) collective-permute-start(bf16[40,4096]{1,0:T(8,128)(2,1)} %get-tuple-element.63), channel_id=1, source_target_pairs={{0,12},{4,8},{8,4},{12,0},{16,28},{20,24},{24,20},{28,16},{1,13},{... | collective-permute-start | bytes 983048 | tf_op jit(solution)/shard_map/ppermute | solution.py:32
  174.6 27.4 %collective-permute-start.15 = (bf16[40,4096]{1,0:T(8,128)(2,1)}, bf16[40,4096]{1,0:T(8,128)(2,1)S(1)}, u32[]{:S(2)}, u32[]{:S(2)}) collective-permute-start(bf16[40,4096]{1,0:T(8,128)(2,1)} %get-tuple-element.64), channel_id=1, source_target_pairs={{0,16},{4,20},{8,24},{12,28},{16,0},{20,4},{24,8},{28,12},{1,17},{... | collective-permute-start | bytes 983048 | tf_op jit(solution)/shard_map/ppermute | solution.py:32
  181.1 6.9 %copy-start.20 = (f32[8,128]{1,0:T(8,128)S(1)}, f32[8,128]{1,0:T(8,128)}, u32[]{:S(2)}) copy-start(f32[8,128]{1,0:T(8,128)} %copy-done.19) | copy-start | bytes 12292
  181.1 42.3 %all-to-all-start.5 = ((bf16[8,40,4096]{2,1,0:T(8,128)(2,1)}), bf16[8,40,4096]{2,1,0:T(8,128)(2,1)}, u32[]{:S(2)}, u32[]{:S(2)}) async-start(bf16[8,40,4096]{2,1,0:T(8,128)(2,1)} %bitcast.38), calls=%async_computation.5 | async-start | bytes 5242880 | tf_op jit(solution)/shard_map/all_to_all | solution.py:36
  201.3 0.8 copy-start.10
  202.1 16.8 %copy-start.23 = (bf16[40,4096]{1,0:T(8,128)(2,1)}, bf16[40,4096]{1,0:T(8,128)(2,1)S(1)}, u32[]{:S(2)}) copy-start(bf16[40,4096]{1,0:T(8,128)(2,1)S(1)} %collective-permute-done.14.refs_3_) | copy-start | bytes 983044
  202.1 16.8 %copy-start.25 = (bf16[40,4096]{1,0:T(8,128)(2,1)}, bf16[40,4096]{1,0:T(8,128)(2,1)S(1)}, u32[]{:S(2)}) copy-start(bf16[40,4096]{1,0:T(8,128)(2,1)S(1)} %collective-permute-done.15.refs_4_) | copy-start | bytes 983044
  202.7 35.2 %collective-permute-start.16 = (bf16[40,4096]{1,0:T(8,128)(2,1)}, bf16[40,4096]{1,0:T(8,128)(2,1)}, u32[]{:S(2)}, u32[]{:S(2)}) collective-permute-start(bf16[40,4096]{1,0:T(8,128)(2,1)} %get-tuple-element.73), channel_id=1, source_target_pairs={{0,20},{4,16},{8,28},{12,24},{16,4},{20,0},{24,12},{28,8},{1,21},{... | collective-permute-start | bytes 983048 | tf_op jit(solution)/shard_map/ppermute | solution.py:32
  202.7 35.2 %collective-permute-start.17 = (bf16[40,4096]{1,0:T(8,128)(2,1)}, bf16[40,4096]{1,0:T(8,128)(2,1)}, u32[]{:S(2)}, u32[]{:S(2)}) collective-permute-start(bf16[40,4096]{1,0:T(8,128)(2,1)} %get-tuple-element.74), channel_id=1, source_target_pairs={{0,24},{4,28},{8,16},{12,20},{16,8},{20,12},{24,0},{28,4},{1,25},{... | collective-permute-start | bytes 983048 | tf_op jit(solution)/shard_map/ppermute | solution.py:32
  204.4 33.5 %collective-permute-start.18 = (bf16[40,4096]{1,0:T(8,128)(2,1)}, bf16[40,4096]{1,0:T(8,128)(2,1)}, u32[]{:S(2)}, u32[]{:S(2)}) collective-permute-start(bf16[40,4096]{1,0:T(8,128)(2,1)} %get-tuple-element.75), channel_id=1, source_target_pairs={{0,28},{4,24},{8,20},{12,16},{16,12},{20,8},{24,4},{28,0},{1,29},{... | collective-permute-start | bytes 983048 | tf_op jit(solution)/shard_map/ppermute | solution.py:32
  218.9 1.5 copy-start.1
  224.7 41.1 %all-to-all-start.6 = ((bf16[8,40,4096]{2,1,0:T(8,128)(2,1)}), bf16[8,40,4096]{2,1,0:T(8,128)(2,1)S(1)}, u32[]{:S(2)}, u32[]{:S(2)}) async-start(bf16[8,40,4096]{2,1,0:T(8,128)(2,1)} %bitcast.33), calls=%async_computation.6 | async-start | bytes 5242880 | tf_op jit(solution)/shard_map/all_to_all | solution.py:36
  229.7 8.2 %copy-start.24 = (bf16[40,4096]{1,0:T(8,128)(2,1)S(1)}, bf16[40,4096]{1,0:T(8,128)(2,1)}, u32[]{:S(2)}) copy-start(bf16[40,4096]{1,0:T(8,128)(2,1)} %copy-done.23) | copy-start | bytes 983044
  229.7 8.2 %copy-start.26 = (bf16[40,4096]{1,0:T(8,128)(2,1)S(1)}, bf16[40,4096]{1,0:T(8,128)(2,1)}, u32[]{:S(2)}) copy-start(bf16[40,4096]{1,0:T(8,128)(2,1)} %copy-done.25) | copy-start | bytes 983044
  229.7 8.2 %copy-start.31 = (bf16[40,4096]{1,0:T(8,128)(2,1)S(1)}, bf16[40,4096]{1,0:T(8,128)(2,1)}, u32[]{:S(2)}) copy-start(bf16[40,4096]{1,0:T(8,128)(2,1)} %copy-done.30) | copy-start | bytes 983044
  234.5 75.0 %collective-permute-start.19 = (bf16[64,4096]{1,0:T(8,128)(2,1)}, bf16[64,4096]{1,0:T(8,128)(2,1)}, u32[]{:S(2)}, u32[]{:S(2)}) collective-permute-start(bf16[64,4096]{1,0:T(8,128)(2,1)} %get-tuple-element.78), channel_id=1, source_target_pairs={{0,2},{1,3},{2,0},{3,1},{4,6},{5,7},{6,4},{7,5},{8,10},{9,11},{10,... | collective-permute-start | bytes 1572872 | tf_op jit(solution)/shard_map/ppermute | solution.py:32
  237.9 71.6 %collective-permute-start.20 = (bf16[64,4096]{1,0:T(8,128)(2,1)}, bf16[64,4096]{1,0:T(8,128)(2,1)}, u32[]{:S(2)}, u32[]{:S(2)}) collective-permute-start(bf16[64,4096]{1,0:T(8,128)(2,1)} %get-tuple-element.79), channel_id=1, source_target_pairs={{0,2},{1,3},{2,0},{3,1},{4,6},{5,7},{6,4},{7,5},{8,10},{9,11},{10,... | collective-permute-start | bytes 1572872 | tf_op jit(solution)/shard_map/ppermute | solution.py:32
  242.6 71.6 %collective-permute-start.21 = (bf16[128,4096]{1,0:T(8,128)(2,1)}, bf16[128,4096]{1,0:T(8,128)(2,1)}, u32[]{:S(2)}, u32[]{:S(2)}) collective-permute-start(bf16[128,4096]{1,0:T(8,128)(2,1)} %get-tuple-element.81), channel_id=1, source_target_pairs={{0,1},{1,0},{2,3},{3,2},{4,5},{5,4},{6,7},{7,6},{8,9},{9,8},{10,11... | collective-permute-start | bytes 3145736 | tf_op jit(solution)/shard_map/ppermute | solution.py:32
  266.4 36.9 %all-to-all-start.7 = ((bf16[8,40,4096]{2,1,0:T(8,128)(2,1)}), bf16[8,40,4096]{2,1,0:T(8,128)(2,1)}, u32[]{:S(2)}, u32[]{:S(2)}) async-start(bf16[8,40,4096]{2,1,0:T(8,128)(2,1)} %bitcast.32), calls=%async_computation.7 | async-start | bytes 5242880 | tf_op jit(solution)/shard_map/all_to_all | solution.py:36
  272.4 37.1 %copy-start.18 = (f32[16,128]{1,0:T(8,128)S(1)}, f32[16,128]{1,0:T(8,128)}, u32[]{:S(2)}) copy-start(f32[16,128]{1,0:T(8,128)} %copy-done.17) | copy-start | bytes 24580
  275.4 42.2 %collective-permute-start.22 = (bf16[64,4096]{1,0:T(8,128)(2,1)}, bf16[64,4096]{1,0:T(8,128)(2,1)S(1)}, u32[]{:S(2)}, u32[]{:S(2)}) collective-permute-start(bf16[64,4096]{1,0:T(8,128)(2,1)} %get-tuple-element.82), channel_id=1, source_target_pairs={{0,3},{1,2},{2,1},{3,0},{4,7},{5,6},{6,5},{7,4},{8,11},{9,10},{10,... | collective-permute-start | bytes 1572872 | tf_op jit(solution)/shard_map/ppermute | solution.py:32
  275.4 52.6 %collective-permute-start.23 = (bf16[64,4096]{1,0:T(8,128)(2,1)S(1)}, bf16[64,4096]{1,0:T(8,128)(2,1)S(1)}, u32[]{:S(2)}, u32[]{:S(2)}) collective-permute-start(bf16[64,4096]{1,0:T(8,128)(2,1)S(1)} %get-tuple-element.83), channel_id=1, source_target_pairs={{0,3},{1,2},{2,1},{3,0},{4,7},{5,6},{6,5},{7,4},{8,11},{9,10},{10,... | collective-permute-start | bytes 1572872 | tf_op jit(solution)/shard_map/ppermute | solution.py:32
  304.6 27.1 %all-to-all-start.8 = ((bf16[8,64,512]{2,1,0:T(8,128)(2,1)}), bf16[8,64,512]{2,1,0:T(8,128)(2,1)S(1)}, u32[]{:S(2)}, u32[]{:S(2)}) async-start(bf16[8,64,512]{2,1,0:T(8,128)(2,1)} %shard_map.118), calls=%async_computation.8 | async-start | bytes 1048576 | tf_op jit(solution)/shard_map/all_to_all | solution.py:36
  (7 other events, 4.7 us)

commit v4 on v3

--- a/solution.py
+++ b/solution.py
@@ -12,7 +12,7 @@
 F32 = jnp.float32
 BF16 = jnp.bfloat16
 VMEM = 48 * 1024 * 1024
-COSTS = {"pack1": 20, "pack2": 20, "pack3": 20, "ffn2": 15, "ffn3": 20, "heads": 20}
+COSTS = {"pack1": 20, "pack2": 40, "pack3": 20, "ffn2": 15, "ffn3": 20}
 COSTS.update({f"combine{s}": 40 for s in range(4)})
 
 
@@ -125,12 +125,14 @@
     )
 
 
-def pack_kernel(plan, count, other, meta_ref, after_ref, arrived_ref, *refs):
+def pack_kernel(plan, count, other, rides, meta_ref, after_ref, arrived_ref, *refs):
     pieces, refs = refs[:count], refs[count:]
     block = jnp.concatenate([ref[...] for ref in pieces], axis=0)
     held = block
     if other:
         held, refs = refs[0][...], refs[1:]
+    if rides:
+        rider, refs = refs[0][...].astype(F32), refs[1:]
     out_ref, token_ref, *copies, pick_ref = refs
     token_ref[...] = jnp.zeros(token_ref.shape, F32)
 
@@ -138,14 +140,22 @@
     def _():
         pick_ref[...] = slot_matrix(meta_ref, plan, False).astype(BF16)
 
-    out_ref[...] = jnp.dot(pick_ref[...], block, preferred_element_type=F32).astype(BF16)
+    packed = jnp.dot(pick_ref[...], block, preferred_element_type=F32)
+    if rides:
+        places, rows = plan[0], plan[3]
+        extra = rider.shape[0] // places
+        parts = []
+        for m in range(places):
+            parts += [packed[m * rows : (m + 1) * rows], rider[m * extra : (m + 1) * extra]]
+        packed = jnp.concatenate(parts, axis=0)
+    out_ref[...] = packed.astype(BF16)
     start = 0
     for ref in copies:
         ref[...] = held[start % held.shape[0] :][: ref.shape[0]]
         start += ref.shape[0]
 
 
-def pack(stage, meta, pieces, after, arrived, other, cuts, plan):
+def pack(stage, meta, pieces, after, arrived, other, cuts, rider, plan):
     places, capacity, top, rows = plan
     tokens, width = meta.shape[1], pieces[0].shape[1]
     columns = width // 4
@@ -159,11 +169,18 @@
     if other is not None:
         operands.append(other)
         in_specs.append(tile(tokens))
-    out_specs = [tile(places * rows), TOKEN] + [tile(size) for size in cuts]
-    out_shape = [jax.ShapeDtypeStruct((places * rows, width), BF16), TOKEN_SHAPE]
+    slots = places * rows
+    if rider is not None:
+        operands.append(rider)
+        in_specs.append(tile(rider.shape[0]))
+        slots += rider.shape[0]
+    out_specs = [tile(slots), TOKEN] + [tile(size) for size in cuts]
+    out_shape = [jax.ShapeDtypeStruct((slots, width), BF16), TOKEN_SHAPE]
     out_shape += [jax.ShapeDtypeStruct((size, width), BF16) for size in cuts]
     return pl.pallas_call(
-        functools.partial(pack_kernel, plan, len(pieces), other is not None),
+        functools.partial(
+            pack_kernel, plan, len(pieces), other is not None, rider is not None
+        ),
         grid=(width // columns,),
         in_specs=in_specs,
         out_specs=out_specs,
@@ -199,17 +216,18 @@
         else:
             total_ref[...] += term
             rows = outs[0].shape[0]
+            stride = total_ref.shape[0] // len(outs)
             for m, out_ref in enumerate(outs):
-                start = pl.multiple_of((lax.axis_index("ctx") ^ m) * rows, 8)
+                start = pl.multiple_of((lax.axis_index("ctx") ^ m) * stride, 8)
                 out_ref[...] = total_ref[pl.ds(start, rows)].astype(BF16)
 
 
-def ffn(stage, x, w_gate, w_up, w_down, after, split):
+def ffn(stage, x, w_gate, w_up, w_down, after, split, kept):
     rows, width = x.shape
     hidden = w_gate.shape[2]
     block = 256
     whole = pl.BlockSpec((rows, width), lambda i: (0, 0))
-    part = pl.BlockSpec((rows // split, width), lambda i: (0, 0))
+    part = pl.BlockSpec((kept, width), lambda i: (0, 0))
     return pl.pallas_call(
         functools.partial(ffn_kernel, split > 1),
         grid=(hidden // block,),
@@ -221,7 +239,7 @@
             ANYWHERE,
         ],
         out_specs=[part] * split + [TOKEN],
-        out_shape=[jax.ShapeDtypeStruct((rows // split, width), BF16)] * split + [TOKEN_SHAPE],
+        out_shape=[jax.ShapeDtypeStruct((kept, width), BF16)] * split + [TOKEN_SHAPE],
         scratch_shapes=[pltpu.VMEM((rows, width), F32)],
         compiler_params=PARAMS,
         cost_estimate=cost(f"ffn{stage}"),
@@ -328,10 +346,11 @@
     k = keys.reshape(sequence, kv_heads, HEAD_WIDTH).transpose(1, 0, 2)
     v = values.reshape(sequence, kv_heads, HEAD_WIDTH).transpose(1, 0, 2)
     kv = jnp.repeat(jnp.concatenate([k, v], axis=2), ctx // kv_heads, axis=0)
-    (heads,) = gate("heads", [jnp.concatenate([q, kv], axis=2)], state["after"])
-    heads = exchange(heads)
-    local_queries = heads[:, :, : query_width // ctx]
-    local_kv = heads[:, :, query_width // ctx :].reshape(ctx * sequence, 2 * HEAD_WIDTH)
+    rider = jnp.concatenate([q, kv], axis=2)
+    flat = rider.size // (ctx * width)
+    extra = -(-flat // 16) * 16
+    rider = jnp.pad(rider.reshape(ctx, flat, width), ((0, 0), (0, extra - flat), (0, 0)))
+    rider = rider.reshape(ctx * extra, width)
 
     halves = [tokens // 2] * 2
     mine = [moe_rows[: tokens // 2], moe_rows[tokens // 2 :]]
@@ -340,17 +359,19 @@
 
     def dispatch(s, after):
         other, cuts = (moe_rows, halves) if s == 1 else (None, [])
-        result = pack(s, metas[s], arrived[s], state["after"], after, other, cuts, plan)
+        result = pack(
+            s, metas[s], arrived[s], state["after"], after, other, cuts, rider if s == 1 else None, plan
+        )
         if s == 1:
             for t in range(3, exp):
                 arrived[t] = [swap(piece, "exp", t) for piece in result[2:]]
-        sent[s] = exchange(result[0].reshape(ctx, rows, width))
+        sent[s] = exchange(result[0].reshape(ctx, -1, width))
         state["after"] = result[1]
 
     def serve(s):
-        x = sent[s].reshape(ctx * rows, width)
-        split = ctx if s == 1 else 1
-        *outs, state["after"] = ffn(s, x, w_gate, w_up, w_down, state["after"], split)
+        x = sent[s].reshape(-1, width)
+        split, kept = (ctx, rows) if s == 1 else (1, ctx * rows)
+        *outs, state["after"] = ffn(s, x, w_gate, w_up, w_down, state["after"], split, kept)
         served[s] = outs[0]
         if s == 1:
             served[s] = outs
@@ -381,7 +402,10 @@
     third = max(1, ctx // 4)
     groups = [range(1, 1 + third), range(1 + third, 1 + 2 * third), range(1 + 2 * third, ctx)]
     dispatch(0, state["after"])
-    dispatch(1, mark(heads))
+    dispatch(1, state["after"])
+    heads = sent[1][:, rows : rows + flat].reshape(ctx, sequence, -1)
+    local_queries = heads[:, :, : query_width // ctx]
+    local_kv = heads[:, :, query_width // ctx :].reshape(ctx * sequence, 2 * HEAD_WIDTH)
     serve(0)
     dispatch(2, state["after"])
     serve(1)

time: 334 us -> 328 us (0.982)
  waiting for transfers between devices: 121 us -> 108 us
  Pallas kernels: 95.1 us -> 99.4 us
    all_to_all x9 -> x8, waiting for transfers between devices: 77 us -> 56.3 us  [exchange(): return lax.all_to_all(value, 'ctx', split_axis=0, concat_axis=0, tiled=True)]
    unnamed x76 -> x62, local copies, waits for them, and re-layouts: 26.2 us -> 17.2 us
    ppermute x24, waiting for transfers between devices: 44.4 us -> 52 us  [swap(): return lax.ppermute(value, axis, [(i, i ^ offset) for i in range(count)])]
    reshape x0 -> x2, local copies, waits for them, and re-layouts: none -> 5.55 us  [the longest x1 2.8 us: body(): heads = sent[1][:, rows:rows + flat].reshape(ctx, sequence, -1)]
    ppermute x24, starting transfers between devices: 27.4 us -> 32.4 us  [swap(): return lax.ppermute(value, axis, [(i, i ^ offset) for i in range(count)])]
    all_to_all x9 -> x8, starting transfers between devices: 46.6 us -> 42.3 us  [exchange(): return lax.all_to_all(value, 'ctx', split_axis=0, concat_axis=0, tiled=True)]
  transfers between devices with their start and end apart: 33 -> 32, of which waited for: 13 -> 13; matrix products, arithmetic and copies ran while one was open for 4% -> 7% of each run, Pallas kernels for 29% -> 31%
where the time goes in v4:
time: 328 us; the launch traced here: 326 us
  waiting for transfers between devices  108 us (33%)
  Pallas kernels  99.4 us (30%)
  starting transfers between devices  74.7 us (23%)
  local copies, waits for them, and re-layouts  33.4 us (10%)
  other arithmetic  8.81 us (3%)
    all_to_all x8, waiting for transfers between devices, exchange(): return lax.all_to_all(value, 'ctx', split_axis=0, concat_axis=0, tiled=True)  56.3 us
    ppermute x24, waiting for transfers between devices, swap(): return lax.ppermute(value, axis, [(i, i ^ offset) for i in range(count)])  52 us
    pallas_call x4, Pallas kernels, ffn(): pl.pallas_call(functools.partial(ffn_kernel, split > 1), grid=(hidden //...  50.9 us
    all_to_all x8, starting transfers between devices, exchange(): return lax.all_to_all(value, 'ctx', split_axis=0, concat_axis=0, tiled=True)  42.3 us
    ppermute x24, starting transfers between devices, swap(): return lax.ppermute(value, axis, [(i, i ^ offset) for i in range(count)])  32.4 us
    pallas_call x4, Pallas kernels, combine(): pl.pallas_call(functools.partial(combine_kernel, plan, len(backs), len(pi...  17.2 us
    unnamed x62, local copies, waits for them, and re-layouts  17.2 us
    pallas_call x4, Pallas kernels, pack(): pl.pallas_call(functools.partial(pack_kernel, plan, len(pieces), other is...  14.5 us
  transfers between devices with their start and end apart: 32, of which 13 were waited for; matrix products, arithmetic and copies ran while one was open for 7% of the time, Pallas kernels for 31%

profile of v4, /device:TPU:12, one launch (start us, length us, event | category | flops | bytes accessed | tf_op | source)
XLA Modules:
  0.0 325.6 jit_solution(17007424402768580518)
XLA Ops:
  2.1 1.6 collective-permute-start.2
  3.7 1.2 collective-permute-start.1
  4.9 1.2 collective-permute-start
  6.2 2.3 fusion
  9.2 1.2 collective-permute-start.3
  10.5 1.7 shard_map.104
  12.3 1.5 copy-done.5
  13.7 4.4 %all-to-all-start.1 = ((bf16[8,40,4096]{2,1,0:T(8,128)(2,1)}), bf16[8,40,4096]{2,1,0:T(8,128)(2,1)S(1)}, u32[]{:S(2)}, u32[]{:S(2)}) async-start(bf16[8,40,4096]{2,1,0:T(8,128)(2,1)} %bitcast.39), calls=%async_computation.1 | async-start | bytes 5242880 | tf_op jit(solution)/shard_map/all_to_all | solution.py:36
  18.1 2.9 collective-permute-start.6
  21.2 1.1 copy.27
  22.3 0.9 pad_maximum_fusion.1
  23.3 2.7 reshape.80
  26.0 1.3 pad.4
  27.4 6.4 %collective-permute-done.4.refs_1_ = bf16[64,4096]{1,0:T(8,128)(2,1)} collective-permute-done((bf16[64,4096]{1,0:T(8,128)(2,1)}, bf16[64,4096]{1,0:T(8,128)(2,1)}, u32[]{:S(2)}, u32[]{:S(2)}) %collective-permute-start.4) | collective-permute-done | bytes 524320 | tf_op jit(solution)/shard_map/ppermute | solution.py:32
  33.7 10.1 %collective-permute-done.3.refs_0_ = bf16[64,4096]{1,0:T(8,128)(2,1)} collective-permute-done((bf16[64,4096]{1,0:T(8,128)(2,1)}, bf16[64,4096]{1,0:T(8,128)(2,1)}, u32[]{:S(2)}, u32[]{:S(2)}) %collective-permute-start.3) | collective-permute-done | bytes 524320 | tf_op jit(solution)/shard_map/ppermute | solution.py:32
  43.8 1.2 copy-done.3
  45.1 5.0 %shard_map.105 = (bf16[448,4096]{1,0:T(8,128)(2,1)}, f32[8,128]{1,0:T(8,128)S(1)}, bf16[64,4096]{1,0:T(8,128)(2,1)}, bf16[64,4096]{1,0:T(8,128)(2,1)}) custom-call(f32[16,128]{1,0:T(8,128)S(1)} %collective-permute-done.meta_ref, f32[8,128]{1,0:T(8,128)S(1)} %get-tuple-element.43.after_ref.arrived_ref, f32[8,128]{1,0:T(8,128)S(1)} %get-tuple-element.43.after_ref.arrived_ref, ...), custom_call_target="tpu_custom_call" | custom-call | flops 20000002048 | bytes 1024 | tf_op jit(solution)/shard_map/pallas_call | solution.py:180
  50.6 1.5 collective-permute-start.8
  52.1 5.1 %all-to-all-start = ((bf16[8,56,4096]{2,1,0:T(8,128)(2,1)}), bf16[8,56,4096]{2,1,0:T(8,128)(2,1)}, u32[]{:S(2)}, u32[]{:S(2)}) async-start(bf16[8,56,4096]{2,1,0:T(8,128)(2,1)} %bitcast.42), calls=%async_computation | async-start | bytes 7340032 | tf_op jit(solution)/shard_map/all_to_all | solution.py:36
  57.2 11.2 %shard_map.106 = (bf16[320,4096]{1,0:T(8,128)(2,1)S(1)}, f32[8,128]{1,0:T(8,128)S(1)}) custom-call(bf16[320,4096]{1,0:T(8,128)(2,1)S(1)} %bitcast.34, bf16[1,4096,768]{2,1,0:T(8,128)(2,1)} %gate_ref.7, bf16[1,4096,768]{2,1,0:T(8,128)(2,1)} %up_ref.7, bf16[1,768,4096]{2,1,0:T(8,128)(2,1)} %down_ref.7, f32[8,128]{1,0:T(8,128)S(1)} %get-tuple-element.46.after_ref), custom_call_target="tpu_custom_call" | custom-call | flops 1024 | bytes 1024 | tf_op jit(solution)/shard_map/pallas_call | solution.py:231
  68.4 1.6 copy-done
  69.9 8.7 %collective-permute-done.6.refs_1_ = bf16[64,4096]{1,0:T(8,128)(2,1)} collective-permute-done((bf16[64,4096]{1,0:T(8,128)(2,1)}, bf16[64,4096]{1,0:T(8,128)(2,1)}, u32[]{:S(2)}, u32[]{:S(2)}) %collective-permute-start.6) | collective-permute-done | bytes 524320 | tf_op jit(solution)/shard_map/ppermute | solution.py:32
  78.6 11.2 %collective-permute-done.5.refs_0_ = bf16[64,4096]{1,0:T(8,128)(2,1)} collective-permute-done((bf16[64,4096]{1,0:T(8,128)(2,1)}, bf16[64,4096]{1,0:T(8,128)(2,1)}, u32[]{:S(2)}, u32[]{:S(2)}) %collective-permute-start.5) | collective-permute-done | bytes 524320 | tf_op jit(solution)/shard_map/ppermute | solution.py:32
  89.8 3.2 shard_map.107
  93.1 1.5 copy-done.6
  94.5 4.7 %all-to-all-done = bf16[8,56,4096]{2,1,0:T(8,128)(2,1)} async-done(((bf16[8,56,4096]{2,1,0:T(8,128)(2,1)}), bf16[8,56,4096]{2,1,0:T(8,128)(2,1)}, u32[]{:S(2)}, u32[]{:S(2)}) %all-to-all-start) | async-done | bytes 3670048 | tf_op jit(solution)/shard_map/all_to_all | solution.py:36
  99.3 5.0 %all-to-all-start.2 = ((bf16[8,40,4096]{2,1,0:T(8,128)(2,1)}), bf16[8,40,4096]{2,1,0:T(8,128)(2,1)S(1)}, u32[]{:S(2)}, u32[]{:S(2)}) async-start(bf16[8,40,4096]{2,1,0:T(8,128)(2,1)} %bitcast.40), calls=%async_computation.2 | async-start | bytes 5242880 | tf_op jit(solution)/shard_map/all_to_all | solution.py:36
  104.3 16.0 %shard_map.108 = (bf16[40,4096]{1,0:T(8,128)(2,1)S(1)}, bf16[40,4096]{1,0:T(8,128)(2,1)S(1)}, bf16[40,4096]{1,0:T(8,128)(2,1)S(1)}, bf16[40,4096]{1,0:T(8,128)(2...) custom-call(bf16[448,4096]{1,0:T(8,128)(2,1)} %bitcast.9.x_ref, ...), custom_call_target="tpu_custom_call" | custom-call | flops 1024 | bytes 1024 | tf_op jit(solution)/shard_map/pallas_call | solution.py:231
  126.2 4.5 %shard_map.109 = (bf16[320,4096]{1,0:T(8,128)(2,1)}, f32[8,128]{1,0:T(8,128)S(1)}) custom-call(f32[16,128]{1,0:T(8,128)S(1)} %collective-permute-done.2.meta_ref, f32[8,128]{1,0:T(8,128)S(1)} %get-tuple-element.49.after_ref.arrived_ref, f32[8,128]{1,0:T(8,128)S(1)} %get-tuple-element.49.after_ref.arrived_ref, ...), custom_call_target="tpu_custom_call" | custom-call | flops 20000002048 | bytes 1024 | tf_op jit(solution)/shard_map/pallas_call | solution.py:180
  131.3 3.8 %all-to-all-done.2 = bf16[8,40,4096]{2,1,0:T(8,128)(2,1)S(1)} async-done(((bf16[8,40,4096]{2,1,0:T(8,128)(2,1)}), bf16[8,40,4096]{2,1,0:T(8,128)(2,1)S(1)}, u32[]{:S(2)}, u32[]{:S(2)}) %all-to-all-start.2) | async-done | bytes 2621472 | tf_op jit(solution)/shard_map/all_to_all | solution.py:36
  135.1 6.0 %all-to-all-start.3 = ((bf16[8,40,4096]{2,1,0:T(8,128)(2,1)}), bf16[8,40,4096]{2,1,0:T(8,128)(2,1)}, u32[]{:S(2)}, u32[]{:S(2)}) async-start(bf16[8,40,4096]{2,1,0:T(8,128)(2,1)} %bitcast.14), calls=%async_computation.3 | async-start | bytes 5242880 | tf_op jit(solution)/shard_map/all_to_all | solution.py:36
  141.1 2.3 slice.59
  143.4 2.8 reshape.83
  146.2 1.7 slice.61
  147.8 1.1 slice.60.q_ref
  149.5 6.2 %collective-permute-start.10 = (bf16[512,256]{1,0:T(8,128)(2,1)}, bf16[512,256]{1,0:T(8,128)(2,1)}, u32[]{:S(2)}, u32[]{:S(2)}) collective-permute-start(bf16[512,256]{1,0:T(8,128)(2,1)} %shard_map.110), channel_id=1, source_target_pairs={{0,2},{1,3},{2,0},{3,1},{4,6},{5,7},{6,4},{7,5},{8,10},{9,11},{10,... | collective-permute-start | bytes 786440 | tf_op jit(solution)/shard_map/ppermute | solution.py:32
  155.7 1.5 collective-permute-start.13
  157.8 11.2 %shard_map.111 = (bf16[320,4096]{1,0:T(8,128)(2,1)S(1)}, f32[8,128]{1,0:T(8,128)S(1)}) custom-call(bf16[320,4096]{1,0:T(8,128)(2,1)S(1)} %bitcast.38, bf16[1,4096,768]{2,1,0:T(8,128)(2,1)} %gate_ref.7, bf16[1,4096,768]{2,1,0:T(8,128)(2,1)} %up_ref.7, bf16[1,768,4096]{2,1,0:T(8,128)(2,1)} %down_ref.7, f32[8,128]{1,0:T(8,128)S(1)} %slice_convert_fusion.3.after_ref), custom_call_target="tpu_custom_call" | custom-call | flops 15000000512 | bytes 1024 | tf_op jit(solution)/shard_map/pallas_call | solution.py:231
  169.0 1.5 copy-done.4
  171.4 1.1 collective-permute-done.10
  172.9 1.3 pad_maximum_fusion.kv_ref
  174.2 6.0 %all-to-all-start.4 = ((bf16[8,40,4096]{2,1,0:T(8,128)(2,1)}), bf16[8,40,4096]{2,1,0:T(8,128)(2,1)}, u32[]{:S(2)}, u32[]{:S(2)}) async-start(bf16[8,40,4096]{2,1,0:T(8,128)(2,1)} %bitcast.37), calls=%async_computation.4 | async-start | bytes 5242880 | tf_op jit(solution)/shard_map/all_to_all | solution.py:36
  180.8 13.2 %shard_map.112 = (bf16[8,64,512]{2,1,0:T(8,128)(2,1)S(1)}, f32[8,128]{1,0:T(8,128)S(1)}) custom-call(bf16[8,64,512]{2,1,0:T(8,128)(2,1)S(1)} %slice.60.q_ref, bf16[2048,256]{1,0:T(8,128)(2,1)S(1)} %pad_maximum_fusion.kv_ref, f32[8,128]{1,0:T(8,128)S(1)} %add_add_fusion.1.after_ref), custom_call_target="tpu_custom_call" | custom-call | flops 1024 | bytes 1024 | tf_op jit(solution)/shard_map/pallas_call | solution.py:85
  195.5 2.6 collective-permute-start.17
  198.8 12.5 %shard_map.114 = (bf16[320,4096]{1,0:T(8,128)(2,1)S(1)}, f32[8,128]{1,0:T(8,128)S(1)}) custom-call(bf16[320,4096]{1,0:T(8,128)(2,1)} %bitcast.15.x_ref, bf16[1,4096,768]{2,1,0:T(8,128)(2,1)} %gate_ref.7, bf16[1,4096,768]{2,1,0:T(8,128)(2,1)} %up_ref.7, bf16[1,768,4096]{2,1,0:T(8,128)(2,1)} %down_ref.7, f32[8,128]{1,0:T(8,128)S(1)} %copy-done.17), custom_call_target="tpu_custom_call" | custom-call | flops 20000002048 | bytes 1024 | tf_op jit(solution)/shard_map/pallas_call | solution.py:231
  211.4 1.5 copy-done.1
  212.9 1.8 all-to-all-done.4
  214.7 1.3 slice_convert_fusion.2.refs_1_
  216.0 5.0 %all-to-all-start.5 = ((bf16[8,40,4096]{2,1,0:T(8,128)(2,1)}), bf16[8,40,4096]{2,1,0:T(8,128)(2,1)S(1)}, u32[]{:S(2)}, u32[]{:S(2)}) async-start(bf16[8,40,4096]{2,1,0:T(8,128)(2,1)} %bitcast.33), calls=%async_computation.5 | async-start | bytes 5242880 | tf_op jit(solution)/shard_map/all_to_all | solution.py:36
  221.1 4.8 %shard_map.118 = (bf16[64,4096]{1,0:T(8,128)(2,1)}, bf16[64,4096]{1,0:T(8,128)(2,1)}, f32[8,128]{1,0:T(8,128)S(1)}) custom-call(f32[16,128]{1,0:T(8,128)S(1)} %collective-permute-done.1.meta_ref, f32[8,128]{1,0:T(8,128)S(1)} %get-tuple-element.67.after_ref, bf16[320,4096]{1,0:T(8,128)(2,1)} %bitcast.17.refs_0_), custom_call_target="tpu_custom_call" | custom-call | flops 40000000000 | bytes 1024 | tf_op jit(solution)/shard_map/pallas_call | solution.py:284
  225.8 4.2 %collective-permute-start.19 = (bf16[64,4096]{1,0:T(8,128)(2,1)}, bf16[64,4096]{1,0:T(8,128)(2,1)}, u32[]{:S(2)}, u32[]{:S(2)}) collective-permute-start(bf16[64,4096]{1,0:T(8,128)(2,1)} %get-tuple-element.78), channel_id=1, source_target_pairs={{0,2},{1,3},{2,0},{3,1},{4,6},{5,7},{6,4},{7,5},{8,10},{9,11},{10,... | collective-permute-start | bytes 1572872 | tf_op jit(solution)/shard_map/ppermute | solution.py:32
  230.7 4.6 %shard_map.120 = (bf16[128,4096]{1,0:T(8,128)(2,1)}, f32[8,128]{1,0:T(8,128)S(1)}) custom-call(f32[16,128]{1,0:T(8,128)S(1)} %copy-done.20, f32[8,128]{1,0:T(8,128)S(1)} %get-tuple-element.68.after_ref, bf16[40,4096]{1,0:T(8,128)(2,1)S(1)} %copy-done.26, bf16[40,4096]{1,0:T(8,128)(2,1)S(1)} %collective-permute-done.12.refs_1_, ...), custom_call_target="tpu_custom_call" | custom-call | flops 40000000000 | bytes 1024 | tf_op jit(solution)/shard_map/pallas_call | solution.py:284
  235.3 3.5 %collective-permute-start.21 = (bf16[128,4096]{1,0:T(8,128)(2,1)}, bf16[128,4096]{1,0:T(8,128)(2,1)}, u32[]{:S(2)}, u32[]{:S(2)}) collective-permute-start(bf16[128,4096]{1,0:T(8,128)(2,1)} %get-tuple-element.81), channel_id=1, source_target_pairs={{0,1},{1,0},{2,3},{3,2},{4,5},{5,4},{6,7},{7,6},{8,9},{9,8},{10,11... | collective-permute-start | bytes 3145736 | tf_op jit(solution)/shard_map/ppermute | solution.py:32
  238.8 20.2 %all-to-all-done.5 = bf16[8,40,4096]{2,1,0:T(8,128)(2,1)S(1)} async-done(((bf16[8,40,4096]{2,1,0:T(8,128)(2,1)}), bf16[8,40,4096]{2,1,0:T(8,128)(2,1)S(1)}, u32[]{:S(2)}, u32[]{:S(2)}) %all-to-all-start.5) | async-done | bytes 2621472 | tf_op jit(solution)/shard_map/all_to_all | solution.py:36
  259.5 6.0 %all-to-all-start.6 = ((bf16[8,40,4096]{2,1,0:T(8,128)(2,1)}), bf16[8,40,4096]{2,1,0:T(8,128)(2,1)}, u32[]{:S(2)}, u32[]{:S(2)}) async-start(bf16[8,40,4096]{2,1,0:T(8,128)(2,1)} %bitcast.32), calls=%async_computation.6 | async-start | bytes 5242880 | tf_op jit(solution)/shard_map/all_to_all | solution.py:36
  265.5 3.1 shard_map.121
  268.7 1.5 collective-permute-start.22
  270.7 25.7 %all-to-all-done.6 = bf16[8,40,4096]{2,1,0:T(8,128)(2,1)} async-done(((bf16[8,40,4096]{2,1,0:T(8,128)(2,1)}), bf16[8,40,4096]{2,1,0:T(8,128)(2,1)}, u32[]{:S(2)}, u32[]{:S(2)}) %all-to-all-start.6) | async-done | bytes 2621472 | tf_op jit(solution)/shard_map/all_to_all | solution.py:36
  296.4 1.3 slice_convert_fusion.refs_1_
  297.7 4.9 %all-to-all-start.7 = ((bf16[8,64,512]{2,1,0:T(8,128)(2,1)}), bf16[8,64,512]{2,1,0:T(8,128)(2,1)S(1)}, u32[]{:S(2)}, u32[]{:S(2)}) async-start(bf16[8,64,512]{2,1,0:T(8,128)(2,1)} %shard_map.117), calls=%async_computation.7 | async-start | bytes 1048576 | tf_op jit(solution)/shard_map/all_to_all | solution.py:36
  302.6 4.7 %shard_map.122 = (f32[128,4096]{1,0:T(8,128)S(1)}, f32[8,128]{1,0:T(8,128)}) custom-call(f32[16,128]{1,0:T(8,128)S(1)} %copy-done.14, f32[8,128]{1,0:T(8,128)S(1)} %get-tuple-element.77.after_ref, bf16[320,4096]{1,0:T(8,128)(2,1)} %bitcast.21.refs_0_, bf16[64,4096]{1,0:T(8,128)(2,1)} %collective-permute-done.19.refs_1_, ...), custom_call_target="tpu_custom_call" | custom-call | flops 40000000000 | bytes 1024 | tf_op jit(solution)/shard_map/pallas_call | solution.py:284
  307.3 2.7 collective-permute-done.22.refs_1_
  310.0 11.2 %collective-permute-done.23.refs_2_ = bf16[64,4096]{1,0:T(8,128)(2,1)S(1)} collective-permute-done((bf16[64,4096]{1,0:T(8,128)(2,1)}, bf16[64,4096]{1,0:T(8,128)(2,1)S(1)}, u32[]{:S(2)}, u32[]{:S(2)}) %collective-permute-start.23) | collective-permute-done | bytes 524320 | tf_op jit(solution)/shard_map/ppermute | solution.py:32
  321.2 3.6 %shard_map.123 = bf16[128,4096]{1,0:T(8,128)(2,1)} custom-call(f32[128,4096]{1,0:T(8,128)S(1)} %get-tuple-element.80.own_ref, bf16[128,4096]{1,0:T(8,128)(2,1)} %collective-permute-done.21.refs_0_, bf16[64,4096]{1,0:T(8,128)(2,1)S(1)} %collective-permute-done.22.refs_1_, bf16[64,4096]{1,0:T(8,128)(2,1)S(1)} %collective-permute-done.23.refs_2_), custom_call_target="tpu_custom_call" | custom-call | flops 1024 | bytes 1024 | tf_op jit(solution)/shard_map/pallas_call | solution.py:315
  (107 shorter events, 17.3 us)
Async XLA Ops:
  0.6 9.9 %copy-start.2 = (bf16[128,4096]{1,0:T(8,128)(2,1)S(1)}, bf16[128,4096]{1,0:T(8,128)(2,1)}, u32[]{:S(2)}) copy-start(bf16[128,4096]{1,0:T(8,128)(2,1)} %refs_2_.1) | copy-start | bytes 3145732
  2.1 10.1 %copy-start.13 = (f32[16,128]{1,0:T(8,128)}, f32[16,128]{1,0:T(8,128)S(1)}, u32[]{:S(2)}) copy-start(f32[16,128]{1,0:T(8,128)S(1)} %pad_maximum_fusion.3.meta_ref) | copy-start | bytes 24580
  2.1 8.3 %collective-permute-start.2 = (f32[16,128]{1,0:T(8,128)S(1)}, f32[16,128]{1,0:T(8,128)S(1)}, u32[]{:S(2)}, u32[]{:S(2)}) collective-permute-start(f32[16,128]{1,0:T(8,128)S(1)} %pad_maximum_fusion.3.meta_ref), channel_id=1, source_target_pairs={{0,3},{1,2},{2,1},{3,0},{4,7},{5,6},{6,5},{7,4},{8,11},{9,10},{10,... | collective-permute-start | bytes 24584 | tf_op jit(solution)/shard_map/ppermute | solution.py:32
  3.7 6.8 %collective-permute-start.1 = (f32[16,128]{1,0:T(8,128)S(1)}, f32[16,128]{1,0:T(8,128)S(1)}, u32[]{:S(2)}, u32[]{:S(2)}) collective-permute-start(f32[16,128]{1,0:T(8,128)S(1)} %pad_maximum_fusion.3.meta_ref), channel_id=1, source_target_pairs={{0,2},{1,3},{2,0},{3,1},{4,6},{5,7},{6,4},{7,5},{8,10},{9,11},{10,... | collective-permute-start | bytes 24584 | tf_op jit(solution)/shard_map/ppermute | solution.py:32
  4.9 5.5 %collective-permute-start = (f32[16,128]{1,0:T(8,128)S(1)}, f32[16,128]{1,0:T(8,128)S(1)}, u32[]{:S(2)}, u32[]{:S(2)}) collective-permute-start(f32[16,128]{1,0:T(8,128)S(1)} %pad_maximum_fusion.3.meta_ref), channel_id=1, source_target_pairs={{0,1},{1,0},{2,3},{3,2},{4,5},{5,4},{6,7},{7,6},{8,9},{9,8},{10,11... | collective-permute-start | bytes 24584 | tf_op jit(solution)/shard_map/ppermute | solution.py:32
  8.4 25.3 %collective-permute-start.4 = (bf16[64,4096]{1,0:T(8,128)(2,1)}, bf16[64,4096]{1,0:T(8,128)(2,1)}, u32[]{:S(2)}, u32[]{:S(2)}) collective-permute-start(bf16[64,4096]{1,0:T(8,128)(2,1)} %get-tuple-element.84), channel_id=1, source_target_pairs={{0,1},{1,0},{2,3},{3,2},{4,5},{5,4},{6,7},{7,6},{8,9},{9,8},{10,11... | collective-permute-start | bytes 1572872 | tf_op jit(solution)/shard_map/ppermute | solution.py:32
  9.2 34.6 %collective-permute-start.3 = (bf16[64,4096]{1,0:T(8,128)(2,1)}, bf16[64,4096]{1,0:T(8,128)(2,1)}, u32[]{:S(2)}, u32[]{:S(2)}) collective-permute-start(bf16[64,4096]{1,0:T(8,128)(2,1)} %get-tuple-element.85), channel_id=1, source_target_pairs={{0,1},{1,0},{2,3},{3,2},{4,5},{5,4},{6,7},{7,6},{8,9},{9,8},{10,11... | collective-permute-start | bytes 1572872 | tf_op jit(solution)/shard_map/ppermute | solution.py:32
  10.5 33.4 %copy-start.19 = (f32[16,128]{1,0:T(8,128)}, f32[16,128]{1,0:T(8,128)S(1)}, u32[]{:S(2)}) copy-start(f32[16,128]{1,0:T(8,128)S(1)} %collective-permute-done.meta_ref) | copy-start | bytes 24580
  12.3 1.5 copy-start.5
  13.7 7.3 %copy-start.29 = (bf16[64,512]{1,0:T(8,128)(2,1)S(1)}, bf16[64,512]{1,0:T(8,128)(2,1)}, u32[]{:S(2)}) copy-start(bf16[64,512]{1,0:T(8,128)(2,1)} %param.10) | copy-start | bytes 196612
  13.7 7.3 %copy-start.30 = (bf16[64,512]{1,0:T(8,128)(2,1)S(1)}, bf16[64,512]{1,0:T(8,128)(2,1)}, u32[]{:S(2)}) copy-start(bf16[64,512]{1,0:T(8,128)(2,1)} %param.11) | copy-start | bytes 196612
  13.7 38.4 %all-to-all-start.1 = ((bf16[8,40,4096]{2,1,0:T(8,128)(2,1)}), bf16[8,40,4096]{2,1,0:T(8,128)(2,1)S(1)}, u32[]{:S(2)}, u32[]{:S(2)}) async-start(bf16[8,40,4096]{2,1,0:T(8,128)(2,1)} %bitcast.39), calls=%async_computation.1 | async-start | bytes 5242880 | tf_op jit(solution)/shard_map/all_to_all | solution.py:36
  18.1 60.5 %collective-permute-start.6 = (bf16[64,4096]{1,0:T(8,128)(2,1)}, bf16[64,4096]{1,0:T(8,128)(2,1)}, u32[]{:S(2)}, u32[]{:S(2)}) collective-permute-start(bf16[64,4096]{1,0:T(8,128)(2,1)} %get-tuple-element.84), channel_id=1, source_target_pairs={{0,2},{1,3},{2,0},{3,1},{4,6},{5,7},{6,4},{7,5},{8,10},{9,11},{10,... | collective-permute-start | bytes 1572872 | tf_op jit(solution)/shard_map/ppermute | solution.py:32
  21.0 68.8 %collective-permute-start.5 = (bf16[64,4096]{1,0:T(8,128)(2,1)}, bf16[64,4096]{1,0:T(8,128)(2,1)}, u32[]{:S(2)}, u32[]{:S(2)}) collective-permute-start(bf16[64,4096]{1,0:T(8,128)(2,1)} %get-tuple-element.85), channel_id=1, source_target_pairs={{0,2},{1,3},{2,0},{3,1},{4,6},{5,7},{6,4},{7,5},{8,10},{9,11},{10,... | collective-permute-start | bytes 1572872 | tf_op jit(solution)/shard_map/ppermute | solution.py:32
  43.8 1.2 copy-start.3
  50.1 76.1 %collective-permute-start.7 = (bf16[64,4096]{1,0:T(8,128)(2,1)}, bf16[64,4096]{1,0:T(8,128)(2,1)}, u32[]{:S(2)}, u32[]{:S(2)}) collective-permute-start(bf16[64,4096]{1,0:T(8,128)(2,1)} %get-tuple-element.50), channel_id=1, source_target_pairs={{0,3},{1,2},{2,1},{3,0},{4,7},{5,6},{6,5},{7,4},{8,11},{9,10},{10,... | collective-permute-start | bytes 1572872 | tf_op jit(solution)/shard_map/ppermute | solution.py:32
  50.6 75.6 %collective-permute-start.8 = (bf16[64,4096]{1,0:T(8,128)(2,1)}, bf16[64,4096]{1,0:T(8,128)(2,1)}, u32[]{:S(2)}, u32[]{:S(2)}) collective-permute-start(bf16[64,4096]{1,0:T(8,128)(2,1)} %get-tuple-element.51), channel_id=1, source_target_pairs={{0,3},{1,2},{2,1},{3,0},{4,7},{5,6},{6,5},{7,4},{8,11},{9,10},{10,... | collective-permute-start | bytes 1572872 | tf_op jit(solution)/shard_map/ppermute | solution.py:32
  52.1 47.2 %all-to-all-start = ((bf16[8,56,4096]{2,1,0:T(8,128)(2,1)}), bf16[8,56,4096]{2,1,0:T(8,128)(2,1)}, u32[]{:S(2)}, u32[]{:S(2)}) async-start(bf16[8,56,4096]{2,1,0:T(8,128)(2,1)} %bitcast.42), calls=%async_computation | async-start | bytes 7340032 | tf_op jit(solution)/shard_map/all_to_all | solution.py:36
  68.3 1.6 copy-start
  93.1 1.5 copy-start.6
  99.3 35.8 %all-to-all-start.2 = ((bf16[8,40,4096]{2,1,0:T(8,128)(2,1)}), bf16[8,40,4096]{2,1,0:T(8,128)(2,1)S(1)}, u32[]{:S(2)}, u32[]{:S(2)}) async-start(bf16[8,40,4096]{2,1,0:T(8,128)(2,1)} %bitcast.40), calls=%async_computation.2 | async-start | bytes 5242880 | tf_op jit(solution)/shard_map/all_to_all | solution.py:36
  120.3 0.7 copy-start.8
  121.1 0.7 copy-start.9
  121.8 0.7 copy-start.10
  122.5 0.7 copy-start.11
  123.3 0.7 copy-start.12
  124.0 0.7 copy-start.25
  124.7 0.7 copy-start.27
  125.4 0.7 copy-start.28
  130.7 0.6 copy-start.18
  135.1 39.0 %all-to-all-start.3 = ((bf16[8,40,4096]{2,1,0:T(8,128)(2,1)}), bf16[8,40,4096]{2,1,0:T(8,128)(2,1)}, u32[]{:S(2)}, u32[]{:S(2)}) async-start(bf16[8,40,4096]{2,1,0:T(8,128)(2,1)} %bitcast.14), calls=%async_computation.3 | async-start | bytes 5242880 | tf_op jit(solution)/shard_map/all_to_all | solution.py:36
  148.9 22.1 %collective-permute-start.11 = (bf16[512,256]{1,0:T(8,128)(2,1)}, bf16[512,256]{1,0:T(8,128)(2,1)}, u32[]{:S(2)}, u32[]{:S(2)}) collective-permute-start(bf16[512,256]{1,0:T(8,128)(2,1)} %shard_map.110), channel_id=1, source_target_pairs={{0,3},{1,2},{2,1},{3,0},{4,7},{5,6},{6,5},{7,4},{8,11},{9,10},{10,... | collective-permute-start | bytes 786440 | tf_op jit(solution)/shard_map/ppermute | solution.py:32
  149.5 23.0 %collective-permute-start.10 = (bf16[512,256]{1,0:T(8,128)(2,1)}, bf16[512,256]{1,0:T(8,128)(2,1)}, u32[]{:S(2)}, u32[]{:S(2)}) collective-permute-start(bf16[512,256]{1,0:T(8,128)(2,1)} %shard_map.110), channel_id=1, source_target_pairs={{0,2},{1,3},{2,0},{3,1},{4,6},{5,7},{6,4},{7,5},{8,10},{9,11},{10,... | collective-permute-start | bytes 786440 | tf_op jit(solution)/shard_map/ppermute | solution.py:32
  155.6 17.2 %collective-permute-start.9 = (bf16[512,256]{1,0:T(8,128)(2,1)}, bf16[512,256]{1,0:T(8,128)(2,1)}, u32[]{:S(2)}, u32[]{:S(2)}) collective-permute-start(bf16[512,256]{1,0:T(8,128)(2,1)} %shard_map.110), channel_id=1, source_target_pairs={{0,1},{1,0},{2,3},{3,2},{4,5},{5,4},{6,7},{7,6},{8,9},{9,8},{10,11... | collective-permute-start | bytes 786440 | tf_op jit(solution)/shard_map/ppermute | solution.py:32
  155.7 24.5 %collective-permute-start.12 = (bf16[40,4096]{1,0:T(8,128)(2,1)}, bf16[40,4096]{1,0:T(8,128)(2,1)S(1)}, u32[]{:S(2)}, u32[]{:S(2)}) collective-permute-start(bf16[40,4096]{1,0:T(8,128)(2,1)} %copy-done.28), channel_id=1, source_target_pairs={{0,4},{4,0},{8,12},{12,8},{16,20},{20,16},{24,28},{28,24},{1,5},{5... | collective-permute-start | bytes 983048 | tf_op jit(solution)/shard_map/ppermute | solution.py:32
  155.7 24.5 %collective-permute-start.13 = (bf16[40,4096]{1,0:T(8,128)(2,1)}, bf16[40,4096]{1,0:T(8,128)(2,1)}, u32[]{:S(2)}, u32[]{:S(2)}) collective-permute-start(bf16[40,4096]{1,0:T(8,128)(2,1)} %copy-done.27), channel_id=1, source_target_pairs={{0,8},{4,12},{8,0},{12,4},{16,24},{20,28},{24,16},{28,20},{1,9},{5... | collective-permute-start | bytes 983048 | tf_op jit(solution)/shard_map/ppermute | solution.py:32
  169.0 1.5 copy-start.4
  170.5 0.6 copy-start.15
  171.1 23.7 %collective-permute-start.14 = (bf16[40,4096]{1,0:T(8,128)(2,1)}, bf16[40,4096]{1,0:T(8,128)(2,1)S(1)}, u32[]{:S(2)}, u32[]{:S(2)}) collective-permute-start(bf16[40,4096]{1,0:T(8,128)(2,1)} %get-tuple-element.63), channel_id=1, source_target_pairs={{0,12},{4,8},{8,4},{12,0},{16,28},{20,24},{24,20},{28,16},{1,13},{... | collective-permute-start | bytes 983048 | tf_op jit(solution)/shard_map/ppermute | solution.py:32
  172.5 22.2 %collective-permute-start.15 = (bf16[40,4096]{1,0:T(8,128)(2,1)}, bf16[40,4096]{1,0:T(8,128)(2,1)S(1)}, u32[]{:S(2)}, u32[]{:S(2)}) collective-permute-start(bf16[40,4096]{1,0:T(8,128)(2,1)} %get-tuple-element.64), channel_id=1, source_target_pairs={{0,16},{4,20},{8,24},{12,28},{16,0},{20,4},{24,8},{28,12},{1,17},{... | collective-permute-start | bytes 983048 | tf_op jit(solution)/shard_map/ppermute | solution.py:32
  174.2 6.0 %copy-start.16 = (f32[8,128]{1,0:T(8,128)S(1)}, f32[8,128]{1,0:T(8,128)}, u32[]{:S(2)}) copy-start(f32[8,128]{1,0:T(8,128)} %copy-done.15) | copy-start | bytes 12292
  174.2 40.6 %all-to-all-start.4 = ((bf16[8,40,4096]{2,1,0:T(8,128)(2,1)}), bf16[8,40,4096]{2,1,0:T(8,128)(2,1)}, u32[]{:S(2)}, u32[]{:S(2)}) async-start(bf16[8,40,4096]{2,1,0:T(8,128)(2,1)} %bitcast.37), calls=%async_computation.4 | async-start | bytes 5242880 | tf_op jit(solution)/shard_map/all_to_all | solution.py:36
  194.0 0.8 copy-start.7
  194.8 16.6 %copy-start.21 = (bf16[40,4096]{1,0:T(8,128)(2,1)}, bf16[40,4096]{1,0:T(8,128)(2,1)S(1)}, u32[]{:S(2)}) copy-start(bf16[40,4096]{1,0:T(8,128)(2,1)S(1)} %collective-permute-done.14.refs_3_) | copy-start | bytes 983044
  194.8 16.6 %copy-start.23 = (bf16[40,4096]{1,0:T(8,128)(2,1)}, bf16[40,4096]{1,0:T(8,128)(2,1)S(1)}, u32[]{:S(2)}) copy-start(bf16[40,4096]{1,0:T(8,128)(2,1)S(1)} %collective-permute-done.15.refs_4_) | copy-start | bytes 983044
  195.4 35.2 %collective-permute-start.16 = (bf16[40,4096]{1,0:T(8,128)(2,1)}, bf16[40,4096]{1,0:T(8,128)(2,1)}, u32[]{:S(2)}, u32[]{:S(2)}) collective-permute-start(bf16[40,4096]{1,0:T(8,128)(2,1)} %get-tuple-element.73), channel_id=1, source_target_pairs={{0,20},{4,16},{8,28},{12,24},{16,4},{20,0},{24,12},{28,8},{1,21},{... | collective-permute-start | bytes 983048 | tf_op jit(solution)/shard_map/ppermute | solution.py:32
  195.5 35.1 %collective-permute-start.17 = (bf16[40,4096]{1,0:T(8,128)(2,1)}, bf16[40,4096]{1,0:T(8,128)(2,1)}, u32[]{:S(2)}, u32[]{:S(2)}) collective-permute-start(bf16[40,4096]{1,0:T(8,128)(2,1)} %get-tuple-element.74), channel_id=1, source_target_pairs={{0,24},{4,28},{8,16},{12,20},{16,8},{20,12},{24,0},{28,4},{1,25},{... | collective-permute-start | bytes 983048 | tf_op jit(solution)/shard_map/ppermute | solution.py:32
  198.1 32.5 %collective-permute-start.18 = (bf16[40,4096]{1,0:T(8,128)(2,1)}, bf16[40,4096]{1,0:T(8,128)(2,1)}, u32[]{:S(2)}, u32[]{:S(2)}) collective-permute-start(bf16[40,4096]{1,0:T(8,128)(2,1)} %get-tuple-element.75), channel_id=1, source_target_pairs={{0,28},{4,24},{8,20},{12,16},{16,12},{20,8},{24,4},{28,0},{1,29},{... | collective-permute-start | bytes 983048 | tf_op jit(solution)/shard_map/ppermute | solution.py:32
  198.1 0.7 copy-start.17
  211.4 1.5 copy-start.1
  216.0 42.9 %all-to-all-start.5 = ((bf16[8,40,4096]{2,1,0:T(8,128)(2,1)}), bf16[8,40,4096]{2,1,0:T(8,128)(2,1)S(1)}, u32[]{:S(2)}, u32[]{:S(2)}) async-start(bf16[8,40,4096]{2,1,0:T(8,128)(2,1)} %bitcast.33), calls=%async_computation.5 | async-start | bytes 5242880 | tf_op jit(solution)/shard_map/all_to_all | solution.py:36
  221.0 9.6 %copy-start.20 = (f32[16,128]{1,0:T(8,128)S(1)}, f32[16,128]{1,0:T(8,128)}, u32[]{:S(2)}) copy-start(f32[16,128]{1,0:T(8,128)} %copy-done.19) | copy-start | bytes 24580
  221.0 9.6 %copy-start.22 = (bf16[40,4096]{1,0:T(8,128)(2,1)S(1)}, bf16[40,4096]{1,0:T(8,128)(2,1)}, u32[]{:S(2)}) copy-start(bf16[40,4096]{1,0:T(8,128)(2,1)} %copy-done.21) | copy-start | bytes 983044
  221.0 9.7 %copy-start.24 = (bf16[40,4096]{1,0:T(8,128)(2,1)S(1)}, bf16[40,4096]{1,0:T(8,128)(2,1)}, u32[]{:S(2)}) copy-start(bf16[40,4096]{1,0:T(8,128)(2,1)} %copy-done.23) | copy-start | bytes 983044
  221.0 9.7 %copy-start.26 = (bf16[40,4096]{1,0:T(8,128)(2,1)S(1)}, bf16[40,4096]{1,0:T(8,128)(2,1)}, u32[]{:S(2)}) copy-start(bf16[40,4096]{1,0:T(8,128)(2,1)} %copy-done.25) | copy-start | bytes 983044
  225.8 76.7 %collective-permute-start.19 = (bf16[64,4096]{1,0:T(8,128)(2,1)}, bf16[64,4096]{1,0:T(8,128)(2,1)}, u32[]{:S(2)}, u32[]{:S(2)}) collective-permute-start(bf16[64,4096]{1,0:T(8,128)(2,1)} %get-tuple-element.78), channel_id=1, source_target_pairs={{0,2},{1,3},{2,0},{3,1},{4,6},{5,7},{6,4},{7,5},{8,10},{9,11},{10,... | collective-permute-start | bytes 1572872 | tf_op jit(solution)/shard_map/ppermute | solution.py:32
  230.1 72.5 %collective-permute-start.20 = (bf16[64,4096]{1,0:T(8,128)(2,1)}, bf16[64,4096]{1,0:T(8,128)(2,1)}, u32[]{:S(2)}, u32[]{:S(2)}) collective-permute-start(bf16[64,4096]{1,0:T(8,128)(2,1)} %get-tuple-element.79), channel_id=1, source_target_pairs={{0,2},{1,3},{2,0},{3,1},{4,6},{5,7},{6,4},{7,5},{8,10},{9,11},{10,... | collective-permute-start | bytes 1572872 | tf_op jit(solution)/shard_map/ppermute | solution.py:32
  235.3 72.0 %collective-permute-start.21 = (bf16[128,4096]{1,0:T(8,128)(2,1)}, bf16[128,4096]{1,0:T(8,128)(2,1)}, u32[]{:S(2)}, u32[]{:S(2)}) collective-permute-start(bf16[128,4096]{1,0:T(8,128)(2,1)} %get-tuple-element.81), channel_id=1, source_target_pairs={{0,1},{1,0},{2,3},{3,2},{4,5},{5,4},{6,7},{7,6},{8,9},{9,8},{10,11... | collective-permute-start | bytes 3145736 | tf_op jit(solution)/shard_map/ppermute | solution.py:32
  259.5 36.9 %all-to-all-start.6 = ((bf16[8,40,4096]{2,1,0:T(8,128)(2,1)}), bf16[8,40,4096]{2,1,0:T(8,128)(2,1)}, u32[]{:S(2)}, u32[]{:S(2)}) async-start(bf16[8,40,4096]{2,1,0:T(8,128)(2,1)} %bitcast.32), calls=%async_computation.6 | async-start | bytes 5242880 | tf_op jit(solution)/shard_map/all_to_all | solution.py:36
  265.5 37.1 %copy-start.14 = (f32[16,128]{1,0:T(8,128)S(1)}, f32[16,128]{1,0:T(8,128)}, u32[]{:S(2)}) copy-start(f32[16,128]{1,0:T(8,128)} %copy-done.13) | copy-start | bytes 24580
  268.7 41.4 %collective-permute-start.22 = (bf16[64,4096]{1,0:T(8,128)(2,1)}, bf16[64,4096]{1,0:T(8,128)(2,1)S(1)}, u32[]{:S(2)}, u32[]{:S(2)}) collective-permute-start(bf16[64,4096]{1,0:T(8,128)(2,1)} %get-tuple-element.82), channel_id=1, source_target_pairs={{0,3},{1,2},{2,1},{3,0},{4,7},{5,6},{6,5},{7,4},{8,11},{9,10},{10,... | collective-permute-start | bytes 1572872 | tf_op jit(solution)/shard_map/ppermute | solution.py:32
  270.2 51.0 %collective-permute-start.23 = (bf16[64,4096]{1,0:T(8,128)(2,1)}, bf16[64,4096]{1,0:T(8,128)(2,1)S(1)}, u32[]{:S(2)}, u32[]{:S(2)}) collective-permute-start(bf16[64,4096]{1,0:T(8,128)(2,1)} %get-tuple-element.83), channel_id=1, source_target_pairs={{0,3},{1,2},{2,1},{3,0},{4,7},{5,6},{6,5},{7,4},{8,11},{9,10},{10,... | collective-permute-start | bytes 1572872 | tf_op jit(solution)/shard_map/ppermute | solution.py:32
  297.7 27.1 %all-to-all-start.7 = ((bf16[8,64,512]{2,1,0:T(8,128)(2,1)}), bf16[8,64,512]{2,1,0:T(8,128)(2,1)S(1)}, u32[]{:S(2)}, u32[]{:S(2)}) async-start(bf16[8,64,512]{2,1,0:T(8,128)(2,1)} %shard_map.117), calls=%async_computation.7 | async-start | bytes 1048576 | tf_op jit(solution)/shard_map/all_to_all | solution.py:36

commit v5 on v4

--- a/solution.py
+++ b/solution.py
@@ -12,7 +12,7 @@
 F32 = jnp.float32
 BF16 = jnp.bfloat16
 VMEM = 48 * 1024 * 1024
-COSTS = {"pack1": 20, "pack2": 40, "pack3": 20, "ffn2": 15, "ffn3": 20}
+COSTS = {"pack1": 20, "pack2": 30, "pack3": 20, "ffn2": 15, "ffn3": 20}
 COSTS.update({f"combine{s}": 40 for s in range(4)})
 
 

time: 328 us -> 326 us (level)
  starting transfers between devices: 74.7 us -> 71.3 us
    ppermute x24, starting transfers between devices: 32.4 us -> 28.9 us  [swap(): return lax.ppermute(value, axis, [(i, i ^ offset) for i in range(count)])]
    unnamed x62 -> x66, local copies, waits for them, and re-layouts: 17.2 us -> 18.8 us
where the time goes in v5:
time: 326 us; the launch traced here: 324 us
  waiting for transfers between devices  108 us (33%)
  Pallas kernels  99.3 us (30%)
  starting transfers between devices  71.3 us (22%)
  local copies, waits for them, and re-layouts  34.9 us (11%)
  other arithmetic  8.88 us (3%)
    all_to_all x8, waiting for transfers between devices, exchange(): return lax.all_to_all(value, 'ctx', split_axis=0, concat_axis=0, tiled=True)  55.7 us
    ppermute x24, waiting for transfers between devices, swap(): return lax.ppermute(value, axis, [(i, i ^ offset) for i in range(count)])  52.5 us
    pallas_call x4, Pallas kernels, ffn(): pl.pallas_call(functools.partial(ffn_kernel, split > 1), grid=(hidden //...  50.9 us
    all_to_all x8, starting transfers between devices, exchange(): return lax.all_to_all(value, 'ctx', split_axis=0, concat_axis=0, tiled=True)  42.3 us
    ppermute x24, starting transfers between devices, swap(): return lax.ppermute(value, axis, [(i, i ^ offset) for i in range(count)])  28.9 us
    unnamed x66, local copies, waits for them, and re-layouts  18.8 us
    pallas_call x4, Pallas kernels, combine(): pl.pallas_call(functools.partial(combine_kernel, plan, len(backs), len(pi...  17.3 us
    pallas_call x4, Pallas kernels, pack(): pl.pallas_call(functools.partial(pack_kernel, plan, len(pieces), other is...  14.4 us
  transfers between devices with their start and end apart: 32, of which 13 were waited for; matrix products, arithmetic and copies ran while one was open for 7% of the time, Pallas kernels for 31%

profile of v5, /device:TPU:12, one launch (start us, length us, event | category | flops | bytes accessed | tf_op | source)
XLA Modules:
  0.0 323.5 jit_solution(17603543005549789972)
XLA Ops:
  2.1 1.6 collective-permute-start.2
  3.7 1.2 collective-permute-start.1
  4.9 1.2 collective-permute-start
  6.2 2.2 fusion
  9.2 1.2 collective-permute-start.3
  10.5 1.7 shard_map.104
  12.2 1.5 copy-done.5
  13.7 4.4 %all-to-all-start.1 = ((bf16[8,40,4096]{2,1,0:T(8,128)(2,1)}), bf16[8,40,4096]{2,1,0:T(8,128)(2,1)S(1)}, u32[]{:S(2)}, u32[]{:S(2)}) async-start(bf16[8,40,4096]{2,1,0:T(8,128)(2,1)} %bitcast.39), calls=%async_computation.1 | async-start | bytes 5242880 | tf_op jit(solution)/shard_map/all_to_all | solution.py:36
  18.1 2.9 collective-permute-start.6
  21.2 1.1 copy.27
  22.3 0.9 pad_maximum_fusion.1
  23.2 2.7 reshape.80
  26.0 1.3 pad.4
  27.3 6.4 %collective-permute-done.4.refs_1_ = bf16[64,4096]{1,0:T(8,128)(2,1)} collective-permute-done((bf16[64,4096]{1,0:T(8,128)(2,1)}, bf16[64,4096]{1,0:T(8,128)(2,1)}, u32[]{:S(2)}, u32[]{:S(2)}) %collective-permute-start.4) | collective-permute-done | bytes 524320 | tf_op jit(solution)/shard_map/ppermute | solution.py:32
  33.7 10.1 %collective-permute-done.3.refs_0_ = bf16[64,4096]{1,0:T(8,128)(2,1)} collective-permute-done((bf16[64,4096]{1,0:T(8,128)(2,1)}, bf16[64,4096]{1,0:T(8,128)(2,1)}, u32[]{:S(2)}, u32[]{:S(2)}) %collective-permute-start.3) | collective-permute-done | bytes 524320 | tf_op jit(solution)/shard_map/ppermute | solution.py:32
  43.8 1.2 copy-done.3
  45.0 4.9 %shard_map.105 = (bf16[448,4096]{1,0:T(8,128)(2,1)}, f32[8,128]{1,0:T(8,128)S(1)}, bf16[64,4096]{1,0:T(8,128)(2,1)S(1)}, bf16[64,4096]{1,0:T(8,128)(2,1)S(1)}) custom-call(f32[16,128]{1,0:T(8,128)S(1)} %collective-permute-done.meta_ref, f32[8,128]{1,0:T(8,128)S(1)} %get-tuple-element.43.after_ref.arrived_ref, ...), custom_call_target="tpu_custom_call" | custom-call | flops 20000002048 | bytes 1024 | tf_op jit(solution)/shard_map/pallas_call | solution.py:180
  51.5 5.0 %all-to-all-start = ((bf16[8,56,4096]{2,1,0:T(8,128)(2,1)}), bf16[8,56,4096]{2,1,0:T(8,128)(2,1)}, u32[]{:S(2)}, u32[]{:S(2)}) async-start(bf16[8,56,4096]{2,1,0:T(8,128)(2,1)} %bitcast.42), calls=%async_computation | async-start | bytes 7340032 | tf_op jit(solution)/shard_map/all_to_all | solution.py:36
  57.1 1.6 collective-permute-start.8
  58.6 11.2 %shard_map.106 = (bf16[320,4096]{1,0:T(8,128)(2,1)S(1)}, f32[8,128]{1,0:T(8,128)S(1)}) custom-call(bf16[320,4096]{1,0:T(8,128)(2,1)S(1)} %bitcast.34, bf16[1,4096,768]{2,1,0:T(8,128)(2,1)} %gate_ref.7, bf16[1,4096,768]{2,1,0:T(8,128)(2,1)} %up_ref.7, bf16[1,768,4096]{2,1,0:T(8,128)(2,1)} %down_ref.7, f32[8,128]{1,0:T(8,128)S(1)} %get-tuple-element.46.after_ref), custom_call_target="tpu_custom_call" | custom-call | flops 1024 | bytes 1024 | tf_op jit(solution)/shard_map/pallas_call | solution.py:231
  69.8 1.5 copy-done
  71.3 18.5 %collective-permute-done.5.refs_0_ = bf16[64,4096]{1,0:T(8,128)(2,1)} collective-permute-done((bf16[64,4096]{1,0:T(8,128)(2,1)}, bf16[64,4096]{1,0:T(8,128)(2,1)}, u32[]{:S(2)}, u32[]{:S(2)}) %collective-permute-start.5) | collective-permute-done | bytes 524320 | tf_op jit(solution)/shard_map/ppermute | solution.py:32
  89.8 3.2 %shard_map.107 = (bf16[320,4096]{1,0:T(8,128)(2,1)S(1)}, f32[8,128]{1,0:T(8,128)S(1)}) custom-call(f32[16,128]{1,0:T(8,128)S(1)} %collective-permute-done.1.meta_ref, f32[8,128]{1,0:T(8,128)S(1)} %get-tuple-element.47.after_ref.arrived_ref, f32[8,128]{1,0:T(8,128)S(1)} %get-tuple-element.47.after_ref.arrived_ref, ...), custom_call_target="tpu_custom_call" | custom-call | flops 30000001024 | bytes 1024 | tf_op jit(solution)/shard_map/pallas_call | solution.py:180
  93.1 1.5 copy-done.6
  94.6 4.2 %all-to-all-done = bf16[8,56,4096]{2,1,0:T(8,128)(2,1)} async-done(((bf16[8,56,4096]{2,1,0:T(8,128)(2,1)}), bf16[8,56,4096]{2,1,0:T(8,128)(2,1)}, u32[]{:S(2)}, u32[]{:S(2)}) %all-to-all-start) | async-done | bytes 3670048 | tf_op jit(solution)/shard_map/all_to_all | solution.py:36
  98.7 5.0 %all-to-all-start.2 = ((bf16[8,40,4096]{2,1,0:T(8,128)(2,1)}), bf16[8,40,4096]{2,1,0:T(8,128)(2,1)S(1)}, u32[]{:S(2)}, u32[]{:S(2)}) async-start(bf16[8,40,4096]{2,1,0:T(8,128)(2,1)} %bitcast.40), calls=%async_computation.2 | async-start | bytes 5242880 | tf_op jit(solution)/shard_map/all_to_all | solution.py:36
  103.8 16.0 %shard_map.108 = (bf16[40,4096]{1,0:T(8,128)(2,1)S(1)}, bf16[40,4096]{1,0:T(8,128)(2,1)S(1)}, bf16[40,4096]{1,0:T(8,128)(2,1)S(1)}, bf16[40,4096]{1,0:T(8,128)(2...) custom-call(bf16[448,4096]{1,0:T(8,128)(2,1)} %bitcast.9.x_ref, ...), custom_call_target="tpu_custom_call" | custom-call | flops 1024 | bytes 1024 | tf_op jit(solution)/shard_map/pallas_call | solution.py:231
  125.6 4.5 %shard_map.109 = (bf16[320,4096]{1,0:T(8,128)(2,1)}, f32[8,128]{1,0:T(8,128)S(1)}) custom-call(f32[16,128]{1,0:T(8,128)S(1)} %collective-permute-done.2.meta_ref, f32[8,128]{1,0:T(8,128)S(1)} %get-tuple-element.49.after_ref.arrived_ref, f32[8,128]{1,0:T(8,128)S(1)} %get-tuple-element.49.after_ref.arrived_ref, ...), custom_call_target="tpu_custom_call" | custom-call | flops 20000002048 | bytes 1024 | tf_op jit(solution)/shard_map/pallas_call | solution.py:180
  130.7 3.8 %all-to-all-done.2 = bf16[8,40,4096]{2,1,0:T(8,128)(2,1)S(1)} async-done(((bf16[8,40,4096]{2,1,0:T(8,128)(2,1)}), bf16[8,40,4096]{2,1,0:T(8,128)(2,1)S(1)}, u32[]{:S(2)}, u32[]{:S(2)}) %all-to-all-start.2) | async-done | bytes 2621472 | tf_op jit(solution)/shard_map/all_to_all | solution.py:36
  134.5 6.0 %all-to-all-start.3 = ((bf16[8,40,4096]{2,1,0:T(8,128)(2,1)}), bf16[8,40,4096]{2,1,0:T(8,128)(2,1)}, u32[]{:S(2)}, u32[]{:S(2)}) async-start(bf16[8,40,4096]{2,1,0:T(8,128)(2,1)} %bitcast.14), calls=%async_computation.3 | async-start | bytes 5242880 | tf_op jit(solution)/shard_map/all_to_all | solution.py:36
  140.5 2.3 slice.59
  142.8 2.7 reshape.83
  145.5 1.7 slice.61
  147.2 1.1 slice.60.q_ref
  148.8 4.4 %collective-permute-start.10 = (bf16[512,256]{1,0:T(8,128)(2,1)}, bf16[512,256]{1,0:T(8,128)(2,1)}, u32[]{:S(2)}, u32[]{:S(2)}) collective-permute-start(bf16[512,256]{1,0:T(8,128)(2,1)} %shard_map.110), channel_id=1, source_target_pairs={{0,2},{1,3},{2,0},{3,1},{4,6},{5,7},{6,4},{7,5},{8,10},{9,11},{10,... | collective-permute-start | bytes 786440 | tf_op jit(solution)/shard_map/ppermute | solution.py:32
  153.2 1.5 collective-permute-start.13
  155.4 11.2 %shard_map.111 = (bf16[320,4096]{1,0:T(8,128)(2,1)S(1)}, f32[8,128]{1,0:T(8,128)S(1)}) custom-call(bf16[320,4096]{1,0:T(8,128)(2,1)S(1)} %bitcast.38, bf16[1,4096,768]{2,1,0:T(8,128)(2,1)} %gate_ref.7, bf16[1,4096,768]{2,1,0:T(8,128)(2,1)} %up_ref.7, bf16[1,768,4096]{2,1,0:T(8,128)(2,1)} %down_ref.7, f32[8,128]{1,0:T(8,128)S(1)} %slice_convert_fusion.3.after_ref), custom_call_target="tpu_custom_call" | custom-call | flops 15000000512 | bytes 1024 | tf_op jit(solution)/shard_map/pallas_call | solution.py:231
  166.6 1.5 copy-done.4
  169.1 2.8 collective-permute-done.10
  172.2 1.3 pad_maximum_fusion.kv_ref
  173.5 6.0 %all-to-all-start.4 = ((bf16[8,40,4096]{2,1,0:T(8,128)(2,1)}), bf16[8,40,4096]{2,1,0:T(8,128)(2,1)}, u32[]{:S(2)}, u32[]{:S(2)}) async-start(bf16[8,40,4096]{2,1,0:T(8,128)(2,1)} %bitcast.37), calls=%async_computation.4 | async-start | bytes 5242880 | tf_op jit(solution)/shard_map/all_to_all | solution.py:36
  180.2 13.2 %shard_map.112 = (bf16[8,64,512]{2,1,0:T(8,128)(2,1)S(1)}, f32[8,128]{1,0:T(8,128)S(1)}) custom-call(bf16[8,64,512]{2,1,0:T(8,128)(2,1)S(1)} %slice.60.q_ref, bf16[2048,256]{1,0:T(8,128)(2,1)S(1)} %pad_maximum_fusion.kv_ref, f32[8,128]{1,0:T(8,128)S(1)} %add_add_fusion.1.after_ref), custom_call_target="tpu_custom_call" | custom-call | flops 1024 | bytes 1024 | tf_op jit(solution)/shard_map/pallas_call | solution.py:85
  194.9 2.6 collective-permute-start.17
  198.2 12.5 %shard_map.114 = (bf16[320,4096]{1,0:T(8,128)(2,1)S(1)}, f32[8,128]{1,0:T(8,128)S(1)}) custom-call(bf16[320,4096]{1,0:T(8,128)(2,1)} %bitcast.15.x_ref, bf16[1,4096,768]{2,1,0:T(8,128)(2,1)} %gate_ref.7, bf16[1,4096,768]{2,1,0:T(8,128)(2,1)} %up_ref.7, bf16[1,768,4096]{2,1,0:T(8,128)(2,1)} %down_ref.7, f32[8,128]{1,0:T(8,128)S(1)} %copy-done.17), custom_call_target="tpu_custom_call" | custom-call | flops 20000002048 | bytes 1024 | tf_op jit(solution)/shard_map/pallas_call | solution.py:231
  210.8 1.4 copy-done.1
  212.3 1.9 all-to-all-done.4
  214.2 1.3 slice_convert_fusion.2.refs_1_
  215.4 5.0 %all-to-all-start.5 = ((bf16[8,40,4096]{2,1,0:T(8,128)(2,1)}), bf16[8,40,4096]{2,1,0:T(8,128)(2,1)S(1)}, u32[]{:S(2)}, u32[]{:S(2)}) async-start(bf16[8,40,4096]{2,1,0:T(8,128)(2,1)} %bitcast.33), calls=%async_computation.5 | async-start | bytes 5242880 | tf_op jit(solution)/shard_map/all_to_all | solution.py:36
  220.5 4.9 %shard_map.118 = (bf16[64,4096]{1,0:T(8,128)(2,1)}, bf16[64,4096]{1,0:T(8,128)(2,1)}, f32[8,128]{1,0:T(8,128)S(1)}) custom-call(f32[16,128]{1,0:T(8,128)S(1)} %collective-permute-done.1.meta_ref, f32[8,128]{1,0:T(8,128)S(1)} %get-tuple-element.67.after_ref, bf16[320,4096]{1,0:T(8,128)(2,1)} %bitcast.17.refs_0_), custom_call_target="tpu_custom_call" | custom-call | flops 40000000000 | bytes 1024 | tf_op jit(solution)/shard_map/pallas_call | solution.py:284
  225.3 2.4 collective-permute-start.19
  228.3 1.8 collective-permute-done.16.refs_5_
  230.1 4.6 %shard_map.120 = (bf16[128,4096]{1,0:T(8,128)(2,1)}, f32[8,128]{1,0:T(8,128)S(1)}) custom-call(f32[16,128]{1,0:T(8,128)S(1)} %copy-done.20, f32[8,128]{1,0:T(8,128)S(1)} %get-tuple-element.68.after_ref, bf16[40,4096]{1,0:T(8,128)(2,1)S(1)} %copy-done.28, bf16[40,4096]{1,0:T(8,128)(2,1)S(1)} %collective-permute-done.12.refs_1_, ...), custom_call_target="tpu_custom_call" | custom-call | flops 40000000000 | bytes 1024 | tf_op jit(solution)/shard_map/pallas_call | solution.py:284
  234.7 3.5 %collective-permute-start.21 = (bf16[128,4096]{1,0:T(8,128)(2,1)}, bf16[128,4096]{1,0:T(8,128)(2,1)}, u32[]{:S(2)}, u32[]{:S(2)}) collective-permute-start(bf16[128,4096]{1,0:T(8,128)(2,1)} %get-tuple-element.81), channel_id=1, source_target_pairs={{0,1},{1,0},{2,3},{3,2},{4,5},{5,4},{6,7},{7,6},{8,9},{9,8},{10,11... | collective-permute-start | bytes 3145736 | tf_op jit(solution)/shard_map/ppermute | solution.py:32
  238.1 20.1 %all-to-all-done.5 = bf16[8,40,4096]{2,1,0:T(8,128)(2,1)S(1)} async-done(((bf16[8,40,4096]{2,1,0:T(8,128)(2,1)}), bf16[8,40,4096]{2,1,0:T(8,128)(2,1)S(1)}, u32[]{:S(2)}, u32[]{:S(2)}) %all-to-all-start.5) | async-done | bytes 2621472 | tf_op jit(solution)/shard_map/all_to_all | solution.py:36
  258.9 6.0 %all-to-all-start.6 = ((bf16[8,40,4096]{2,1,0:T(8,128)(2,1)}), bf16[8,40,4096]{2,1,0:T(8,128)(2,1)}, u32[]{:S(2)}, u32[]{:S(2)}) async-start(bf16[8,40,4096]{2,1,0:T(8,128)(2,1)} %bitcast.32), calls=%async_computation.6 | async-start | bytes 5242880 | tf_op jit(solution)/shard_map/all_to_all | solution.py:36
  264.9 3.2 shard_map.121
  268.1 1.6 collective-permute-start.22
  270.1 25.7 %all-to-all-done.6 = bf16[8,40,4096]{2,1,0:T(8,128)(2,1)} async-done(((bf16[8,40,4096]{2,1,0:T(8,128)(2,1)}), bf16[8,40,4096]{2,1,0:T(8,128)(2,1)}, u32[]{:S(2)}, u32[]{:S(2)}) %all-to-all-start.6) | async-done | bytes 2621472 | tf_op jit(solution)/shard_map/all_to_all | solution.py:36
  295.8 1.3 slice_convert_fusion.refs_1_
  297.1 4.9 %all-to-all-start.7 = ((bf16[8,64,512]{2,1,0:T(8,128)(2,1)}), bf16[8,64,512]{2,1,0:T(8,128)(2,1)S(1)}, u32[]{:S(2)}, u32[]{:S(2)}) async-start(bf16[8,64,512]{2,1,0:T(8,128)(2,1)} %shard_map.117), calls=%async_computation.7 | async-start | bytes 1048576 | tf_op jit(solution)/shard_map/all_to_all | solution.py:36
  302.0 4.7 %shard_map.122 = (f32[128,4096]{1,0:T(8,128)S(1)}, f32[8,128]{1,0:T(8,128)}) custom-call(f32[16,128]{1,0:T(8,128)S(1)} %copy-done.14, f32[8,128]{1,0:T(8,128)S(1)} %get-tuple-element.77.after_ref, bf16[320,4096]{1,0:T(8,128)(2,1)} %bitcast.21.refs_0_, bf16[64,4096]{1,0:T(8,128)(2,1)} %collective-permute-done.19.refs_1_, ...), custom_call_target="tpu_custom_call" | custom-call | flops 40000000000 | bytes 1024 | tf_op jit(solution)/shard_map/pallas_call | solution.py:284
  306.7 1.3 collective-permute-done.22.refs_1_
  307.9 11.2 %collective-permute-done.23.refs_2_ = bf16[64,4096]{1,0:T(8,128)(2,1)S(1)} collective-permute-done((bf16[64,4096]{1,0:T(8,128)(2,1)}, bf16[64,4096]{1,0:T(8,128)(2,1)S(1)}, u32[]{:S(2)}, u32[]{:S(2)}) %collective-permute-start.23) | collective-permute-done | bytes 524320 | tf_op jit(solution)/shard_map/ppermute | solution.py:32
  319.1 3.6 %shard_map.123 = bf16[128,4096]{1,0:T(8,128)(2,1)} custom-call(f32[128,4096]{1,0:T(8,128)S(1)} %get-tuple-element.80.own_ref, bf16[128,4096]{1,0:T(8,128)(2,1)} %collective-permute-done.21.refs_0_, bf16[64,4096]{1,0:T(8,128)(2,1)S(1)} %collective-permute-done.22.refs_1_, bf16[64,4096]{1,0:T(8,128)(2,1)S(1)} %collective-permute-done.23.refs_2_), custom_call_target="tpu_custom_call" | custom-call | flops 1024 | bytes 1024 | tf_op jit(solution)/shard_map/pallas_call | solution.py:315
  (111 shorter events, 19.0 us)
Async XLA Ops:
  0.6 9.8 %copy-start.2 = (bf16[128,4096]{1,0:T(8,128)(2,1)S(1)}, bf16[128,4096]{1,0:T(8,128)(2,1)}, u32[]{:S(2)}) copy-start(bf16[128,4096]{1,0:T(8,128)(2,1)} %refs_2_.1) | copy-start | bytes 3145732
  2.1 10.1 %copy-start.13 = (f32[16,128]{1,0:T(8,128)}, f32[16,128]{1,0:T(8,128)S(1)}, u32[]{:S(2)}) copy-start(f32[16,128]{1,0:T(8,128)S(1)} %pad_maximum_fusion.3.meta_ref) | copy-start | bytes 24580
  2.1 8.3 %collective-permute-start.2 = (f32[16,128]{1,0:T(8,128)S(1)}, f32[16,128]{1,0:T(8,128)S(1)}, u32[]{:S(2)}, u32[]{:S(2)}) collective-permute-start(f32[16,128]{1,0:T(8,128)S(1)} %pad_maximum_fusion.3.meta_ref), channel_id=1, source_target_pairs={{0,3},{1,2},{2,1},{3,0},{4,7},{5,6},{6,5},{7,4},{8,11},{9,10},{10,... | collective-permute-start | bytes 24584 | tf_op jit(solution)/shard_map/ppermute | solution.py:32
  3.7 6.8 %collective-permute-start.1 = (f32[16,128]{1,0:T(8,128)S(1)}, f32[16,128]{1,0:T(8,128)S(1)}, u32[]{:S(2)}, u32[]{:S(2)}) collective-permute-start(f32[16,128]{1,0:T(8,128)S(1)} %pad_maximum_fusion.3.meta_ref), channel_id=1, source_target_pairs={{0,2},{1,3},{2,0},{3,1},{4,6},{5,7},{6,4},{7,5},{8,10},{9,11},{10,... | collective-permute-start | bytes 24584 | tf_op jit(solution)/shard_map/ppermute | solution.py:32
  4.9 5.5 %collective-permute-start = (f32[16,128]{1,0:T(8,128)S(1)}, f32[16,128]{1,0:T(8,128)S(1)}, u32[]{:S(2)}, u32[]{:S(2)}) collective-permute-start(f32[16,128]{1,0:T(8,128)S(1)} %pad_maximum_fusion.3.meta_ref), channel_id=1, source_target_pairs={{0,1},{1,0},{2,3},{3,2},{4,5},{5,4},{6,7},{7,6},{8,9},{9,8},{10,11... | collective-permute-start | bytes 24584 | tf_op jit(solution)/shard_map/ppermute | solution.py:32
  8.4 25.3 %collective-permute-start.4 = (bf16[64,4096]{1,0:T(8,128)(2,1)}, bf16[64,4096]{1,0:T(8,128)(2,1)}, u32[]{:S(2)}, u32[]{:S(2)}) collective-permute-start(bf16[64,4096]{1,0:T(8,128)(2,1)} %get-tuple-element.84), channel_id=1, source_target_pairs={{0,1},{1,0},{2,3},{3,2},{4,5},{5,4},{6,7},{7,6},{8,9},{9,8},{10,11... | collective-permute-start | bytes 1572872 | tf_op jit(solution)/shard_map/ppermute | solution.py:32
  9.2 34.6 %collective-permute-start.3 = (bf16[64,4096]{1,0:T(8,128)(2,1)}, bf16[64,4096]{1,0:T(8,128)(2,1)}, u32[]{:S(2)}, u32[]{:S(2)}) collective-permute-start(bf16[64,4096]{1,0:T(8,128)(2,1)} %get-tuple-element.85), channel_id=1, source_target_pairs={{0,1},{1,0},{2,3},{3,2},{4,5},{5,4},{6,7},{7,6},{8,9},{9,8},{10,11... | collective-permute-start | bytes 1572872 | tf_op jit(solution)/shard_map/ppermute | solution.py:32
  10.4 33.4 %copy-start.19 = (f32[16,128]{1,0:T(8,128)}, f32[16,128]{1,0:T(8,128)S(1)}, u32[]{:S(2)}) copy-start(f32[16,128]{1,0:T(8,128)S(1)} %collective-permute-done.meta_ref) | copy-start | bytes 24580
  12.2 1.5 copy-start.5
  13.7 7.3 %copy-start.31 = (bf16[64,512]{1,0:T(8,128)(2,1)S(1)}, bf16[64,512]{1,0:T(8,128)(2,1)}, u32[]{:S(2)}) copy-start(bf16[64,512]{1,0:T(8,128)(2,1)} %param.10) | copy-start | bytes 196612
  13.7 7.3 %copy-start.32 = (bf16[64,512]{1,0:T(8,128)(2,1)S(1)}, bf16[64,512]{1,0:T(8,128)(2,1)}, u32[]{:S(2)}) copy-start(bf16[64,512]{1,0:T(8,128)(2,1)} %param.11) | copy-start | bytes 196612
  13.7 37.8 %all-to-all-start.1 = ((bf16[8,40,4096]{2,1,0:T(8,128)(2,1)}), bf16[8,40,4096]{2,1,0:T(8,128)(2,1)S(1)}, u32[]{:S(2)}, u32[]{:S(2)}) async-start(bf16[8,40,4096]{2,1,0:T(8,128)(2,1)} %bitcast.39), calls=%async_computation.1 | async-start | bytes 5242880 | tf_op jit(solution)/shard_map/all_to_all | solution.py:36
  18.1 53.2 %collective-permute-start.6 = (bf16[64,4096]{1,0:T(8,128)(2,1)}, bf16[64,4096]{1,0:T(8,128)(2,1)}, u32[]{:S(2)}, u32[]{:S(2)}) collective-permute-start(bf16[64,4096]{1,0:T(8,128)(2,1)} %get-tuple-element.84), channel_id=1, source_target_pairs={{0,2},{1,3},{2,0},{3,1},{4,6},{5,7},{6,4},{7,5},{8,10},{9,11},{10,... | collective-permute-start | bytes 1572872 | tf_op jit(solution)/shard_map/ppermute | solution.py:32
  21.0 68.8 %collective-permute-start.5 = (bf16[64,4096]{1,0:T(8,128)(2,1)}, bf16[64,4096]{1,0:T(8,128)(2,1)}, u32[]{:S(2)}, u32[]{:S(2)}) collective-permute-start(bf16[64,4096]{1,0:T(8,128)(2,1)} %get-tuple-element.85), channel_id=1, source_target_pairs={{0,2},{1,3},{2,0},{3,1},{4,6},{5,7},{6,4},{7,5},{8,10},{9,11},{10,... | collective-permute-start | bytes 1572872 | tf_op jit(solution)/shard_map/ppermute | solution.py:32
  43.8 1.2 copy-start.3
  49.9 0.8 copy-start.25
  50.7 0.8 copy-start.26
  51.5 47.2 %all-to-all-start = ((bf16[8,56,4096]{2,1,0:T(8,128)(2,1)}), bf16[8,56,4096]{2,1,0:T(8,128)(2,1)}, u32[]{:S(2)}, u32[]{:S(2)}) async-start(bf16[8,56,4096]{2,1,0:T(8,128)(2,1)} %bitcast.42), calls=%async_computation | async-start | bytes 7340032 | tf_op jit(solution)/shard_map/all_to_all | solution.py:36
  56.6 69.0 %collective-permute-start.7 = (bf16[64,4096]{1,0:T(8,128)(2,1)}, bf16[64,4096]{1,0:T(8,128)(2,1)}, u32[]{:S(2)}, u32[]{:S(2)}) collective-permute-start(bf16[64,4096]{1,0:T(8,128)(2,1)} %copy-done.26), channel_id=1, source_target_pairs={{0,3},{1,2},{2,1},{3,0},{4,7},{5,6},{6,5},{7,4},{8,11},{9,10},{10,... | collective-permute-start | bytes 1572872 | tf_op jit(solution)/shard_map/ppermute | solution.py:32
  57.1 68.6 %collective-permute-start.8 = (bf16[64,4096]{1,0:T(8,128)(2,1)}, bf16[64,4096]{1,0:T(8,128)(2,1)}, u32[]{:S(2)}, u32[]{:S(2)}) collective-permute-start(bf16[64,4096]{1,0:T(8,128)(2,1)} %copy-done.25), channel_id=1, source_target_pairs={{0,3},{1,2},{2,1},{3,0},{4,7},{5,6},{6,5},{7,4},{8,11},{9,10},{10,... | collective-permute-start | bytes 1572872 | tf_op jit(solution)/shard_map/ppermute | solution.py:32
  69.8 1.5 copy-start
  93.1 1.5 copy-start.6
  98.7 35.8 %all-to-all-start.2 = ((bf16[8,40,4096]{2,1,0:T(8,128)(2,1)}), bf16[8,40,4096]{2,1,0:T(8,128)(2,1)S(1)}, u32[]{:S(2)}, u32[]{:S(2)}) async-start(bf16[8,40,4096]{2,1,0:T(8,128)(2,1)} %bitcast.40), calls=%async_computation.2 | async-start | bytes 5242880 | tf_op jit(solution)/shard_map/all_to_all | solution.py:36
  119.7 0.8 copy-start.8
  120.5 0.7 copy-start.9
  121.2 0.7 copy-start.10
  122.0 0.7 copy-start.11
  122.7 0.7 copy-start.12
  123.5 0.7 copy-start.27
  124.2 0.7 copy-start.29
  124.9 0.7 copy-start.30
  130.1 0.6 copy-start.18
  134.5 39.0 %all-to-all-start.3 = ((bf16[8,40,4096]{2,1,0:T(8,128)(2,1)}), bf16[8,40,4096]{2,1,0:T(8,128)(2,1)}, u32[]{:S(2)}, u32[]{:S(2)}) async-start(bf16[8,40,4096]{2,1,0:T(8,128)(2,1)} %bitcast.14), calls=%async_computation.3 | async-start | bytes 5242880 | tf_op jit(solution)/shard_map/all_to_all | solution.py:36
  148.3 20.8 %collective-permute-start.11 = (bf16[512,256]{1,0:T(8,128)(2,1)}, bf16[512,256]{1,0:T(8,128)(2,1)}, u32[]{:S(2)}, u32[]{:S(2)}) collective-permute-start(bf16[512,256]{1,0:T(8,128)(2,1)} %shard_map.110), channel_id=1, source_target_pairs={{0,3},{1,2},{2,1},{3,0},{4,7},{5,6},{6,5},{7,4},{8,11},{9,10},{10,... | collective-permute-start | bytes 786440 | tf_op jit(solution)/shard_map/ppermute | solution.py:32
  148.8 23.0 %collective-permute-start.10 = (bf16[512,256]{1,0:T(8,128)(2,1)}, bf16[512,256]{1,0:T(8,128)(2,1)}, u32[]{:S(2)}, u32[]{:S(2)}) collective-permute-start(bf16[512,256]{1,0:T(8,128)(2,1)} %shard_map.110), channel_id=1, source_target_pairs={{0,2},{1,3},{2,0},{3,1},{4,6},{5,7},{6,4},{7,5},{8,10},{9,11},{10,... | collective-permute-start | bytes 786440 | tf_op jit(solution)/shard_map/ppermute | solution.py:32
  153.2 19.0 %collective-permute-start.9 = (bf16[512,256]{1,0:T(8,128)(2,1)}, bf16[512,256]{1,0:T(8,128)(2,1)}, u32[]{:S(2)}, u32[]{:S(2)}) collective-permute-start(bf16[512,256]{1,0:T(8,128)(2,1)} %shard_map.110), channel_id=1, source_target_pairs={{0,1},{1,0},{2,3},{3,2},{4,5},{5,4},{6,7},{7,6},{8,9},{9,8},{10,11... | collective-permute-start | bytes 786440 | tf_op jit(solution)/shard_map/ppermute | solution.py:32
  153.2 26.3 %collective-permute-start.12 = (bf16[40,4096]{1,0:T(8,128)(2,1)}, bf16[40,4096]{1,0:T(8,128)(2,1)S(1)}, u32[]{:S(2)}, u32[]{:S(2)}) collective-permute-start(bf16[40,4096]{1,0:T(8,128)(2,1)} %copy-done.30), channel_id=1, source_target_pairs={{0,4},{4,0},{8,12},{12,8},{16,20},{20,16},{24,28},{28,24},{1,5},{5... | collective-permute-start | bytes 983048 | tf_op jit(solution)/shard_map/ppermute | solution.py:32
  153.2 26.3 %collective-permute-start.13 = (bf16[40,4096]{1,0:T(8,128)(2,1)}, bf16[40,4096]{1,0:T(8,128)(2,1)}, u32[]{:S(2)}, u32[]{:S(2)}) collective-permute-start(bf16[40,4096]{1,0:T(8,128)(2,1)} %copy-done.29), channel_id=1, source_target_pairs={{0,8},{4,12},{8,0},{12,4},{16,24},{20,28},{24,16},{28,20},{1,9},{5... | collective-permute-start | bytes 983048 | tf_op jit(solution)/shard_map/ppermute | solution.py:32
  166.6 1.6 copy-start.4
  169.1 25.1 %collective-permute-start.14 = (bf16[40,4096]{1,0:T(8,128)(2,1)}, bf16[40,4096]{1,0:T(8,128)(2,1)S(1)}, u32[]{:S(2)}, u32[]{:S(2)}) collective-permute-start(bf16[40,4096]{1,0:T(8,128)(2,1)} %get-tuple-element.63), channel_id=1, source_target_pairs={{0,12},{4,8},{8,4},{12,0},{16,28},{20,24},{24,20},{28,16},{1,13},{... | collective-permute-start | bytes 983048 | tf_op jit(solution)/shard_map/ppermute | solution.py:32
  171.9 22.3 %collective-permute-start.15 = (bf16[40,4096]{1,0:T(8,128)(2,1)}, bf16[40,4096]{1,0:T(8,128)(2,1)S(1)}, u32[]{:S(2)}, u32[]{:S(2)}) collective-permute-start(bf16[40,4096]{1,0:T(8,128)(2,1)} %get-tuple-element.64), channel_id=1, source_target_pairs={{0,16},{4,20},{8,24},{12,28},{16,0},{20,4},{24,8},{28,12},{1,17},{... | collective-permute-start | bytes 983048 | tf_op jit(solution)/shard_map/ppermute | solution.py:32
  173.5 6.0 %copy-start.16 = (f32[8,128]{1,0:T(8,128)S(1)}, f32[8,128]{1,0:T(8,128)}, u32[]{:S(2)}) copy-start(f32[8,128]{1,0:T(8,128)} %copy-done.15) | copy-start | bytes 12292
  173.5 40.6 %all-to-all-start.4 = ((bf16[8,40,4096]{2,1,0:T(8,128)(2,1)}), bf16[8,40,4096]{2,1,0:T(8,128)(2,1)}, u32[]{:S(2)}, u32[]{:S(2)}) async-start(bf16[8,40,4096]{2,1,0:T(8,128)(2,1)} %bitcast.37), calls=%async_computation.4 | async-start | bytes 5242880 | tf_op jit(solution)/shard_map/all_to_all | solution.py:36
  193.4 0.8 copy-start.7
  194.2 16.6 %copy-start.21 = (bf16[40,4096]{1,0:T(8,128)(2,1)}, bf16[40,4096]{1,0:T(8,128)(2,1)S(1)}, u32[]{:S(2)}) copy-start(bf16[40,4096]{1,0:T(8,128)(2,1)S(1)} %collective-permute-done.14.refs_3_) | copy-start | bytes 983044
  194.2 16.6 %copy-start.23 = (bf16[40,4096]{1,0:T(8,128)(2,1)}, bf16[40,4096]{1,0:T(8,128)(2,1)S(1)}, u32[]{:S(2)}) copy-start(bf16[40,4096]{1,0:T(8,128)(2,1)S(1)} %collective-permute-done.15.refs_4_) | copy-start | bytes 983044
  194.8 35.2 %collective-permute-start.16 = (bf16[40,4096]{1,0:T(8,128)(2,1)}, bf16[40,4096]{1,0:T(8,128)(2,1)}, u32[]{:S(2)}, u32[]{:S(2)}) collective-permute-start(bf16[40,4096]{1,0:T(8,128)(2,1)} %get-tuple-element.73), channel_id=1, source_target_pairs={{0,20},{4,16},{8,28},{12,24},{16,4},{20,0},{24,12},{28,8},{1,21},{... | collective-permute-start | bytes 983048 | tf_op jit(solution)/shard_map/ppermute | solution.py:32
  194.9 35.1 %collective-permute-start.17 = (bf16[40,4096]{1,0:T(8,128)(2,1)}, bf16[40,4096]{1,0:T(8,128)(2,1)}, u32[]{:S(2)}, u32[]{:S(2)}) collective-permute-start(bf16[40,4096]{1,0:T(8,128)(2,1)} %get-tuple-element.74), channel_id=1, source_target_pairs={{0,24},{4,28},{8,16},{12,20},{16,8},{20,12},{24,0},{28,4},{1,25},{... | collective-permute-start | bytes 983048 | tf_op jit(solution)/shard_map/ppermute | solution.py:32
  197.6 32.5 %collective-permute-start.18 = (bf16[40,4096]{1,0:T(8,128)(2,1)}, bf16[40,4096]{1,0:T(8,128)(2,1)}, u32[]{:S(2)}, u32[]{:S(2)}) collective-permute-start(bf16[40,4096]{1,0:T(8,128)(2,1)} %get-tuple-element.75), channel_id=1, source_target_pairs={{0,28},{4,24},{8,20},{12,16},{16,12},{20,8},{24,4},{28,0},{1,29},{... | collective-permute-start | bytes 983048 | tf_op jit(solution)/shard_map/ppermute | solution.py:32
  197.6 0.7 copy-start.17
  210.8 1.5 copy-start.1
  215.4 42.9 %all-to-all-start.5 = ((bf16[8,40,4096]{2,1,0:T(8,128)(2,1)}), bf16[8,40,4096]{2,1,0:T(8,128)(2,1)S(1)}, u32[]{:S(2)}, u32[]{:S(2)}) async-start(bf16[8,40,4096]{2,1,0:T(8,128)(2,1)} %bitcast.33), calls=%async_computation.5 | async-start | bytes 5242880 | tf_op jit(solution)/shard_map/all_to_all | solution.py:36
  220.5 9.6 %copy-start.20 = (f32[16,128]{1,0:T(8,128)S(1)}, f32[16,128]{1,0:T(8,128)}, u32[]{:S(2)}) copy-start(f32[16,128]{1,0:T(8,128)} %copy-done.19) | copy-start | bytes 24580
  220.5 9.6 %copy-start.22 = (bf16[40,4096]{1,0:T(8,128)(2,1)S(1)}, bf16[40,4096]{1,0:T(8,128)(2,1)}, u32[]{:S(2)}) copy-start(bf16[40,4096]{1,0:T(8,128)(2,1)} %copy-done.21) | copy-start | bytes 983044
  220.5 9.6 %copy-start.24 = (bf16[40,4096]{1,0:T(8,128)(2,1)S(1)}, bf16[40,4096]{1,0:T(8,128)(2,1)}, u32[]{:S(2)}) copy-start(bf16[40,4096]{1,0:T(8,128)(2,1)} %copy-done.23) | copy-start | bytes 983044
  220.5 9.6 %copy-start.28 = (bf16[40,4096]{1,0:T(8,128)(2,1)S(1)}, bf16[40,4096]{1,0:T(8,128)(2,1)}, u32[]{:S(2)}) copy-start(bf16[40,4096]{1,0:T(8,128)(2,1)} %copy-done.27) | copy-start | bytes 983044
  225.3 76.6 %collective-permute-start.19 = (bf16[64,4096]{1,0:T(8,128)(2,1)}, bf16[64,4096]{1,0:T(8,128)(2,1)}, u32[]{:S(2)}, u32[]{:S(2)}) collective-permute-start(bf16[64,4096]{1,0:T(8,128)(2,1)} %get-tuple-element.78), channel_id=1, source_target_pairs={{0,2},{1,3},{2,0},{3,1},{4,6},{5,7},{6,4},{7,5},{8,10},{9,11},{10,... | collective-permute-start | bytes 1572872 | tf_op jit(solution)/shard_map/ppermute | solution.py:32
  227.7 74.2 %collective-permute-start.20 = (bf16[64,4096]{1,0:T(8,128)(2,1)}, bf16[64,4096]{1,0:T(8,128)(2,1)}, u32[]{:S(2)}, u32[]{:S(2)}) collective-permute-start(bf16[64,4096]{1,0:T(8,128)(2,1)} %get-tuple-element.79), channel_id=1, source_target_pairs={{0,2},{1,3},{2,0},{3,1},{4,6},{5,7},{6,4},{7,5},{8,10},{9,11},{10,... | collective-permute-start | bytes 1572872 | tf_op jit(solution)/shard_map/ppermute | solution.py:32
  234.7 72.0 %collective-permute-start.21 = (bf16[128,4096]{1,0:T(8,128)(2,1)}, bf16[128,4096]{1,0:T(8,128)(2,1)}, u32[]{:S(2)}, u32[]{:S(2)}) collective-permute-start(bf16[128,4096]{1,0:T(8,128)(2,1)} %get-tuple-element.81), channel_id=1, source_target_pairs={{0,1},{1,0},{2,3},{3,2},{4,5},{5,4},{6,7},{7,6},{8,9},{9,8},{10,11... | collective-permute-start | bytes 3145736 | tf_op jit(solution)/shard_map/ppermute | solution.py:32
  258.9 36.9 %all-to-all-start.6 = ((bf16[8,40,4096]{2,1,0:T(8,128)(2,1)}), bf16[8,40,4096]{2,1,0:T(8,128)(2,1)}, u32[]{:S(2)}, u32[]{:S(2)}) async-start(bf16[8,40,4096]{2,1,0:T(8,128)(2,1)} %bitcast.32), calls=%async_computation.6 | async-start | bytes 5242880 | tf_op jit(solution)/shard_map/all_to_all | solution.py:36
  264.9 37.1 %copy-start.14 = (f32[16,128]{1,0:T(8,128)S(1)}, f32[16,128]{1,0:T(8,128)}, u32[]{:S(2)}) copy-start(f32[16,128]{1,0:T(8,128)} %copy-done.13) | copy-start | bytes 24580
  268.1 39.9 %collective-permute-start.22 = (bf16[64,4096]{1,0:T(8,128)(2,1)}, bf16[64,4096]{1,0:T(8,128)(2,1)S(1)}, u32[]{:S(2)}, u32[]{:S(2)}) collective-permute-start(bf16[64,4096]{1,0:T(8,128)(2,1)} %get-tuple-element.82), channel_id=1, source_target_pairs={{0,3},{1,2},{2,1},{3,0},{4,7},{5,6},{6,5},{7,4},{8,11},{9,10},{10,... | collective-permute-start | bytes 1572872 | tf_op jit(solution)/shard_map/ppermute | solution.py:32
  269.6 49.5 %collective-permute-start.23 = (bf16[64,4096]{1,0:T(8,128)(2,1)}, bf16[64,4096]{1,0:T(8,128)(2,1)S(1)}, u32[]{:S(2)}, u32[]{:S(2)}) collective-permute-start(bf16[64,4096]{1,0:T(8,128)(2,1)} %get-tuple-element.83), channel_id=1, source_target_pairs={{0,3},{1,2},{2,1},{3,0},{4,7},{5,6},{6,5},{7,4},{8,11},{9,10},{10,... | collective-permute-start | bytes 1572872 | tf_op jit(solution)/shard_map/ppermute | solution.py:32
  297.1 25.6 %all-to-all-start.7 = ((bf16[8,64,512]{2,1,0:T(8,128)(2,1)}), bf16[8,64,512]{2,1,0:T(8,128)(2,1)S(1)}, u32[]{:S(2)}, u32[]{:S(2)}) async-start(bf16[8,64,512]{2,1,0:T(8,128)(2,1)} %shard_map.117), calls=%async_computation.7 | async-start | bytes 1048576 | tf_op jit(solution)/shard_map/all_to_all | solution.py:36
  (1 other events, 0.6 us)
